TPU v7x, 32 devices: a whole 2x2x4 slice. The times are simulated.
32 devices in a mesh: row: 8 (over y, x, core), col: 4 (over z).
Axes of the slice: x: 2, y: 2, z: 4, core: 2. Of those that a mesh axis runs over, the one named last changes fastest.
Arguments:
- tiles: bfloat16 [8192, 4096], P('row', 'col'), may hold values from -0.0625 to 0.0625
- block_map: int32 [8, 4, 8, 8], P('row', 'col'), may hold values from 0 to 1, as said below
- lanczos_block: bfloat16 [8, 8192], P(None, ('row', 'col')), may hold values from -6 to 6
Outputs:
- product: float32 [8, 8192], P(None, ('row', 'col'))
- projected: float32 [8, 8], replicated
Inputs may be any that keep to these rules, and one draw needn't show every extreme that they name: `block_map`: 0 or 1; the share of nonzero sub-blocks differs from tile to tile.
All inputs are finite; a program needn't handle non-finite values.
Results may differ from a plain program's by a relative error of at most 0.0003.
Values may be sent and summed in bfloat16 or wider, within the bound.
No kernel may reach another device: no remote copies, remote signals or barrier semaphores. Data moves between devices by JAX's collectives and lax.ppermute only.
A program may use at most 64 MiB of HBM per device.

v0:
```python
import jax
import jax.numpy as jnp
from jax import lax
from jax.sharding import PartitionSpec as P

SUB = 128


def passed_along(block, axis, distance):
    devices = range(lax.axis_size(axis))
    route = [(i - distance, i) for i in devices if i - distance in devices]
    return lax.ppermute(block, axis, route)


def on_device(tiles, block_map, lanczos_block):
    width = tiles.shape[0]
    groups = width // SUB
    row_idx = lax.axis_index("row")
    col_idx = lax.axis_index("col")
    rows_total = lax.axis_size("row")
    cols_total = lax.axis_size("col")
    valid = (row_idx + col_idx < rows_total).astype(jnp.bfloat16)
    keep = block_map[0, 0].astype(jnp.bfloat16) * valid
    matrix = (tiles.reshape(groups, SUB, groups, SUB) * keep[:, None, :, None]).reshape(
        width, width
    )
    source = lax.all_gather(lanczos_block, "col", axis=1, tiled=True)
    mirror = jnp.dot(source, matrix, preferred_element_type=jnp.float32)
    nbits = cols_total.bit_length() - 1
    far_vec = source
    for bit in range(nbits):
        moved_vec = passed_along(far_vec, "row", -(1 << bit))
        far_vec = jnp.where((col_idx >> bit) % 2 == 1, moved_vec, far_vec)
    arrived = mirror
    for bit in range(nbits):
        moved_sum = passed_along(arrived, "row", 1 << bit)
        arrived = jnp.where((col_idx >> bit) % 2 == 1, moved_sum, arrived)
    plain = lax.dot_general(
        far_vec, matrix, (((1,), (1,)), ((), ())), preferred_element_type=jnp.float32
    )
    product = lax.psum_scatter(plain + arrived, "col", scatter_dimension=1, tiled=True)
    partial_gram = jnp.dot(
        lanczos_block.astype(jnp.float32), product.T, precision=lax.Precision.HIGHEST
    )
    inner = lax.psum(partial_gram, ("row", "col"))
    projected = inner * (1.0 / jnp.sqrt(jnp.float32(width * rows_total)))
    return (product, projected)


def solution(mesh):
    placed = (P("row", "col"), P("row", "col", None, None), P(None, ("row", "col")))
    return jax.shard_map(
        on_device,
        mesh=mesh,
        in_specs=placed,
        out_specs=(P(None, ("row", "col")), P()),
        check_vma=False,
    )
```

profile of v0, /device:TPU:0, one launch (start us, length us, event | category | flops | bytes accessed | tf_op | source)
XLA Modules:
  0.0 109.1 jit_solution(1547619634605930814)
XLA Ops:
  7.2 0.0 reduce-scatter.2.cloned.1.call-start
  7.2 0.0 copy-start
  7.2 15.1 %all_gather.3 = bf16[8,1024]{1,0:T(8,128)(2,1)S(1)} all-gather(bf16[8,256]{1,0:T(8,128)(2,1)} %param.5), channel_id=1, replica_groups=mesh['row'=8,'col'=4] {'col'}, dimensions={1}, use_global_device_ids=true | all-gather | bytes 20480 | tf_op jit(solution)/shard_map/all_gather | solution.py:27
  22.3 0.7 multiply_bitcast_fusion
  23.0 0.3 mul.33
  23.3 0.0 copy-done
  23.4 0.5 convolution_bitcast_fusion
  23.8 1.3 %collective-permute-start.2 = (f32[8,1024]{1,0:T(8,128)S(1)}, f32[8,1024]{1,0:T(8,128)S(1)}, u32[]{:S(2)}, u32[]{:S(2)}) collective-permute-start(f32[8,1024]{1,0:T(8,128)S(1)} %convolution_bitcast_fusion), channel_id=1, source_target_pairs={{0,4},{4,8},{8,12},{12,16},{16,20},{20,24},{24,28},{1,5},{5,9},{9,... | collective-permute-start | bytes 98312 | tf_op jit(solution)/shard_map/ppermute | solution.py:12
  25.1 1.3 %collective-permute-start = (bf16[8,1024]{1,0:T(8,128)(2,1)S(1)}, bf16[8,1024]{1,0:T(8,128)(2,1)S(1)}, u32[]{:S(2)}, u32[]{:S(2)}) collective-permute-start(bf16[8,1024]{1,0:T(8,128)(2,1)S(1)} %all_gather.3), channel_id=1, source_target_pairs={{4,0},{8,4},{12,8},{16,12},{20,16},{24,20},{28,24},{5,1},{9,5},{13... | collective-permute-start | bytes 49160 | tf_op jit(solution)/shard_map/ppermute | solution.py:12
  26.4 0.0 collective-permute-done.2
  26.4 6.4 %collective-permute-start.3 = (f32[8,1024]{1,0:T(8,128)S(1)}, f32[8,1024]{1,0:T(8,128)S(1)}, u32[]{:S(2)}, u32[]{:S(2)}) collective-permute-start(f32[8,1024]{1,0:T(8,128)S(1)} %broadcast_select_fusion), channel_id=1, source_target_pairs={{0,8},{4,12},{8,16},{12,20},{16,24},{20,28},{1,9},{5,13},{9,17},{1... | collective-permute-start | bytes 98312 | tf_op jit(solution)/shard_map/ppermute | solution.py:12
  32.8 0.0 collective-permute-done
  32.8 1.3 %collective-permute-start.1 = (bf16[8,1024]{1,0:T(8,128)(2,1)S(1)}, bf16[8,1024]{1,0:T(8,128)(2,1)S(1)}, u32[]{:S(2)}, u32[]{:S(2)}) collective-permute-start(bf16[8,1024]{1,0:T(8,128)(2,1)S(1)} %broadcast_select_fusion.1), channel_id=1, source_target_pairs={{8,0},{12,4},{16,8},{20,12},{24,16},{28,20},{9,1},{13,5},{17,9},{2... | collective-permute-start | bytes 49160 | tf_op jit(solution)/shard_map/ppermute | solution.py:12
  34.2 0.0 copy-start.1
  34.2 4.7 %collective-permute-done.1 = bf16[8,1024]{1,0:T(8,128)(2,1)S(1)} collective-permute-done((bf16[8,1024]{1,0:T(8,128)(2,1)S(1)}, bf16[8,1024]{1,0:T(8,128)(2,1)S(1)}, u32[]{:S(2)}, u32[]{:S(2)}) %collective-permute-start.1) | collective-permute-done | bytes 16416 | tf_op jit(solution)/shard_map/ppermute | solution.py:12
  38.9 0.0 collective-permute-done.3
  38.9 2.9 %convolution_add_fusion = f32[8,1024]{1,0:T(8,128)} fusion(bf16[1024,1024]{1,0:T(8,128)(2,1)} %param.3, bf16[128,8,8,128]{3,2,1,0:T(8,128)(2,1)S(1)} %bitcast.16, f32[8,1024]{1,0:T(8,128)S(1)} %collective-permute-done.3, f32[8,1024]{1,0:T(8,128)S(1)} %broadcast_select_fusion, bf16[8,1024]{1,0:T(8,128)(2,1)S(1)} %collective-permute-done.1, ...), kind=kOutput, calls=%fused_computation.2 | convolution fusion | flops 17850368 | bytes 4325377 | tf_op jit(solution)/shard_map/dot_general | solution.py:38
  41.7 0.0 reduce-scatter.2.cloned.1.call-update
  41.7 20.6 %reduce-scatter.2.cloned.1.call-done = f32[8,256]{1,0:T(8,128)} async-done(((f32[8,1024]{1,0:T(8,128)}), f32[8,256]{1,0:T(8,128)}) %reduce-scatter.2.cloned.1.call-update) | async-done | bytes 8208 | tf_op jit(solution)/shard_map/reduce_scatter | solution.py:41
  62.3 0.0 copy-done.1
  62.3 0.8 convolution_bitcast_fusion.1
  63.1 38.4 %psum.7 = f32[8,8]{0,1:T(8,128)S(1)} all-reduce(f32[8,8]{0,1:T(8,128)S(1)} %convolution_bitcast_fusion.1), channel_id=1, replica_groups=mesh['row'=8,'col'=4] {'row','col'}, use_global_device_ids=true, to_apply=%region_1.2 | all-reduce | flops 64 | bytes 512 | tf_op jit(solution)/shard_map/psum | solution.py:45
  101.6 0.7 copy.5
  (3 shorter events, 0.0 us)
Async XLA Ops:
  7.2 55.2 %reduce-scatter.2.cloned.1.call-start = ((), (), s32[]{:S(2)}) async-start(), calls=%async_computation.1 | async-start | bytes 40960 | tf_op jit(solution)/shard_map/reduce_scatter | solution.py:41
  7.2 16.1 %copy-start = (bf16[1024,1024]{1,0:T(8,128)(2,1)S(1)}, bf16[1024,1024]{1,0:T(8,128)(2,1)}, u32[]{:S(2)}) copy-start(bf16[1024,1024]{1,0:T(8,128)(2,1)} %param.3) | copy-start | bytes 6291460
  23.8 2.6 %collective-permute-start.2 = (f32[8,1024]{1,0:T(8,128)S(1)}, f32[8,1024]{1,0:T(8,128)S(1)}, u32[]{:S(2)}, u32[]{:S(2)}) collective-permute-start(f32[8,1024]{1,0:T(8,128)S(1)} %convolution_bitcast_fusion), channel_id=1, source_target_pairs={{0,4},{4,8},{8,12},{12,16},{16,20},{20,24},{24,28},{1,5},{5,9},{9,... | collective-permute-start | bytes 98312 | tf_op jit(solution)/shard_map/ppermute | solution.py:12
  25.1 7.7 %collective-permute-start = (bf16[8,1024]{1,0:T(8,128)(2,1)S(1)}, bf16[8,1024]{1,0:T(8,128)(2,1)S(1)}, u32[]{:S(2)}, u32[]{:S(2)}) collective-permute-start(bf16[8,1024]{1,0:T(8,128)(2,1)S(1)} %all_gather.3), channel_id=1, source_target_pairs={{4,0},{8,4},{12,8},{16,12},{20,16},{24,20},{28,24},{5,1},{9,5},{13... | collective-permute-start | bytes 49160 | tf_op jit(solution)/shard_map/ppermute | solution.py:12
  26.4 12.4 %collective-permute-start.3 = (f32[8,1024]{1,0:T(8,128)S(1)}, f32[8,1024]{1,0:T(8,128)S(1)}, u32[]{:S(2)}, u32[]{:S(2)}) collective-permute-start(f32[8,1024]{1,0:T(8,128)S(1)} %broadcast_select_fusion), channel_id=1, source_target_pairs={{0,8},{4,12},{8,16},{12,20},{16,24},{20,28},{1,9},{5,13},{9,17},{1... | collective-permute-start | bytes 98312 | tf_op jit(solution)/shard_map/ppermute | solution.py:12
  32.8 6.0 %collective-permute-start.1 = (bf16[8,1024]{1,0:T(8,128)(2,1)S(1)}, bf16[8,1024]{1,0:T(8,128)(2,1)S(1)}, u32[]{:S(2)}, u32[]{:S(2)}) collective-permute-start(bf16[8,1024]{1,0:T(8,128)(2,1)S(1)} %broadcast_select_fusion.1), channel_id=1, source_target_pairs={{8,0},{12,4},{16,8},{20,12},{24,16},{28,20},{9,1},{13,5},{17,9},{2... | collective-permute-start | bytes 49160 | tf_op jit(solution)/shard_map/ppermute | solution.py:12
  34.2 28.2 %copy-start.1 = (bf16[8,256]{1,0:T(8,128)(2,1)S(1)}, bf16[8,256]{1,0:T(8,128)(2,1)}, u32[]{:S(2)}) copy-start(bf16[8,256]{1,0:T(8,128)(2,1)} %param.5) | copy-start | bytes 12292
Sparse Core Ops, SparseCore 0:
  41.9 20.4 reduce-scatter.1
where the time goes:
time: 109 us
  blocking collectives  53.5 us (49%)
  waiting for transfers between devices  25.3 us (23%)
  between operations  14.2 us (13%)
  starting transfers between devices  10.3 us (9%)
  matrix products  4.12 us (4%)
    psum x1, blocking collectives, on_device(): inner = lax.psum(partial_gram, ('row', 'col'))  38.4 us
    reduce_scatter x1, waiting for transfers between devices, on_device(): lax.psum_scatter(plain + arrived, 'col', scatter_dimension=1, tiled=True)  20.6 us
    all_gather x1, blocking collectives, on_device(): source = lax.all_gather(lanczos_block, 'col', axis=1, tiled=True)  15.1 us
    ppermute x4, starting transfers between devices, passed_along(): return lax.ppermute(block, axis, route)  10.2 us
    ppermute x4, waiting for transfers between devices, passed_along(): return lax.ppermute(block, axis, route)  4.7 us
    dot_general x1, matrix products, on_device(): lax.dot_general(far_vec, matrix, (((1,), (1,)), ((), ())), preferred_elem...  2.85 us
  transfers between devices with their start and end apart: 5, of which 2 were waited for; matrix products, arithmetic and copies ran while one was open for 0% of the time, Pallas kernels for 0%

commit v1 on v0

v1 whole, which is shorter than its diff:
```python
import jax
import jax.numpy as jnp
from jax import lax
from jax.sharding import PartitionSpec as P

SUB = 128
AXES = ("row", "col")


def bits_of(axis):
    return range(lax.axis_size(axis).bit_length() - 1)


def route(target):
    rows, cols = lax.axis_size("row"), lax.axis_size("col")
    pairs = []
    for r in range(rows):
        for c in range(cols):
            to_row, to_col = target(r, c)
            if 0 <= to_row < rows:
                pairs.append((r * cols + c, to_row * cols + to_col))
    return pairs


def across_row(block, bit):
    return lax.ppermute(block, AXES, route(lambda r, c: (r ^ (1 << bit), c)))


def across_col(block, bit):
    return lax.ppermute(block, AXES, route(lambda r, c: (r, c ^ (1 << bit))))


def from_far(block):
    return lax.ppermute(block, AXES, route(lambda r, c: (r - c, c)))


def to_far(block):
    return lax.ppermute(block, AXES, route(lambda r, c: (r + c, c)))


def on_device(tiles, block_map, lanczos_block):
    width = tiles.shape[0]
    vectors = lanczos_block.shape[0]
    groups = width // SUB
    col_idx = lax.axis_index("col")
    total = width * lax.axis_size("row")

    keep = block_map[0, 0].astype(jnp.bfloat16)
    matrix = (tiles.reshape(groups, SUB, groups, SUB) * keep[:, None, :, None]).reshape(
        width, width
    )

    source = lanczos_block
    for bit in bits_of("col"):
        other = across_col(source, bit)
        upper = (col_idx >> bit) % 2 == 1
        source = jnp.concatenate(
            [jnp.where(upper, other, source), jnp.where(upper, source, other)], axis=1
        )
    far_vec = from_far(source)
    mirror = jnp.dot(source, matrix, preferred_element_type=jnp.float32)
    arrived = to_far(mirror)
    plain = lax.dot_general(
        far_vec, matrix, (((1,), (1,)), ((), ())), preferred_element_type=jnp.float32
    )
    gram = lax.dot_general(
        mirror,
        far_vec.astype(jnp.float32),
        (((1,), (1,)), ((), ())),
        precision=lax.Precision.HIGHEST,
    )
    for bit in bits_of("row"):
        gram = gram + across_row(gram, bit)
    gram = jnp.pad(gram, ((0, 0), (0, SUB - vectors)))
    sums = plain + arrived
    for bit in reversed(bits_of("col")):
        half = sums.shape[1] // 2
        upper = (col_idx >> bit) % 2 == 1
        given = jnp.where(upper, sums[:, :half], sums[:, half:])
        kept = jnp.where(upper, sums[:, half:], sums[:, :half])
        other = across_col(jnp.concatenate([given, gram], axis=1), bit)
        sums = kept + other[:, :half]
        gram = gram + other[:, half:]
    gram = gram[:, :vectors]
    projected = (gram + gram.T) * (1.0 / jnp.sqrt(jnp.float32(total)))
    return (sums, projected)


def solution(mesh):
    placed = (P("row", "col"), P("row", "col", None, None), P(None, ("row", "col")))
    return jax.shard_map(
        on_device,
        mesh=mesh,
        in_specs=placed,
        out_specs=(P(None, ("row", "col")), P()),
        check_vma=False,
    )
```

time: 109 us -> 37.2 us (0.34)
  blocking collectives: 53.5 us -> 0 us
  waiting for transfers between devices: 25.3 us -> 11.6 us
  between operations: 14.2 us -> 0.72 us
  starting transfers between devices: 10.3 us -> 20.3 us
  matrix products: 4.12 us -> 1.23 us
  other arithmetic: 0.71 us -> 2.65 us
    psum x1 -> x0, blocking collectives: 38.4 us -> none  [on_device(): inner = lax.psum(partial_gram, ('row', 'col'))]
    reduce_scatter x1 -> x0, waiting for transfers between devices: 20.6 us -> none  [on_device(): lax.psum_scatter(plain + arrived, 'col', scatter_dimension=1, tiled=True)]
    all_gather x1 -> x0, blocking collectives: 15.1 us -> none  [on_device(): source = lax.all_gather(lanczos_block, 'col', axis=1, tiled=True)]
    ppermute x4 -> x9, starting transfers between devices: 10.2 us -> 20.3 us  [the longest x4 15.4 us: across_col(): return lax.ppermute(block, AXES, route(lambda r, c: (r, c ^ 1 << bit)))]
    ppermute x4 -> x9, waiting for transfers between devices: 4.7 us -> 11.6 us  [the longest x4 6.9 us: across_col(): return lax.ppermute(block, AXES, route(lambda r, c: (r, c ^ 1 << bit)))]
    dot_general x1, matrix products: 2.85 us -> 0.65 us  [on_device(): lax.dot_general(far_vec, matrix, (((1,), (1,)), ((), ())), preferred_elem...]
  transfers between devices with their start and end apart: 5 -> 9, of which waited for: 2 -> 7; matrix products, arithmetic and copies ran while one was open for 0% -> 4% of each run, Pallas kernels for 0% -> 0%
where the time goes in v1:
time: 37.2 us; the launch traced here: 37 us
  starting transfers between devices  20.3 us (55%)
  waiting for transfers between devices  11.6 us (31%)
  other arithmetic  2.65 us (7%)
  matrix products  1.23 us (3%)
  between operations  0.72 us (2%)
  local copies, waits for them, and re-layouts  0.42 us (1%)
    ppermute x4, starting transfers between devices, across_col(): return lax.ppermute(block, AXES, route(lambda r, c: (r, c ^ 1 << bit)))  15.4 us
    ppermute x4, waiting for transfers between devices, across_col(): return lax.ppermute(block, AXES, route(lambda r, c: (r, c ^ 1 << bit)))  6.9 us
    ppermute x3, waiting for transfers between devices, across_row(): return lax.ppermute(block, AXES, route(lambda r, c: (r ^ 1 << bit, c)))  4.73 us
    ppermute x3, starting transfers between devices, across_row(): return lax.ppermute(block, AXES, route(lambda r, c: (r ^ 1 << bit, c)))  3.68 us
  transfers between devices with their start and end apart: 9, of which 7 were waited for; matrix products, arithmetic and copies ran while one was open for 4% of the time, Pallas kernels for 0%

profile of v1, /device:TPU:0, one launch (start us, length us, event | category | flops | bytes accessed | tf_op | source)
XLA Modules:
  0.0 37.0 jit_solution(16898814036184156847)
XLA Ops:
  0.6 0.0 copy-start
  0.6 3.1 %collective-permute-start = (bf16[8,256]{1,0:T(8,128)(2,1)}, bf16[8,256]{1,0:T(8,128)(2,1)S(1)}, u32[]{:S(2)}, u32[]{:S(2)}) collective-permute-start(bf16[8,256]{1,0:T(8,128)(2,1)} %param.5), channel_id=1, source_target_pairs={{0,1},{1,0},{2,3},{3,2},{4,5},{5,4},{6,7},{7,6},{8,9},{9,8},{10,11... | collective-permute-start | bytes 12296 | tf_op jit(solution)/shard_map/ppermute | solution.py:30
  3.7 1.8 %collective-permute-done = bf16[8,256]{1,0:T(8,128)(2,1)S(1)} collective-permute-done((bf16[8,256]{1,0:T(8,128)(2,1)}, bf16[8,256]{1,0:T(8,128)(2,1)S(1)}, u32[]{:S(2)}, u32[]{:S(2)}) %collective-permute-start) | collective-permute-done | bytes 4128 | tf_op jit(solution)/shard_map/ppermute | solution.py:30
  5.5 0.7 %broadcast_select_fusion.3 = (bf16[8,256]{1,0:T(8,128)(2,1)S(1)}, bf16[8,256]{1,0:T(8,128)(2,1)S(1)}) fusion(bf16[8,256]{1,0:T(8,128)(2,1)S(1)} %collective-permute-done, bf16[8,256]{1,0:T(8,128)(2,1)} %param.5, pred[]{:T(512)S(6)} %eq.13), kind=kLoop, calls=%fused_computation.18 | loop fusion | flops 4096 | bytes 16385 | tf_op jit(solution)/shard_map/jit(_where)/select_n | solution.py:58
  6.2 3.0 %collective-permute-start.1 = (bf16[8,512]{1,0:T(8,128)(2,1)S(1)}, bf16[8,512]{1,0:T(8,128)(2,1)S(1)}, u32[]{:S(2)}, u32[]{:S(2)}) collective-permute-start(bf16[8,512]{1,0:T(8,128)(2,1)S(1)} %pad_maximum_fusion.3), channel_id=1, source_target_pairs={{0,2},{1,3},{2,0},{3,1},{4,6},{5,7},{6,4},{7,5},{8,10},{9,11},{10,... | collective-permute-start | bytes 24584 | tf_op jit(solution)/shard_map/ppermute | solution.py:30
  9.3 0.7 %convert_bitcast_fusion = bf16[8,8]{1,0:T(8,128)(2,1)S(1)} fusion(s32[1,1,8,8]{3,2,1,0:T(8,128)} %param.4), kind=kLoop, calls=%fused_computation.19 | loop fusion | flops 64 | bytes 384 | tf_op jit(solution)/shard_map/convert_element_type | solution.py:48
  9.9 0.9 %collective-permute-done.1 = bf16[8,512]{1,0:T(8,128)(2,1)S(1)} collective-permute-done((bf16[8,512]{1,0:T(8,128)(2,1)S(1)}, bf16[8,512]{1,0:T(8,128)(2,1)S(1)}, u32[]{:S(2)}, u32[]{:S(2)}) %collective-permute-start.1) | collective-permute-done | bytes 8224 | tf_op jit(solution)/shard_map/ppermute | solution.py:30
  10.9 0.7 %collective-permute-start.2 = (bf16[8,1024]{1,0:T(8,128)(2,1)S(1)}, bf16[8,1024]{1,0:T(8,128)(2,1)S(1)}, u32[]{:S(2)}, u32[]{:S(2)}) collective-permute-start(bf16[8,1024]{1,0:T(8,128)(2,1)S(1)} %pad_maximum_fusion.1), channel_id=1, source_target_pairs={{0,0},{4,4},{5,1},{8,8},{9,5},{10,2},{12,12},{13,9},{14,6},{15,3},... | collective-permute-start | bytes 49160 | tf_op jit(solution)/shard_map/ppermute | solution.py:34
  11.6 0.3 mul.17
  11.9 0.0 copy-done
  11.9 0.5 %fusion = f32[8,1024]{1,0:T(8,128)S(1)} fusion(bf16[1024,1024]{1,0:T(8,128)(2,1)S(1)} %copy-done, bf16[128,8,8,128]{3,2,1,0:T(8,128)(2,1)S(1)} %bitcast.16, bf16[8,512]{1,0:T(8,128)(2,1)S(1)} %get-tuple-element.3, bf16[8,512]{1,0:T(8,128)(2,1)S(1)} %get-tuple-element.2), kind=kOutput, calls=%fused_computation.2 | convolution fusion | flops 17858560 | bytes 4243456 | tf_op jit(solution)/shard_map/dot_general | solution.py:61
  12.4 0.7 %collective-permute-start.3 = (f32[8,1024]{1,0:T(8,128)S(1)}, f32[8,1024]{1,0:T(8,128)S(1)}, u32[]{:S(2)}, u32[]{:S(2)}) collective-permute-start(f32[8,1024]{1,0:T(8,128)S(1)} %fusion), channel_id=1, source_target_pairs={{0,0},{1,5},{2,10},{3,15},{4,4},{5,9},{6,14},{7,19},{8,8},{9,13},{... | collective-permute-start | bytes 98312 | tf_op jit(solution)/shard_map/ppermute | solution.py:38
  13.0 0.0 collective-permute-done.2
  13.1 0.1 fusion.2
  13.2 0.0 collective-permute-start.4
  13.2 1.2 %collective-permute-done.4 = f32[8,8]{1,0:T(8,128)S(1)} collective-permute-done((f32[8,8]{1,0:T(8,128)S(1)}, f32[8,8]{1,0:T(8,128)S(1)}, u32[]{:S(2)}, u32[]{:S(2)}) %collective-permute-start.4) | collective-permute-done | bytes 288 | tf_op jit(solution)/shard_map/ppermute | solution.py:26
  14.4 1.8 %collective-permute-start.5 = (f32[8,8]{1,0:T(8,128)S(1)}, f32[8,8]{1,0:T(8,128)S(1)}, u32[]{:S(2)}, u32[]{:S(2)}) collective-permute-start(f32[8,8]{1,0:T(8,128)S(1)} %add.41), channel_id=1, source_target_pairs={{0,8},{1,9},{2,10},{3,11},{4,12},{5,13},{6,14},{7,15},{8,0},{9,1},... | collective-permute-start | bytes 776 | tf_op jit(solution)/shard_map/ppermute | solution.py:26
  16.2 1.8 %collective-permute-done.5 = f32[8,8]{1,0:T(8,128)S(1)} collective-permute-done((f32[8,8]{1,0:T(8,128)S(1)}, f32[8,8]{1,0:T(8,128)S(1)}, u32[]{:S(2)}, u32[]{:S(2)}) %collective-permute-start.5) | collective-permute-done | bytes 288 | tf_op jit(solution)/shard_map/ppermute | solution.py:26
  18.0 1.9 %collective-permute-start.6 = (f32[8,8]{1,0:T(8,128)S(1)}, f32[8,8]{1,0:T(8,128)S(1)}, u32[]{:S(2)}, u32[]{:S(2)}) collective-permute-start(f32[8,8]{1,0:T(8,128)S(1)} %add.42), channel_id=1, source_target_pairs={{0,16},{1,17},{2,18},{3,19},{4,20},{5,21},{6,22},{7,23},{8,24},{9,... | collective-permute-start | bytes 776 | tf_op jit(solution)/shard_map/ppermute | solution.py:26
  19.8 1.8 %collective-permute-done.6 = f32[8,8]{1,0:T(8,128)S(1)} collective-permute-done((f32[8,8]{1,0:T(8,128)S(1)}, f32[8,8]{1,0:T(8,128)S(1)}, u32[]{:S(2)}, u32[]{:S(2)}) %collective-permute-start.6) | collective-permute-done | bytes 288 | tf_op jit(solution)/shard_map/ppermute | solution.py:26
  21.6 0.0 collective-permute-done.3
  21.6 0.7 %convolution_add_fusion = f32[8,1024]{1,0:T(8,128)S(1)} fusion(f32[8,1024]{1,0:T(8,128)S(1)} %collective-permute-done.3, bf16[8,1024]{1,0:T(8,128)(2,1)S(1)} %collective-permute-done.2, bf16[1024,1024]{1,0:T(8,128)(2,1)S(1)} %copy-done, bf16[128,8,8,128]{3,2,1,0:T(8,128)(2,1)S(1)} %bitcast.17), kind=kOutput, calls=%fused_computation.1 | convolution fusion | flops 17833984 | bytes 4276224 | tf_op jit(solution)/shard_map/dot_general | solution.py:63
  22.3 7.9 %collective-permute-start.7 = (f32[8,640]{1,0:T(8,128)S(1)}, f32[8,640]{1,0:T(8,128)S(1)}, u32[]{:S(2)}, u32[]{:S(2)}) collective-permute-start(f32[8,640]{1,0:T(8,128)S(1)} %pad_maximum_fusion), channel_id=1, source_target_pairs={{0,2},{1,3},{2,0},{3,1},{4,6},{5,7},{6,4},{7,5},{8,10},{9,11},{10,... | collective-permute-start | bytes 61448 | tf_op jit(solution)/shard_map/ppermute | solution.py:30
  30.2 1.8 %collective-permute-done.7 = f32[8,640]{1,0:T(8,128)S(1)} collective-permute-done((f32[8,640]{1,0:T(8,128)S(1)}, f32[8,640]{1,0:T(8,128)S(1)}, u32[]{:S(2)}, u32[]{:S(2)}) %collective-permute-start.7) | collective-permute-done | bytes 20512 | tf_op jit(solution)/shard_map/ppermute | solution.py:30
  32.0 1.4 %collective-permute-start.8 = (f32[8,384]{1,0:T(8,128)S(1)}, f32[8,384]{1,0:T(8,128)S(1)}, u32[]{:S(2)}, u32[]{:S(2)}) collective-permute-start(f32[8,384]{1,0:T(8,128)S(1)} %pad_maximum_fusion.2), channel_id=1, source_target_pairs={{0,1},{1,0},{2,3},{3,2},{4,5},{5,4},{6,7},{7,6},{8,9},{9,8},{10,11... | collective-permute-start | bytes 36872 | tf_op jit(solution)/shard_map/ppermute | solution.py:30
  33.3 2.4 %collective-permute-done.8 = f32[8,384]{1,0:T(8,128)S(1)} collective-permute-done((f32[8,384]{1,0:T(8,128)S(1)}, f32[8,384]{1,0:T(8,128)S(1)}, u32[]{:S(2)}, u32[]{:S(2)}) %collective-permute-start.8) | collective-permute-done | bytes 12320 | tf_op jit(solution)/shard_map/ppermute | solution.py:30
  35.7 0.1 copy.5
  35.8 0.6 %fusion.1 = f32[8,8]{1,0:T(8,128)} fusion(f32[8,8]{0,1:T(8,128)S(1)} %copy.5, f32[8,128]{1,0:T(8,128)S(1)} %slice_add_fusion.2), kind=kLoop, calls=%fused_computation.16 | loop fusion | flops 128 | bytes 768 | tf_op jit(solution)/shard_map/mul | solution.py:85
  36.4 0.6 %slice_add_fusion.1 = f32[8,256]{1,0:T(8,128)} fusion(f32[8,384]{1,0:T(8,128)S(1)} %collective-permute-done.8, f32[8,512]{1,0:T(8,128)S(1)} %slice_add_fusion, pred[]{:T(512)S(6)} %eq.13), kind=kLoop, calls=%fused_computation.8 | loop fusion | flops 4096 | bytes 32769 | tf_op jit(solution)/shard_map/add | solution.py:82
  (14 shorter events, 0.1 us)
Async XLA Ops:
  0.6 11.3 %copy-start = (bf16[1024,1024]{1,0:T(8,128)(2,1)S(1)}, bf16[1024,1024]{1,0:T(8,128)(2,1)}, u32[]{:S(2)}) copy-start(bf16[1024,1024]{1,0:T(8,128)(2,1)} %param.3) | copy-start | bytes 6291460
  0.6 4.9 %collective-permute-start = (bf16[8,256]{1,0:T(8,128)(2,1)}, bf16[8,256]{1,0:T(8,128)(2,1)S(1)}, u32[]{:S(2)}, u32[]{:S(2)}) collective-permute-start(bf16[8,256]{1,0:T(8,128)(2,1)} %param.5), channel_id=1, source_target_pairs={{0,1},{1,0},{2,3},{3,2},{4,5},{5,4},{6,7},{7,6},{8,9},{9,8},{10,11... | collective-permute-start | bytes 12296 | tf_op jit(solution)/shard_map/ppermute | solution.py:30
  6.2 4.7 %collective-permute-start.1 = (bf16[8,512]{1,0:T(8,128)(2,1)S(1)}, bf16[8,512]{1,0:T(8,128)(2,1)S(1)}, u32[]{:S(2)}, u32[]{:S(2)}) collective-permute-start(bf16[8,512]{1,0:T(8,128)(2,1)S(1)} %pad_maximum_fusion.3), channel_id=1, source_target_pairs={{0,2},{1,3},{2,0},{3,1},{4,6},{5,7},{6,4},{7,5},{8,10},{9,11},{10,... | collective-permute-start | bytes 24584 | tf_op jit(solution)/shard_map/ppermute | solution.py:30
  10.9 2.1 %collective-permute-start.2 = (bf16[8,1024]{1,0:T(8,128)(2,1)S(1)}, bf16[8,1024]{1,0:T(8,128)(2,1)S(1)}, u32[]{:S(2)}, u32[]{:S(2)}) collective-permute-start(bf16[8,1024]{1,0:T(8,128)(2,1)S(1)} %pad_maximum_fusion.1), channel_id=1, source_target_pairs={{0,0},{4,4},{5,1},{8,8},{9,5},{10,2},{12,12},{13,9},{14,6},{15,3},... | collective-permute-start | bytes 49160 | tf_op jit(solution)/shard_map/ppermute | solution.py:34
  12.4 9.2 %collective-permute-start.3 = (f32[8,1024]{1,0:T(8,128)S(1)}, f32[8,1024]{1,0:T(8,128)S(1)}, u32[]{:S(2)}, u32[]{:S(2)}) collective-permute-start(f32[8,1024]{1,0:T(8,128)S(1)} %fusion), channel_id=1, source_target_pairs={{0,0},{1,5},{2,10},{3,15},{4,4},{5,9},{6,14},{7,19},{8,8},{9,13},{... | collective-permute-start | bytes 98312 | tf_op jit(solution)/shard_map/ppermute | solution.py:38
  13.2 1.2 %collective-permute-start.4 = (f32[8,8]{1,0:T(8,128)S(1)}, f32[8,8]{1,0:T(8,128)S(1)}, u32[]{:S(2)}, u32[]{:S(2)}) collective-permute-start(f32[8,8]{1,0:T(8,128)S(1)} %fusion.2), channel_id=1, source_target_pairs={{0,4},{1,5},{2,6},{3,7},{4,0},{5,1},{6,2},{7,3},{8,12},{9,13},{10,... | collective-permute-start | bytes 776 | tf_op jit(solution)/shard_map/ppermute | solution.py:26
  14.4 3.6 %collective-permute-start.5 = (f32[8,8]{1,0:T(8,128)S(1)}, f32[8,8]{1,0:T(8,128)S(1)}, u32[]{:S(2)}, u32[]{:S(2)}) collective-permute-start(f32[8,8]{1,0:T(8,128)S(1)} %add.41), channel_id=1, source_target_pairs={{0,8},{1,9},{2,10},{3,11},{4,12},{5,13},{6,14},{7,15},{8,0},{9,1},... | collective-permute-start | bytes 776 | tf_op jit(solution)/shard_map/ppermute | solution.py:26
  18.0 3.6 %collective-permute-start.6 = (f32[8,8]{1,0:T(8,128)S(1)}, f32[8,8]{1,0:T(8,128)S(1)}, u32[]{:S(2)}, u32[]{:S(2)}) collective-permute-start(f32[8,8]{1,0:T(8,128)S(1)} %add.42), channel_id=1, source_target_pairs={{0,16},{1,17},{2,18},{3,19},{4,20},{5,21},{6,22},{7,23},{8,24},{9,... | collective-permute-start | bytes 776 | tf_op jit(solution)/shard_map/ppermute | solution.py:26
  22.3 9.6 %collective-permute-start.7 = (f32[8,640]{1,0:T(8,128)S(1)}, f32[8,640]{1,0:T(8,128)S(1)}, u32[]{:S(2)}, u32[]{:S(2)}) collective-permute-start(f32[8,640]{1,0:T(8,128)S(1)} %pad_maximum_fusion), channel_id=1, source_target_pairs={{0,2},{1,3},{2,0},{3,1},{4,6},{5,7},{6,4},{7,5},{8,10},{9,11},{10,... | collective-permute-start | bytes 61448 | tf_op jit(solution)/shard_map/ppermute | solution.py:30
  32.0 3.8 %collective-permute-start.8 = (f32[8,384]{1,0:T(8,128)S(1)}, f32[8,384]{1,0:T(8,128)S(1)}, u32[]{:S(2)}, u32[]{:S(2)}) collective-permute-start(f32[8,384]{1,0:T(8,128)S(1)} %pad_maximum_fusion.2), channel_id=1, source_target_pairs={{0,1},{1,0},{2,3},{3,2},{4,5},{5,4},{6,7},{7,6},{8,9},{9,8},{10,11... | collective-permute-start | bytes 36872 | tf_op jit(solution)/shard_map/ppermute | solution.py:30

commit v2 on v1

v2 whole, which is shorter than its diff:
```python
import jax
import jax.numpy as jnp
from jax import lax
from jax.sharding import PartitionSpec as P

SUB = 128
AXES = ("row", "col")


def bits_of(axis):
    return range(lax.axis_size(axis).bit_length() - 1)


def send(block, target):
    rows, cols = lax.axis_size("row"), lax.axis_size("col")
    pairs = []
    for r in range(rows):
        for c in range(cols):
            to_row, to_col = target(r, c)
            pairs.append((r * cols + c, (to_row % rows) * cols + to_col))
    return lax.ppermute(block, AXES, pairs)


def across_row(block, bit):
    return send(block, lambda r, c: (r ^ (1 << bit) ^ (1 if bit else 0), c))


def across_col(block, bit):
    return send(block, lambda r, c: (r, c ^ (1 << bit)))


def from_far(block):
    return send(block, lambda r, c: (r - c if c else r ^ 1, c))


def to_far(block):
    return send(block, lambda r, c: (r + c if c else r ^ 1, c))


def on_device(tiles, block_map, lanczos_block):
    width = tiles.shape[0]
    vectors = lanczos_block.shape[0]
    groups = width // SUB
    rows = lax.axis_size("row")
    row_idx = lax.axis_index("row")
    col_idx = lax.axis_index("col")

    keep = block_map[0, 0].astype(jnp.bfloat16)
    matrix = (tiles.reshape(groups, SUB, groups, SUB) * keep[:, None, :, None]).reshape(
        width, width
    )

    source = lanczos_block
    for bit in bits_of("col"):
        other = across_col(source, bit)
        upper = (col_idx >> bit) % 2 == 1
        zero = jnp.zeros_like(source)
        low, high = jnp.where(upper, zero, source), jnp.where(upper, source, zero)
        if bit == 0:
            low, high = lax.optimization_barrier((low, high))
        source = jnp.concatenate(
            [jnp.where(upper, other, low), jnp.where(upper, high, other)], axis=1
        )
    far_vec = from_far(source)
    mirror = jnp.dot(source, matrix, preferred_element_type=jnp.float32)
    arrived = to_far(mirror)
    inside = row_idx + col_idx < rows
    far_vec = jnp.where(inside, far_vec, jnp.zeros_like(far_vec))
    far_vec = jnp.where(col_idx == 0, source, far_vec)
    gram = lax.dot_general(
        mirror,
        far_vec.astype(jnp.float32),
        (((1,), (1,)), ((), ())),
        precision=lax.Precision.HIGHEST,
    )
    plain = lax.dot_general(
        far_vec, matrix, (((1,), (1,)), ((), ())), preferred_element_type=jnp.float32
    )
    for bit in bits_of("row"):
        gram = gram + across_row(gram, bit)
        if bit == 1:
            gram, plain = lax.optimization_barrier((gram, plain))
    gram = jnp.pad(gram, ((0, 0), (0, SUB - vectors)))
    arrived = jnp.where(row_idx >= col_idx, arrived, jnp.zeros_like(arrived))
    arrived = jnp.where(col_idx == 0, mirror, arrived)
    sums = plain + arrived
    for bit in reversed(bits_of("col")):
        half = sums.shape[1] // 2
        upper = (col_idx >> bit) % 2 == 1
        given = jnp.where(upper, sums[:, :half], sums[:, half:])
        kept = jnp.where(upper, sums[:, half:], sums[:, :half])
        other = across_col(jnp.concatenate([given, gram], axis=1), bit)
        sums = kept + other[:, :half]
        gram = gram + other[:, half:]
    gram = gram[:, :vectors]
    projected = (gram + gram.T) * (1.0 / jnp.sqrt(jnp.float32(width * rows)))
    return (sums, projected)


def solution(mesh):
    placed = (P("row", "col"), P("row", "col", None, None), P(None, ("row", "col")))
    return jax.shard_map(
        on_device,
        mesh=mesh,
        in_specs=placed,
        out_specs=(P(None, ("row", "col")), P()),
        check_vma=False,
    )
```

time: 37.2 us -> 33 us (0.89)
  starting transfers between devices: 20.3 us -> 17.8 us
  waiting for transfers between devices: 11.6 us -> 9.94 us
    ppermute x9, starting transfers between devices: 20.3 us -> 17.8 us  [send(): return lax.ppermute(block, AXES, pairs)]
    ppermute x9, waiting for transfers between devices: 11.6 us -> 9.94 us  [send(): return lax.ppermute(block, AXES, pairs)]
  transfers between devices with their start and end apart: 9 -> 9, of which waited for: 7 -> 8; matrix products, arithmetic and copies ran while one was open for 4% -> 9% of each run, Pallas kernels for 0% -> 0%
where the time goes in v2:
time: 33 us; the launch traced here: 32.8 us
  starting transfers between devices  17.8 us (54%)
  waiting for transfers between devices  9.94 us (30%)
  other arithmetic  2.69 us (8%)
  matrix products  1.23 us (4%)
  between operations  0.72 us (2%)
  local copies, waits for them, and re-layouts  0.42 us (1%)
    ppermute x9, starting transfers between devices, send(): return lax.ppermute(block, AXES, pairs)  17.8 us
    ppermute x9, waiting for transfers between devices, send(): return lax.ppermute(block, AXES, pairs)  9.94 us
    select_n x1, other arithmetic, on_device(): low, high = (jnp.where(upper, zero, source), jnp.where(upper, source, zero))  0.72 us
    convert_element_type x1, other arithmetic, on_device(): keep = block_map[0, 0].astype(jnp.bfloat16)  0.69 us
  transfers between devices with their start and end apart: 9, of which 8 were waited for; matrix products, arithmetic and copies ran while one was open for 9% of the time, Pallas kernels for 0%

profile of v2, /device:TPU:0, one launch (start us, length us, event | category | flops | bytes accessed | tf_op | source)
XLA Modules:
  0.0 32.8 jit_solution(1067744268896291440)
XLA Ops:
  0.6 0.0 copy-start
  0.6 3.1 %collective-permute-start = (bf16[8,256]{1,0:T(8,128)(2,1)}, bf16[8,256]{1,0:T(8,128)(2,1)S(1)}, u32[]{:S(2)}, u32[]{:S(2)}) collective-permute-start(bf16[8,256]{1,0:T(8,128)(2,1)} %param.5), channel_id=1, source_target_pairs={{0,1},{1,0},{2,3},{3,2},{4,5},{5,4},{6,7},{7,6},{8,9},{9,8},{10,11... | collective-permute-start | bytes 12296 | tf_op jit(solution)/shard_map/ppermute | solution.py:21
  3.7 0.7 %broadcast_select_fusion.2 = (bf16[8,256]{1,0:T(8,128)(2,1)S(1)}, bf16[8,256]{1,0:T(8,128)(2,1)S(1)}) fusion(bf16[8,256]{1,0:T(8,128)(2,1)} %param.5, pred[]{:T(512)S(6)} %eq.17), kind=kLoop, calls=%fused_computation.21 | loop fusion | flops 4096 | bytes 12289 | tf_op jit(solution)/shard_map/jit(_where)/select_n | solution.py:58
  4.5 1.1 %collective-permute-done = bf16[8,256]{1,0:T(8,128)(2,1)S(1)} collective-permute-done((bf16[8,256]{1,0:T(8,128)(2,1)}, bf16[8,256]{1,0:T(8,128)(2,1)S(1)}, u32[]{:S(2)}, u32[]{:S(2)}) %collective-permute-start) | collective-permute-done | bytes 4128 | tf_op jit(solution)/shard_map/ppermute | solution.py:21
  5.5 3.1 %collective-permute-start.1 = (bf16[8,512]{1,0:T(8,128)(2,1)S(1)}, bf16[8,512]{1,0:T(8,128)(2,1)S(1)}, u32[]{:S(2)}, u32[]{:S(2)}) collective-permute-start(bf16[8,512]{1,0:T(8,128)(2,1)S(1)} %pad_maximum_fusion.3), channel_id=1, source_target_pairs={{0,2},{1,3},{2,0},{3,1},{4,6},{5,7},{6,4},{7,5},{8,10},{9,11},{10,... | collective-permute-start | bytes 24584 | tf_op jit(solution)/shard_map/ppermute | solution.py:21
  8.6 0.7 %convert_bitcast_fusion = bf16[8,8]{1,0:T(8,128)(2,1)S(1)} fusion(s32[1,1,8,8]{3,2,1,0:T(8,128)} %param.4), kind=kLoop, calls=%fused_computation.24 | loop fusion | flops 64 | bytes 384 | tf_op jit(solution)/shard_map/convert_element_type | solution.py:48
  9.3 0.9 %collective-permute-done.1 = bf16[8,512]{1,0:T(8,128)(2,1)S(1)} collective-permute-done((bf16[8,512]{1,0:T(8,128)(2,1)S(1)}, bf16[8,512]{1,0:T(8,128)(2,1)S(1)}, u32[]{:S(2)}, u32[]{:S(2)}) %collective-permute-start.1) | collective-permute-done | bytes 8224 | tf_op jit(solution)/shard_map/ppermute | solution.py:21
  10.3 0.1 collective-permute-start.2
  10.3 0.3 %mul.17 = bf16[8,128,8,128]{3,2,1,0:T(8,128)(2,1)S(1)} broadcast(bf16[8,8]{1,0:T(8,128)(2,1)S(1)} %convert_bitcast_fusion), dimensions={0,2} | broadcast | bytes 2097280 | tf_op jit(solution)/shard_map/mul | solution.py:49
  10.7 0.0 copy-done
  10.7 0.5 %fusion.1 = f32[8,1024]{1,0:T(8,128)S(1)} fusion(bf16[1024,1024]{1,0:T(8,128)(2,1)S(1)} %copy-done, bf16[128,8,8,128]{3,2,1,0:T(8,128)(2,1)S(1)} %bitcast.14, bf16[8,512]{1,0:T(8,128)(2,1)S(1)} %get-tuple-element.11, bf16[8,512]{1,0:T(8,128)(2,1)S(1)} %get-tuple-element.10), kind=kOutput, calls=%fused_computation.2 | convolution fusion | flops 17858560 | bytes 4243456 | tf_op jit(solution)/shard_map/dot_general | solution.py:65
  11.2 0.4 %collective-permute-done.2 = bf16[8,1024]{1,0:T(8,128)(2,1)S(1)} collective-permute-done((bf16[8,1024]{1,0:T(8,128)(2,1)S(1)}, bf16[8,1024]{1,0:T(8,128)(2,1)S(1)}, u32[]{:S(2)}, u32[]{:S(2)}) %collective-permute-start.2) | collective-permute-done | bytes 16416 | tf_op jit(solution)/shard_map/ppermute | solution.py:21
  11.5 0.1 fusion.3
  11.6 0.2 collective-permute-start.3
  11.8 0.3 %collective-permute-start.5 = (f32[8,1024]{1,0:T(8,128)S(1)}, f32[8,1024]{1,0:T(8,128)S(1)}, u32[]{:S(2)}, u32[]{:S(2)}) collective-permute-start(f32[8,1024]{1,0:T(8,128)S(1)} %fusion.1), channel_id=1, source_target_pairs={{0,4},{1,5},{2,10},{3,15},{4,0},{5,9},{6,14},{7,19},{8,12},{9,13},... | collective-permute-start | bytes 98312 | tf_op jit(solution)/shard_map/ppermute | solution.py:21
  12.2 0.7 %collective-permute-done.3 = f32[8,8]{1,0:T(8,128)S(1)} collective-permute-done((f32[8,8]{1,0:T(8,128)S(1)}, f32[8,8]{1,0:T(8,128)S(1)}, u32[]{:S(2)}, u32[]{:S(2)}) %collective-permute-start.3) | collective-permute-done | bytes 288 | tf_op jit(solution)/shard_map/ppermute | solution.py:21
  12.8 1.6 %collective-permute-start.4 = (f32[8,8]{1,0:T(8,128)S(1)}, f32[8,8]{1,0:T(8,128)S(1)}, u32[]{:S(2)}, u32[]{:S(2)}) collective-permute-start(f32[8,8]{1,0:T(8,128)S(1)} %add.44), channel_id=1, source_target_pairs={{0,12},{1,13},{2,14},{3,15},{4,8},{5,9},{6,10},{7,11},{8,4},{9,5},... | collective-permute-start | bytes 776 | tf_op jit(solution)/shard_map/ppermute | solution.py:21
  14.4 0.7 %fusion = f32[8,1024]{1,0:T(8,128)S(1)} fusion(bf16[1024,1024]{1,0:T(8,128)(2,1)S(1)} %copy-done, bf16[128,8,8,128]{3,2,1,0:T(8,128)(2,1)S(1)} %bitcast.15, bf16[8,1024]{1,0:T(8,128)(2,1)S(1)} %collective-permute-done.2, pred[]{:T(512)S(6)} %lt.19, pred[]{:T(512)S(6)} %eq.19, bf16[8,512]{1,0:T(8,128)(2,1)S(1)} %get-tuple-element.11, ...), kind=kOutput, calls=%fused_computation.1 | convolution fusion | flops 17874944 | bytes 4259842 | tf_op jit(solution)/shard_map/dot_general | solution.py:76
  15.1 0.8 %collective-permute-done.4 = f32[8,8]{1,0:T(8,128)S(1)} collective-permute-done((f32[8,8]{1,0:T(8,128)S(1)}, f32[8,8]{1,0:T(8,128)S(1)}, u32[]{:S(2)}, u32[]{:S(2)}) %collective-permute-start.4) | collective-permute-done | bytes 288 | tf_op jit(solution)/shard_map/ppermute | solution.py:21
  15.9 1.6 %collective-permute-start.6 = (f32[8,8]{1,0:T(8,128)S(1)}, f32[8,8]{1,0:T(8,128)S(1)}, u32[]{:S(2)}, u32[]{:S(2)}) collective-permute-start(f32[8,8]{1,0:T(8,128)S(1)} %add.45), channel_id=1, source_target_pairs={{0,20},{1,21},{2,22},{3,23},{4,16},{5,17},{6,18},{7,19},{8,28},{9,... | collective-permute-start | bytes 776 | tf_op jit(solution)/shard_map/ppermute | solution.py:21
  17.5 1.4 %collective-permute-done.6 = f32[8,8]{1,0:T(8,128)S(1)} collective-permute-done((f32[8,8]{1,0:T(8,128)S(1)}, f32[8,8]{1,0:T(8,128)S(1)}, u32[]{:S(2)}, u32[]{:S(2)}) %collective-permute-start.6) | collective-permute-done | bytes 288 | tf_op jit(solution)/shard_map/ppermute | solution.py:21
  18.9 0.0 collective-permute-done.5
  19.0 6.8 %collective-permute-start.7 = (f32[8,640]{1,0:T(8,128)S(1)}, f32[8,640]{1,0:T(8,128)S(1)}, u32[]{:S(2)}, u32[]{:S(2)}) collective-permute-start(f32[8,640]{1,0:T(8,128)S(1)} %pad_maximum_fusion), channel_id=1, source_target_pairs={{0,2},{1,3},{2,0},{3,1},{4,6},{5,7},{6,4},{7,5},{8,10},{9,11},{10,... | collective-permute-start | bytes 61448 | tf_op jit(solution)/shard_map/ppermute | solution.py:21
  25.8 1.9 %collective-permute-done.7 = f32[8,640]{1,0:T(8,128)S(1)} collective-permute-done((f32[8,640]{1,0:T(8,128)S(1)}, f32[8,640]{1,0:T(8,128)S(1)}, u32[]{:S(2)}, u32[]{:S(2)}) %collective-permute-start.7) | collective-permute-done | bytes 20512 | tf_op jit(solution)/shard_map/ppermute | solution.py:21
  27.7 1.0 %collective-permute-start.8 = (f32[8,384]{1,0:T(8,128)S(1)}, f32[8,384]{1,0:T(8,128)S(1)}, u32[]{:S(2)}, u32[]{:S(2)}) collective-permute-start(f32[8,384]{1,0:T(8,128)S(1)} %pad_maximum_fusion.2), channel_id=1, source_target_pairs={{0,1},{1,0},{2,3},{3,2},{4,5},{5,4},{6,7},{7,6},{8,9},{9,8},{10,11... | collective-permute-start | bytes 36872 | tf_op jit(solution)/shard_map/ppermute | solution.py:21
  28.7 2.8 %collective-permute-done.8 = f32[8,384]{1,0:T(8,128)S(1)} collective-permute-done((f32[8,384]{1,0:T(8,128)S(1)}, f32[8,384]{1,0:T(8,128)S(1)}, u32[]{:S(2)}, u32[]{:S(2)}) %collective-permute-start.8) | collective-permute-done | bytes 12320 | tf_op jit(solution)/shard_map/ppermute | solution.py:21
  31.5 0.1 copy.5
  31.6 0.6 %fusion.2 = f32[8,8]{1,0:T(8,128)} fusion(f32[8,8]{0,1:T(8,128)S(1)} %copy.5, f32[8,128]{1,0:T(8,128)S(1)} %slice_add_fusion.2), kind=kLoop, calls=%fused_computation.18 | loop fusion | flops 128 | bytes 768 | tf_op jit(solution)/shard_map/mul | solution.py:96
  32.2 0.6 %slice_add_fusion.1 = f32[8,256]{1,0:T(8,128)} fusion(f32[8,384]{1,0:T(8,128)S(1)} %collective-permute-done.8, f32[8,512]{1,0:T(8,128)S(1)} %slice_add_fusion, pred[]{:T(512)S(6)} %eq.17), kind=kLoop, calls=%fused_computation.10 | loop fusion | flops 4096 | bytes 32769 | tf_op jit(solution)/shard_map/add | solution.py:93
  (16 shorter events, 0.1 us)
Async XLA Ops:
  0.6 10.1 %copy-start = (bf16[1024,1024]{1,0:T(8,128)(2,1)S(1)}, bf16[1024,1024]{1,0:T(8,128)(2,1)}, u32[]{:S(2)}) copy-start(bf16[1024,1024]{1,0:T(8,128)(2,1)} %param.3) | copy-start | bytes 6291460
  0.6 4.9 %collective-permute-start = (bf16[8,256]{1,0:T(8,128)(2,1)}, bf16[8,256]{1,0:T(8,128)(2,1)S(1)}, u32[]{:S(2)}, u32[]{:S(2)}) collective-permute-start(bf16[8,256]{1,0:T(8,128)(2,1)} %param.5), channel_id=1, source_target_pairs={{0,1},{1,0},{2,3},{3,2},{4,5},{5,4},{6,7},{7,6},{8,9},{9,8},{10,11... | collective-permute-start | bytes 12296 | tf_op jit(solution)/shard_map/ppermute | solution.py:21
  5.5 4.7 %collective-permute-start.1 = (bf16[8,512]{1,0:T(8,128)(2,1)S(1)}, bf16[8,512]{1,0:T(8,128)(2,1)S(1)}, u32[]{:S(2)}, u32[]{:S(2)}) collective-permute-start(bf16[8,512]{1,0:T(8,128)(2,1)S(1)} %pad_maximum_fusion.3), channel_id=1, source_target_pairs={{0,2},{1,3},{2,0},{3,1},{4,6},{5,7},{6,4},{7,5},{8,10},{9,11},{10,... | collective-permute-start | bytes 24584 | tf_op jit(solution)/shard_map/ppermute | solution.py:21
  10.3 1.2 %collective-permute-start.2 = (bf16[8,1024]{1,0:T(8,128)(2,1)S(1)}, bf16[8,1024]{1,0:T(8,128)(2,1)S(1)}, u32[]{:S(2)}, u32[]{:S(2)}) collective-permute-start(bf16[8,1024]{1,0:T(8,128)(2,1)S(1)} %pad_maximum_fusion.1), channel_id=1, source_target_pairs={{0,4},{1,29},{2,26},{3,23},{4,0},{5,1},{6,30},{7,27},{8,12},{9,5},... | collective-permute-start | bytes 49160 | tf_op jit(solution)/shard_map/ppermute | solution.py:21
  11.6 1.2 %collective-permute-start.3 = (f32[8,8]{1,0:T(8,128)S(1)}, f32[8,8]{1,0:T(8,128)S(1)}, u32[]{:S(2)}, u32[]{:S(2)}) collective-permute-start(f32[8,8]{1,0:T(8,128)S(1)} %fusion.3), channel_id=1, source_target_pairs={{0,4},{1,5},{2,6},{3,7},{4,0},{5,1},{6,2},{7,3},{8,12},{9,13},{10,... | collective-permute-start | bytes 776 | tf_op jit(solution)/shard_map/ppermute | solution.py:21
  11.8 7.1 %collective-permute-start.5 = (f32[8,1024]{1,0:T(8,128)S(1)}, f32[8,1024]{1,0:T(8,128)S(1)}, u32[]{:S(2)}, u32[]{:S(2)}) collective-permute-start(f32[8,1024]{1,0:T(8,128)S(1)} %fusion.1), channel_id=1, source_target_pairs={{0,4},{1,5},{2,10},{3,15},{4,0},{5,9},{6,14},{7,19},{8,12},{9,13},... | collective-permute-start | bytes 98312 | tf_op jit(solution)/shard_map/ppermute | solution.py:21
  12.8 3.0 %collective-permute-start.4 = (f32[8,8]{1,0:T(8,128)S(1)}, f32[8,8]{1,0:T(8,128)S(1)}, u32[]{:S(2)}, u32[]{:S(2)}) collective-permute-start(f32[8,8]{1,0:T(8,128)S(1)} %add.44), channel_id=1, source_target_pairs={{0,12},{1,13},{2,14},{3,15},{4,8},{5,9},{6,10},{7,11},{8,4},{9,5},... | collective-permute-start | bytes 776 | tf_op jit(solution)/shard_map/ppermute | solution.py:21
  15.9 3.0 %collective-permute-start.6 = (f32[8,8]{1,0:T(8,128)S(1)}, f32[8,8]{1,0:T(8,128)S(1)}, u32[]{:S(2)}, u32[]{:S(2)}) collective-permute-start(f32[8,8]{1,0:T(8,128)S(1)} %add.45), channel_id=1, source_target_pairs={{0,20},{1,21},{2,22},{3,23},{4,16},{5,17},{6,18},{7,19},{8,28},{9,... | collective-permute-start | bytes 776 | tf_op jit(solution)/shard_map/ppermute | solution.py:21
  19.0 8.7 %collective-permute-start.7 = (f32[8,640]{1,0:T(8,128)S(1)}, f32[8,640]{1,0:T(8,128)S(1)}, u32[]{:S(2)}, u32[]{:S(2)}) collective-permute-start(f32[8,640]{1,0:T(8,128)S(1)} %pad_maximum_fusion), channel_id=1, source_target_pairs={{0,2},{1,3},{2,0},{3,1},{4,6},{5,7},{6,4},{7,5},{8,10},{9,11},{10,... | collective-permute-start | bytes 61448 | tf_op jit(solution)/shard_map/ppermute | solution.py:21
  27.7 3.8 %collective-permute-start.8 = (f32[8,384]{1,0:T(8,128)S(1)}, f32[8,384]{1,0:T(8,128)S(1)}, u32[]{:S(2)}, u32[]{:S(2)}) collective-permute-start(f32[8,384]{1,0:T(8,128)S(1)} %pad_maximum_fusion.2), channel_id=1, source_target_pairs={{0,1},{1,0},{2,3},{3,2},{4,5},{5,4},{6,7},{7,6},{8,9},{9,8},{10,11... | collective-permute-start | bytes 36872 | tf_op jit(solution)/shard_map/ppermute | solution.py:21

commit v3 on v2

v3 whole, which is shorter than its diff:
```python
import jax
import jax.numpy as jnp
from jax import lax
from jax.sharding import PartitionSpec as P

SUB = 128
AXES = ("row", "col")


def send(block, target):
    rows, cols = lax.axis_size("row"), lax.axis_size("col")
    pairs = []
    for r in range(rows):
        for c in range(cols):
            to_row, to_col = target(r, c)
            pairs.append((r * cols + c, (to_row % rows) * cols + to_col))
    return lax.ppermute(block, AXES, pairs)


def across_row(block, mask):
    return send(block, lambda r, c: (r ^ mask, c))


def across_col(block, mask):
    return send(block, lambda r, c: (r, c ^ mask))


def from_far(block):
    return send(block, lambda r, c: (r - c if c else r ^ 1, c))


def to_far(block):
    return send(block, lambda r, c: (r + c if c else r ^ 1, c))


def groups_of(first, last):
    return [(bit, 4 if bit + 1 < last else 2) for bit in range(first, last, 2)]


def choose(place, blocks):
    chosen = blocks[-1]
    for k in reversed(range(len(blocks) - 1)):
        chosen = jnp.where(place == k, blocks[k], chosen)
    return chosen


def tree_sum(blocks):
    while len(blocks) > 1:
        blocks = [a + b for a, b in zip(blocks[::2], blocks[1::2])]
    return blocks[0]


def on_device(tiles, block_map, lanczos_block):
    width = tiles.shape[0]
    vectors = lanczos_block.shape[0]
    parts = width // SUB
    rows, cols = lax.axis_size("row"), lax.axis_size("col")
    row_idx = lax.axis_index("row")
    col_idx = lax.axis_index("col")
    row_bits, col_bits = rows.bit_length() - 1, cols.bit_length() - 1

    keep = block_map[0, 0].astype(jnp.bfloat16)
    matrix = (tiles.reshape(parts, SUB, parts, SUB) * keep[:, None, :, None]).reshape(
        width, width
    )

    source = lanczos_block
    for bit, members in groups_of(0, col_bits):
        place = (col_idx >> bit) % members
        got = {k: across_col(source, k << bit) for k in reversed(range(1, members))}
        if members == 4:
            vals = lax.optimization_barrier(tuple(got[k] for k in (2, 3, 1)))
            got = dict(zip((2, 3, 1), vals))
        placed = jnp.concatenate(
            [
                jnp.where(place == at, source, jnp.zeros_like(source))
                for at in range(members)
            ],
            axis=1,
        )
        if bit == 0:
            placed = lax.optimization_barrier(placed)
        got[0] = jnp.zeros_like(source)
        source = placed + jnp.concatenate(
            [
                choose(place, [got[at ^ k] for k in range(members)])
                for at in range(members)
            ],
            axis=1,
        )
    far_vec = from_far(source)
    mirror = jnp.dot(source, matrix, preferred_element_type=jnp.float32)
    inside = row_idx + col_idx < rows
    far_vec = jnp.where(inside, far_vec, jnp.zeros_like(far_vec))
    far_vec = jnp.where(col_idx == 0, source, far_vec)
    gram = lax.dot_general(
        mirror,
        far_vec.astype(jnp.float32),
        (((1,), (1,)), ((), ())),
        precision=lax.Precision.HIGHEST,
    )
    plain = lax.dot_general(
        far_vec, matrix, (((1,), (1,)), ((), ())), preferred_element_type=jnp.float32
    )
    gram = gram + across_row(gram, 1)
    gram, plain = lax.optimization_barrier((gram, plain))
    arrived = to_far(mirror)
    for bit, members in groups_of(1, row_bits):
        got = {k: across_row(gram, k << bit | 1) for k in reversed(range(1, members))}
        if bit == 1 and 1 in got:
            got[1], arrived = lax.optimization_barrier((got[1], arrived))
        gram = tree_sum([gram] + [got[k] for k in range(1, members)])
    gram = jnp.pad(gram, ((0, 0), (0, SUB - vectors)))
    arrived = jnp.where(row_idx >= col_idx, arrived, jnp.zeros_like(arrived))
    arrived = jnp.where(col_idx == 0, mirror, arrived)
    sums = plain + arrived
    for bit, members in reversed(groups_of(0, col_bits)):
        place = (col_idx >> bit) % members
        pieces = jnp.split(sums, members, axis=1)
        given = {
            k: jnp.concatenate(
                [choose(place, [pieces[at ^ k] for at in range(members)]), gram], axis=1
            )
            for k in range(1, members)
        }
        got = {k: across_col(given[k], k << bit) for k in reversed(range(1, members))}
        own = jnp.concatenate([choose(place, pieces), gram], axis=1)
        others = (2, 1, 3) if members == 4 else (1,)
        both = tree_sum([own] + [got[k] for k in others])
        sums, gram = both[:, : -SUB], both[:, -SUB:]
    gram = gram[:, :vectors]
    projected = (gram + gram.T) * (1.0 / jnp.sqrt(jnp.float32(width * rows)))
    return (sums, projected)


def solution(mesh):
    placed = (P("row", "col"), P("row", "col", None, None), P(None, ("row", "col")))
    return jax.shard_map(
        on_device,
        mesh=mesh,
        in_specs=placed,
        out_specs=(P(None, ("row", "col")), P()),
        check_vma=False,
    )
```

time: 33 us -> 29.2 us (0.88)
  starting transfers between devices: 17.8 us -> 13.7 us
  other arithmetic: 2.69 us -> 2.04 us
  local copies, waits for them, and re-layouts: 0.42 us -> 1.01 us
    ppermute x9 -> x12, starting transfers between devices: 17.8 us -> 13.7 us  [send(): return lax.ppermute(block, AXES, pairs)]
    slice x0 -> x1, local copies, waits for them, and re-layouts: none -> 0.6 us  [on_device(): sums, gram = (both[:, :-SUB], both[:, -SUB:])]
    add x7 -> x4, other arithmetic: 0.62 us -> 0.03 us  [the longest x2 0.01 us: tree_sum(): blocks = [a + b for a, b in zip(blocks[::2], blocks[1::2])]]
    ppermute x9 -> x12, waiting for transfers between devices: 9.94 us -> 10.2 us  [send(): return lax.ppermute(block, AXES, pairs)]
    select_n x5 -> x3, other arithmetic: 0.75 us -> 0.71 us  [the longest x1 0.69 us: on_device(): jnp.where(place == at, source, jnp.zeros_like(source))]
  transfers between devices with their start and end apart: 9 -> 12, of which waited for: 8 -> 8; matrix products, arithmetic and copies ran while one was open for 9% -> 10% of each run, Pallas kernels for 0% -> 0%
where the time goes in v3:
time: 29.2 us; the launch traced here: 28.9 us
  starting transfers between devices  13.7 us (47%)
  waiting for transfers between devices  10.2 us (35%)
  other arithmetic  2.04 us (7%)
  matrix products  1.23 us (4%)
  local copies, waits for them, and re-layouts  1.01 us (3%)
  between operations  0.7 us (2%)
    ppermute x12, starting transfers between devices, send(): return lax.ppermute(block, AXES, pairs)  13.7 us
    ppermute x12, waiting for transfers between devices, send(): return lax.ppermute(block, AXES, pairs)  10.2 us
    select_n x1, other arithmetic, on_device(): jnp.where(place == at, source, jnp.zeros_like(source))  0.69 us
    convert_element_type x1, other arithmetic, on_device(): keep = block_map[0, 0].astype(jnp.bfloat16)  0.69 us
    dot_general x1, matrix products, on_device(): lax.dot_general(far_vec, matrix, (((1,), (1,)), ((), ())), preferred_elem...  0.65 us
    slice x1, local copies, waits for them, and re-layouts, on_device(): sums, gram = (both[:, :-SUB], both[:, -SUB:])  0.6 us
    mul x1, other arithmetic, on_device(): projected = (gram + gram.T) * (1.0 / jnp.sqrt(jnp.float32(width * rows)))  0.6 us
  transfers between devices with their start and end apart: 12, of which 8 were waited for; matrix products, arithmetic and copies ran while one was open for 10% of the time, Pallas kernels for 0%

profile of v3, /device:TPU:0, one launch (start us, length us, event | category | flops | bytes accessed | tf_op | source)
XLA Modules:
  0.0 28.9 jit_solution(3840256251665211488)
XLA Ops:
  0.6 4.1 %collective-permute-start = (bf16[8,256]{1,0:T(8,128)(2,1)}, bf16[8,256]{1,0:T(8,128)(2,1)S(1)}, u32[]{:S(2)}, u32[]{:S(2)}) collective-permute-start(bf16[8,256]{1,0:T(8,128)(2,1)} %param.5), channel_id=1, source_target_pairs={{0,2},{1,3},{2,0},{3,1},{4,6},{5,7},{6,4},{7,5},{8,10},{9,11},{10,... | collective-permute-start | bytes 12296 | tf_op jit(solution)/shard_map/ppermute | solution.py:17
  4.7 1.6 %collective-permute-start.2 = (bf16[8,256]{1,0:T(8,128)(2,1)}, bf16[8,256]{1,0:T(8,128)(2,1)S(1)}, u32[]{:S(2)}, u32[]{:S(2)}) collective-permute-start(bf16[8,256]{1,0:T(8,128)(2,1)} %param.5), channel_id=1, source_target_pairs={{0,1},{1,0},{2,3},{3,2},{4,5},{5,4},{6,7},{7,6},{8,9},{9,8},{10,11... | collective-permute-start | bytes 12296 | tf_op jit(solution)/shard_map/ppermute | solution.py:17
  6.3 0.0 collective-permute-start.1
  6.3 0.7 %convert_bitcast_fusion = bf16[8,8]{1,0:T(8,128)(2,1)S(1)} fusion(s32[1,1,8,8]{3,2,1,0:T(8,128)} %param.4), kind=kLoop, calls=%fused_computation.31 | loop fusion | flops 64 | bytes 384 | tf_op jit(solution)/shard_map/convert_element_type | solution.py:62
  7.0 0.7 %broadcast_select_fusion.3 = (bf16[8,256]{1,0:T(8,128)(2,1)S(1)}, bf16[8,256]{1,0:T(8,128)(2,1)S(1)}, bf16[8,256]{1,0:T(8,128)(2,1)S(1)}, bf16[8,256]{1,0:T(8,128)(2,1)S(1)}) fusion(bf16[8,256]{1,0:T(8,128)(2,1)} %param.5, pred[]{:T(512)S(6)} %eq.13, pred[]{:T(512)S(6)} %eq.16, pred[]{:T(512)S(6)} %eq.15, pred[]{:T(512)S(6)} %eq.14), kind=kLoop, calls=%fused_computation.29 | loop fusion | flops 8192 | bytes 20484 | tf_op jit(solution)/shard_map/jit(_where)/select_n | solution.py:76
  7.7 0.0 collective-permute-done
  7.7 0.8 %collective-permute-done.2 = bf16[8,256]{1,0:T(8,128)(2,1)S(1)} collective-permute-done((bf16[8,256]{1,0:T(8,128)(2,1)}, bf16[8,256]{1,0:T(8,128)(2,1)S(1)}, u32[]{:S(2)}, u32[]{:S(2)}) %collective-permute-start.2) | collective-permute-done | bytes 4128 | tf_op jit(solution)/shard_map/ppermute | solution.py:17
  8.6 3.4 %collective-permute-done.1 = bf16[8,256]{1,0:T(8,128)(2,1)S(1)} collective-permute-done((bf16[8,256]{1,0:T(8,128)(2,1)}, bf16[8,256]{1,0:T(8,128)(2,1)S(1)}, u32[]{:S(2)}, u32[]{:S(2)}) %collective-permute-start.1) | collective-permute-done | bytes 4128 | tf_op jit(solution)/shard_map/ppermute | solution.py:17
  12.0 0.1 collective-permute-start.3
  12.0 0.3 %mul.17 = bf16[8,128,8,128]{3,2,1,0:T(8,128)(2,1)S(1)} broadcast(bf16[8,8]{1,0:T(8,128)(2,1)S(1)} %convert_bitcast_fusion), dimensions={0,2} | broadcast | bytes 2097280 | tf_op jit(solution)/shard_map/mul | solution.py:63
  12.4 0.5 %fusion.1 = f32[8,1024]{1,0:T(8,128)S(1)} fusion(bf16[8,1024]{1,0:T(8,128)(2,1)S(1)} %maximum_add_fusion, bf16[1024,1024]{1,0:T(8,128)(2,1)S(1)} %copy-done, bf16[128,8,8,128]{3,2,1,0:T(8,128)(2,1)S(1)} %bitcast.14), kind=kOutput, calls=%fused_computation.2 | convolution fusion | flops 17825792 | bytes 4243456 | tf_op jit(solution)/shard_map/dot_general | solution.py:92
  12.8 0.5 %collective-permute-start.6 = (f32[8,1024]{1,0:T(8,128)S(1)}, f32[8,1024]{1,0:T(8,128)S(1)}, u32[]{:S(2)}, u32[]{:S(2)}) collective-permute-start(f32[8,1024]{1,0:T(8,128)S(1)} %fusion.1), channel_id=1, source_target_pairs={{0,4},{1,5},{2,10},{3,15},{4,0},{5,9},{6,14},{7,19},{8,12},{9,13},... | collective-permute-start | bytes 98312 | tf_op jit(solution)/shard_map/ppermute | solution.py:17
  13.3 0.0 collective-permute-done.3
  13.3 0.1 fusion.9
  13.4 0.1 collective-permute-start.4
  13.5 0.7 %fusion = f32[8,1024]{1,0:T(8,128)S(1)} fusion(bf16[1024,1024]{1,0:T(8,128)(2,1)S(1)} %copy-done, bf16[128,8,8,128]{3,2,1,0:T(8,128)(2,1)S(1)} %bitcast.15, bf16[8,1024]{1,0:T(8,128)(2,1)S(1)} %maximum_add_fusion, bf16[8,1024]{1,0:T(8,128)(2,1)S(1)} %collective-permute-done.3, pred[]{:T(512)S(6)} %lt.12, pred[]{:T(512)S(6)} %eq.17), kind=kOutput, calls=%fused_computation.1 | convolution fusion | flops 17842176 | bytes 4259842 | tf_op jit(solution)/shard_map/dot_general | solution.py:102
  14.2 0.5 %collective-permute-done.4 = f32[8,8]{1,0:T(8,128)S(1)} collective-permute-done((f32[8,8]{1,0:T(8,128)S(1)}, f32[8,8]{1,0:T(8,128)S(1)}, u32[]{:S(2)}, u32[]{:S(2)}) %collective-permute-start.4) | collective-permute-done | bytes 288 | tf_op jit(solution)/shard_map/ppermute | solution.py:17
  14.7 1.3 %collective-permute-start.5 = (f32[8,8]{1,0:T(8,128)S(1)}, f32[8,8]{1,0:T(8,128)S(1)}, u32[]{:S(2)}, u32[]{:S(2)}) collective-permute-start(f32[8,8]{1,0:T(8,128)S(1)} %add.43), channel_id=1, source_target_pairs={{0,12},{1,13},{2,14},{3,15},{4,8},{5,9},{6,10},{7,11},{8,4},{9,5},... | collective-permute-start | bytes 776 | tf_op jit(solution)/shard_map/ppermute | solution.py:17
  15.9 1.4 %collective-permute-start.8 = (f32[8,8]{1,0:T(8,128)S(1)}, f32[8,8]{1,0:T(8,128)S(1)}, u32[]{:S(2)}, u32[]{:S(2)}) collective-permute-start(f32[8,8]{1,0:T(8,128)S(1)} %add.43), channel_id=1, source_target_pairs={{0,28},{1,29},{2,30},{3,31},{4,24},{5,25},{6,26},{7,27},{8,20},{9,... | collective-permute-start | bytes 776 | tf_op jit(solution)/shard_map/ppermute | solution.py:17
  17.4 0.3 collective-permute-start.7
  17.6 0.1 collective-permute-done.5
  17.7 0.0 collective-permute-done.6
  17.7 2.1 %collective-permute-done.8 = f32[8,8]{1,0:T(8,128)S(1)} collective-permute-done((f32[8,8]{1,0:T(8,128)S(1)}, f32[8,8]{1,0:T(8,128)S(1)}, u32[]{:S(2)}, u32[]{:S(2)}) %collective-permute-start.8) | collective-permute-done | bytes 288 | tf_op jit(solution)/shard_map/ppermute | solution.py:17
  19.8 0.6 %collective-permute-done.7 = f32[8,8]{1,0:T(8,128)S(1)} collective-permute-done((f32[8,8]{1,0:T(8,128)S(1)}, f32[8,8]{1,0:T(8,128)S(1)}, u32[]{:S(2)}, u32[]{:S(2)}) %collective-permute-start.7) | collective-permute-done | bytes 288 | tf_op jit(solution)/shard_map/ppermute | solution.py:17
  20.4 2.6 %collective-permute-start.11 = (f32[8,384]{1,0:T(8,128)S(1)}, f32[8,384]{1,0:T(8,128)S(1)}, u32[]{:S(2)}, u32[]{:S(2)}) collective-permute-start(f32[8,384]{1,0:T(8,128)S(1)} %get-tuple-element.24), channel_id=1, source_target_pairs={{0,3},{1,2},{2,1},{3,0},{4,7},{5,6},{6,5},{7,4},{8,11},{9,10},{10,... | collective-permute-start | bytes 36872 | tf_op jit(solution)/shard_map/ppermute | solution.py:17
  23.1 0.0 collective-permute-start.9
  23.1 1.8 %collective-permute-start.10 = (f32[8,384]{1,0:T(8,128)S(1)}, f32[8,384]{1,0:T(8,128)S(1)}, u32[]{:S(2)}, u32[]{:S(2)}) collective-permute-start(f32[8,384]{1,0:T(8,128)S(1)} %get-tuple-element.26), channel_id=1, source_target_pairs={{0,1},{1,0},{2,3},{3,2},{4,5},{5,4},{6,7},{7,6},{8,9},{9,8},{10,11... | collective-permute-start | bytes 36872 | tf_op jit(solution)/shard_map/ppermute | solution.py:17
  24.9 1.1 %collective-permute-done.11 = f32[8,384]{1,0:T(8,128)S(1)} collective-permute-done((f32[8,384]{1,0:T(8,128)S(1)}, f32[8,384]{1,0:T(8,128)S(1)}, u32[]{:S(2)}, u32[]{:S(2)}) %collective-permute-start.11) | collective-permute-done | bytes 12320 | tf_op jit(solution)/shard_map/ppermute | solution.py:17
  26.0 1.7 %collective-permute-done.9 = f32[8,384]{1,0:T(8,128)S(1)} collective-permute-done((f32[8,384]{1,0:T(8,128)S(1)}, f32[8,384]{1,0:T(8,128)S(1)}, u32[]{:S(2)}, u32[]{:S(2)}) %collective-permute-start.9) | collective-permute-done | bytes 12320 | tf_op jit(solution)/shard_map/ppermute | solution.py:17
  27.7 0.6 %slice.10 = f32[8,256]{1,0:T(8,128)} slice(f32[8,384]{1,0:T(8,128)S(1)} %fusion.7), slice={[0:8], [0:256]} | slice | bytes 16384 | tf_op jit(solution)/shard_map/slice | solution.py:130
  28.3 0.1 copy.5
  28.3 0.6 %fusion.8 = f32[8,8]{1,0:T(8,128)} fusion(f32[8,8]{0,1:T(8,128)S(1)} %copy.5, f32[8,384]{1,0:T(8,128)S(1)} %fusion.7), kind=kLoop, calls=%fused_computation.20 | loop fusion | flops 128 | bytes 768 | tf_op jit(solution)/shard_map/mul | solution.py:132
  (13 shorter events, 0.1 us)
Async XLA Ops:
  0.6 11.7 %copy-start = (bf16[1024,1024]{1,0:T(8,128)(2,1)S(1)}, bf16[1024,1024]{1,0:T(8,128)(2,1)}, u32[]{:S(2)}) copy-start(bf16[1024,1024]{1,0:T(8,128)(2,1)} %param.3) | copy-start | bytes 6291460
  0.6 7.1 %collective-permute-start = (bf16[8,256]{1,0:T(8,128)(2,1)}, bf16[8,256]{1,0:T(8,128)(2,1)S(1)}, u32[]{:S(2)}, u32[]{:S(2)}) collective-permute-start(bf16[8,256]{1,0:T(8,128)(2,1)} %param.5), channel_id=1, source_target_pairs={{0,2},{1,3},{2,0},{3,1},{4,6},{5,7},{6,4},{7,5},{8,10},{9,11},{10,... | collective-permute-start | bytes 12296 | tf_op jit(solution)/shard_map/ppermute | solution.py:17
  4.7 3.8 %collective-permute-start.2 = (bf16[8,256]{1,0:T(8,128)(2,1)}, bf16[8,256]{1,0:T(8,128)(2,1)S(1)}, u32[]{:S(2)}, u32[]{:S(2)}) collective-permute-start(bf16[8,256]{1,0:T(8,128)(2,1)} %param.5), channel_id=1, source_target_pairs={{0,1},{1,0},{2,3},{3,2},{4,5},{5,4},{6,7},{7,6},{8,9},{9,8},{10,11... | collective-permute-start | bytes 12296 | tf_op jit(solution)/shard_map/ppermute | solution.py:17
  6.3 5.6 %collective-permute-start.1 = (bf16[8,256]{1,0:T(8,128)(2,1)}, bf16[8,256]{1,0:T(8,128)(2,1)S(1)}, u32[]{:S(2)}, u32[]{:S(2)}) collective-permute-start(bf16[8,256]{1,0:T(8,128)(2,1)} %param.5), channel_id=1, source_target_pairs={{0,3},{1,2},{2,1},{3,0},{4,7},{5,6},{6,5},{7,4},{8,11},{9,10},{10,... | collective-permute-start | bytes 12296 | tf_op jit(solution)/shard_map/ppermute | solution.py:17
  12.0 1.4 %collective-permute-start.3 = (bf16[8,1024]{1,0:T(8,128)(2,1)S(1)}, bf16[8,1024]{1,0:T(8,128)(2,1)S(1)}, u32[]{:S(2)}, u32[]{:S(2)}) collective-permute-start(bf16[8,1024]{1,0:T(8,128)(2,1)S(1)} %maximum_add_fusion), channel_id=1, source_target_pairs={{0,4},{1,29},{2,26},{3,23},{4,0},{5,1},{6,30},{7,27},{8,12},{9,5},... | collective-permute-start | bytes 49160 | tf_op jit(solution)/shard_map/ppermute | solution.py:17
  12.8 4.9 %collective-permute-start.6 = (f32[8,1024]{1,0:T(8,128)S(1)}, f32[8,1024]{1,0:T(8,128)S(1)}, u32[]{:S(2)}, u32[]{:S(2)}) collective-permute-start(f32[8,1024]{1,0:T(8,128)S(1)} %fusion.1), channel_id=1, source_target_pairs={{0,4},{1,5},{2,10},{3,15},{4,0},{5,9},{6,14},{7,19},{8,12},{9,13},... | collective-permute-start | bytes 98312 | tf_op jit(solution)/shard_map/ppermute | solution.py:17
  13.4 1.2 %collective-permute-start.4 = (f32[8,8]{1,0:T(8,128)S(1)}, f32[8,8]{1,0:T(8,128)S(1)}, u32[]{:S(2)}, u32[]{:S(2)}) collective-permute-start(f32[8,8]{1,0:T(8,128)S(1)} %fusion.9), channel_id=1, source_target_pairs={{0,4},{1,5},{2,6},{3,7},{4,0},{5,1},{6,2},{7,3},{8,12},{9,13},{10,... | collective-permute-start | bytes 776 | tf_op jit(solution)/shard_map/ppermute | solution.py:17
  14.7 3.0 %collective-permute-start.5 = (f32[8,8]{1,0:T(8,128)S(1)}, f32[8,8]{1,0:T(8,128)S(1)}, u32[]{:S(2)}, u32[]{:S(2)}) collective-permute-start(f32[8,8]{1,0:T(8,128)S(1)} %add.43), channel_id=1, source_target_pairs={{0,12},{1,13},{2,14},{3,15},{4,8},{5,9},{6,10},{7,11},{8,4},{9,5},... | collective-permute-start | bytes 776 | tf_op jit(solution)/shard_map/ppermute | solution.py:17
  15.9 3.9 %collective-permute-start.8 = (f32[8,8]{1,0:T(8,128)S(1)}, f32[8,8]{1,0:T(8,128)S(1)}, u32[]{:S(2)}, u32[]{:S(2)}) collective-permute-start(f32[8,8]{1,0:T(8,128)S(1)} %add.43), channel_id=1, source_target_pairs={{0,28},{1,29},{2,30},{3,31},{4,24},{5,25},{6,26},{7,27},{8,20},{9,... | collective-permute-start | bytes 776 | tf_op jit(solution)/shard_map/ppermute | solution.py:17
  17.4 3.1 %collective-permute-start.7 = (f32[8,8]{1,0:T(8,128)S(1)}, f32[8,8]{1,0:T(8,128)S(1)}, u32[]{:S(2)}, u32[]{:S(2)}) collective-permute-start(f32[8,8]{1,0:T(8,128)S(1)} %add.43), channel_id=1, source_target_pairs={{0,20},{1,21},{2,22},{3,23},{4,16},{5,17},{6,18},{7,19},{8,28},{9,... | collective-permute-start | bytes 776 | tf_op jit(solution)/shard_map/ppermute | solution.py:17
  20.4 5.6 %collective-permute-start.11 = (f32[8,384]{1,0:T(8,128)S(1)}, f32[8,384]{1,0:T(8,128)S(1)}, u32[]{:S(2)}, u32[]{:S(2)}) collective-permute-start(f32[8,384]{1,0:T(8,128)S(1)} %get-tuple-element.24), channel_id=1, source_target_pairs={{0,3},{1,2},{2,1},{3,0},{4,7},{5,6},{6,5},{7,4},{8,11},{9,10},{10,... | collective-permute-start | bytes 36872 | tf_op jit(solution)/shard_map/ppermute | solution.py:17
  23.1 4.6 %collective-permute-start.9 = (f32[8,384]{1,0:T(8,128)S(1)}, f32[8,384]{1,0:T(8,128)S(1)}, u32[]{:S(2)}, u32[]{:S(2)}) collective-permute-start(f32[8,384]{1,0:T(8,128)S(1)} %get-tuple-element.25), channel_id=1, source_target_pairs={{0,2},{1,3},{2,0},{3,1},{4,6},{5,7},{6,4},{7,5},{8,10},{9,11},{10,... | collective-permute-start | bytes 36872 | tf_op jit(solution)/shard_map/ppermute | solution.py:17
  23.1 4.6 %collective-permute-start.10 = (f32[8,384]{1,0:T(8,128)S(1)}, f32[8,384]{1,0:T(8,128)S(1)}, u32[]{:S(2)}, u32[]{:S(2)}) collective-permute-start(f32[8,384]{1,0:T(8,128)S(1)} %get-tuple-element.26), channel_id=1, source_target_pairs={{0,1},{1,0},{2,3},{3,2},{4,5},{5,4},{6,7},{7,6},{8,9},{9,8},{10,11... | collective-permute-start | bytes 36872 | tf_op jit(solution)/shard_map/ppermute | solution.py:17

commit v4 on v3

v4 whole, which is shorter than its diff:
```python
import functools

import jax
import jax.numpy as jnp
from jax import lax
from jax.experimental import pallas as pl
from jax.experimental.pallas import tpu as pltpu
from jax.sharding import PartitionSpec as P

SUB = 128
AXES = ("row", "col")
ONE = ((1, 0),)
ROW_TABLES = ((1, 0, 3, 2), (2, 3, 0, 1), (3, 2, 1, 0))
ROW_ORDER = (0, 1, 2)
GATHER_TABLES = ((1, 0, 3, 2), (2, 3, 0, 1), (3, 2, 1, 0))
GATHER_ORDER = (1, 2, 0)
SUM_TABLES = ((1, 3, 0, 2), (3, 2, 1, 0), (2, 0, 3, 1))
SUM_ORDER = (1, 2, 0)


def send(block, target):
    rows, cols = lax.axis_size("row"), lax.axis_size("col")
    pairs = []
    for r in range(rows):
        for c in range(cols):
            to_row, to_col = target(r, c)
            pairs.append((r * cols + c, (to_row % rows) * cols + to_col))
    return lax.ppermute(block, AXES, pairs)


def moved(index, bit, table):
    size = len(table) - 1
    return index & ~(size << bit) | table[index >> bit & size] << bit


def exchanged(blocks, bit, tables, axis):
    if axis == "row":
        goes = [lambda r, c, t=t: (moved(r, bit, t) ^ 1, c) for t in tables]
    else:
        goes = [lambda r, c, t=t: (r, moved(c, bit, t)) for t in tables]
    return [send(block, to) for block, to in zip(blocks, goes)]


def held(blocks, order):
    if len(blocks) != len(order):
        return blocks
    kept = lax.optimization_barrier(tuple(blocks[k] for k in order))
    return [kept[order.index(k)] for k in range(len(blocks))]


def from_far(block):
    return send(block, lambda r, c: (r - c if c else r ^ 1, c))


def to_far(block):
    return send(block, lambda r, c: (r + c if c else r ^ 1, c))


def groups_of(first, last):
    return [(bit, 4 if bit + 1 < last else 2) for bit in range(first, last, 2)]


def choose(place, blocks):
    chosen = blocks[-1]
    for k in reversed(range(len(blocks) - 1)):
        chosen = jnp.where(place == k, blocks[k], chosen)
    return chosen


def in_place(own, got, tables, place):
    members = len(tables) + 1

    def source(d, k):
        return next(g for g, t in zip(got, tables) if t[d ^ k] == d)

    return [own] + [
        choose(place, [source(d, k) for d in range(members)]) for k in range(1, members)
    ]


def tree_sum(blocks):
    while len(blocks) > 1:
        blocks = [a + b for a, b in zip(blocks[::2], blocks[1::2])]
    return blocks[0]


def write_results(scale, both_ref, product_ref, projected_ref):
    vectors = projected_ref.shape[0]
    product_ref[...] = both_ref[:, :-SUB]
    gram = both_ref[:, -SUB:]
    square = jnp.concatenate([gram, jnp.zeros((SUB - vectors, SUB), jnp.float32)])
    gram = gram + square.T[:vectors]
    projected_ref[...] = (gram * scale)[:, :vectors]


def on_device(tiles, block_map, lanczos_block):
    width = tiles.shape[0]
    vectors = lanczos_block.shape[0]
    parts = width // SUB
    rows, cols = lax.axis_size("row"), lax.axis_size("col")
    row_idx = lax.axis_index("row")
    col_idx = lax.axis_index("col")
    row_bits, col_bits = rows.bit_length() - 1, cols.bit_length() - 1

    keep = block_map[0, 0].astype(jnp.bfloat16)
    matrix = (tiles.reshape(parts, SUB, parts, SUB) * keep[:, None, :, None]).reshape(
        width, width
    )

    source = lanczos_block
    for bit, members in groups_of(0, col_bits):
        place = (col_idx >> bit) % members
        tables = GATHER_TABLES if members == 4 else ONE
        got = held(
            exchanged([source] * len(tables), bit, tables, "col"), GATHER_ORDER
        )
        zero = jnp.zeros_like(source)
        placed = jnp.concatenate(
            [jnp.where(place == at, source, zero) for at in range(members)], axis=1
        )
        if bit == 0:
            placed = lax.optimization_barrier(placed)
        others = in_place(zero, got, tables, place)
        source = placed + jnp.concatenate(
            [
                choose(place, [others[at ^ d] for d in range(members)])
                for at in range(members)
            ],
            axis=1,
        )

    far_vec = from_far(source)
    mirror = jnp.dot(source, matrix, preferred_element_type=jnp.float32)
    inside = row_idx + col_idx < rows
    far_vec = jnp.where(inside, far_vec, jnp.zeros_like(far_vec))
    far_vec = jnp.where(col_idx == 0, source, far_vec)
    gram = lax.dot_general(
        mirror,
        far_vec.astype(jnp.float32),
        (((1,), (1,)), ((), ())),
        precision=lax.Precision.HIGHEST,
    )
    plain = lax.dot_general(
        far_vec, matrix, (((1,), (1,)), ((), ())), preferred_element_type=jnp.float32
    )

    gram = gram + send(gram, lambda r, c: (r ^ 1, c))
    gram, plain = lax.optimization_barrier((gram, plain))
    arrived = to_far(mirror)
    for bit, members in groups_of(1, row_bits):
        place = (row_idx >> bit) % members
        tables = ROW_TABLES if members == 4 else ONE
        got = exchanged([gram] * len(tables), bit, tables, "row")
        if bit == 1:
            got[0], arrived = lax.optimization_barrier((got[0], arrived))
        gram = tree_sum(in_place(gram, held(got, ROW_ORDER), tables, place))

    gram = jnp.pad(gram, ((0, 0), (0, SUB - vectors)))
    arrived = jnp.where(row_idx >= col_idx, arrived, jnp.zeros_like(arrived))
    arrived = jnp.where(col_idx == 0, mirror, arrived)
    both = jnp.concatenate([plain + arrived, gram], axis=1)
    for bit, members in reversed(groups_of(0, col_bits)):
        place = (col_idx >> bit) % members
        tables = SUM_TABLES if members == 4 else ONE
        pieces = jnp.split(both[:, :-SUB], members, axis=1)
        gram = both[:, -SUB:]
        given = [
            jnp.concatenate([choose(place, [pieces[to] for to in table]), gram], axis=1)
            for table in tables
        ]
        own = jnp.concatenate([choose(place, pieces), gram], axis=1)
        got = held(exchanged(given, bit, tables, "col"), SUM_ORDER)
        both = tree_sum(in_place(own, got, tables, place))

    return pl.pallas_call(
        functools.partial(write_results, 1.0 / (width * rows) ** 0.5),
        out_shape=(
            jax.ShapeDtypeStruct(lanczos_block.shape, jnp.float32),
            jax.ShapeDtypeStruct((vectors, vectors), jnp.float32),
        ),
        in_specs=[pl.BlockSpec(memory_space=pltpu.VMEM)],
        out_specs=(pl.BlockSpec(memory_space=pltpu.VMEM),) * 2,
        compiler_params=pltpu.CompilerParams(vmem_limit_bytes=1 << 20),
    )(both)


def solution(mesh):
    placed = (P("row", "col"), P("row", "col", None, None), P(None, ("row", "col")))
    return jax.shard_map(
        on_device,
        mesh=mesh,
        in_specs=placed,
        out_specs=(P(None, ("row", "col")), P()),
        check_vma=False,
    )
```

time: 29.2 us -> 27.9 us (0.955)
  waiting for transfers between devices: 10.2 us -> 9.38 us
  Pallas kernels: 0 us -> 0.67 us
  local copies, waits for them, and re-layouts: 1.01 us -> 0.34 us
  other arithmetic: 2.04 us -> 1.45 us
    ppermute x12, waiting for transfers between devices: 10.2 us -> 9.38 us  [send(): return lax.ppermute(block, AXES, pairs)]
    slice x3 -> x0, local copies, waits for them, and re-layouts: 0.67 us -> none  [the longest x1 0.6 us: on_device(): sums, gram = (both[:, :-SUB], both[:, -SUB:])]
    pallas_call x0 -> x1, Pallas kernels: none -> 0.67 us  [on_device(): pl.pallas_call(functools.partial(write_results, 1.0 / (width * rows) ** 0...]
    mul x1 -> x0, other arithmetic: 0.6 us -> none  [on_device(): projected = (gram + gram.T) * (1.0 / jnp.sqrt(jnp.float32(width * rows)))]
  transfers between devices with their start and end apart: 12 -> 12, of which waited for: 8 -> 8; matrix products, arithmetic and copies ran while one was open for 10% -> 11% of each run, Pallas kernels for 0% -> 0%
where the time goes in v4:
time: 27.9 us; the launch traced here: 27.7 us
  starting transfers between devices  13.9 us (50%)
  waiting for transfers between devices  9.38 us (34%)
  other arithmetic  1.45 us (5%)
  matrix products  1.23 us (4%)
  between operations  0.7 us (3%)
  Pallas kernels  0.67 us (2%)
  local copies, waits for them, and re-layouts  0.34 us (1%)
    ppermute x12, starting transfers between devices, send(): return lax.ppermute(block, AXES, pairs)  13.9 us
    ppermute x12, waiting for transfers between devices, send(): return lax.ppermute(block, AXES, pairs)  9.38 us
    select_n x1, other arithmetic, on_device(): jnp.where(place == at, source, zero)  0.69 us
    convert_element_type x1, other arithmetic, on_device(): keep = block_map[0, 0].astype(jnp.bfloat16)  0.69 us
    pallas_call x1, Pallas kernels, on_device(): pl.pallas_call(functools.partial(write_results, 1.0 / (width * rows) ** 0...  0.67 us
    dot_general x1, matrix products, on_device(): lax.dot_general(far_vec, matrix, (((1,), (1,)), ((), ())), preferred_elem...  0.65 us
  transfers between devices with their start and end apart: 12, of which 8 were waited for; matrix products, arithmetic and copies ran while one was open for 11% of the time, Pallas kernels for 0%

profile of v4, /device:TPU:0, one launch (start us, length us, event | category | flops | bytes accessed | tf_op | source)
XLA Modules:
  0.0 27.7 jit_solution(16068515268192105683)
XLA Ops:
  0.6 4.1 %collective-permute-start = (bf16[8,256]{1,0:T(8,128)(2,1)}, bf16[8,256]{1,0:T(8,128)(2,1)S(1)}, u32[]{:S(2)}, u32[]{:S(2)}) collective-permute-start(bf16[8,256]{1,0:T(8,128)(2,1)} %param.5), channel_id=1, source_target_pairs={{0,2},{1,3},{2,0},{3,1},{4,6},{5,7},{6,4},{7,5},{8,10},{9,11},{10,... | collective-permute-start | bytes 12296 | tf_op jit(solution)/shard_map/ppermute | solution.py:28
  4.7 1.6 %collective-permute-start.2 = (bf16[8,256]{1,0:T(8,128)(2,1)}, bf16[8,256]{1,0:T(8,128)(2,1)S(1)}, u32[]{:S(2)}, u32[]{:S(2)}) collective-permute-start(bf16[8,256]{1,0:T(8,128)(2,1)} %param.5), channel_id=1, source_target_pairs={{0,1},{1,0},{2,3},{3,2},{4,5},{5,4},{6,7},{7,6},{8,9},{9,8},{10,11... | collective-permute-start | bytes 12296 | tf_op jit(solution)/shard_map/ppermute | solution.py:28
  6.3 0.0 collective-permute-start.1
  6.3 0.7 %convert_bitcast_fusion = bf16[8,8]{1,0:T(8,128)(2,1)S(1)} fusion(s32[1,1,8,8]{3,2,1,0:T(8,128)} %param.4), kind=kLoop, calls=%fused_computation.34 | loop fusion | flops 64 | bytes 384 | tf_op jit(solution)/shard_map/convert_element_type | solution.py:105
  7.0 0.7 %broadcast_select_fusion.3 = (bf16[8,256]{1,0:T(8,128)(2,1)S(1)}, bf16[8,256]{1,0:T(8,128)(2,1)S(1)}, bf16[8,256]{1,0:T(8,128)(2,1)S(1)}, bf16[8,256]{1,0:T(8,128)(2,1)S(1)}) fusion(bf16[8,256]{1,0:T(8,128)(2,1)} %param.5, pred[]{:T(512)S(6)} %eq.14, pred[]{:T(512)S(6)} %eq.17, pred[]{:T(512)S(6)} %eq.16, pred[]{:T(512)S(6)} %eq.15), kind=kLoop, calls=%fused_computation.32 | loop fusion | flops 8192 | bytes 20484 | tf_op jit(solution)/shard_map/jit(_where)/select_n | solution.py:119
  7.7 0.0 collective-permute-done
  7.7 0.8 %collective-permute-done.2 = bf16[8,256]{1,0:T(8,128)(2,1)S(1)} collective-permute-done((bf16[8,256]{1,0:T(8,128)(2,1)}, bf16[8,256]{1,0:T(8,128)(2,1)S(1)}, u32[]{:S(2)}, u32[]{:S(2)}) %collective-permute-start.2) | collective-permute-done | bytes 4128 | tf_op jit(solution)/shard_map/ppermute | solution.py:28
  8.6 3.4 %collective-permute-done.1 = bf16[8,256]{1,0:T(8,128)(2,1)S(1)} collective-permute-done((bf16[8,256]{1,0:T(8,128)(2,1)}, bf16[8,256]{1,0:T(8,128)(2,1)S(1)}, u32[]{:S(2)}, u32[]{:S(2)}) %collective-permute-start.1) | collective-permute-done | bytes 4128 | tf_op jit(solution)/shard_map/ppermute | solution.py:28
  12.0 0.1 collective-permute-start.3
  12.0 0.3 %mul.11 = bf16[8,128,8,128]{3,2,1,0:T(8,128)(2,1)S(1)} broadcast(bf16[8,8]{1,0:T(8,128)(2,1)S(1)} %convert_bitcast_fusion), dimensions={0,2} | broadcast | bytes 2097280 | tf_op jit(solution)/shard_map/mul | solution.py:106
  12.4 0.0 copy-done
  12.4 0.5 %fusion.1 = f32[8,1024]{1,0:T(8,128)S(1)} fusion(bf16[8,1024]{1,0:T(8,128)(2,1)S(1)} %maximum_add_fusion, bf16[1024,1024]{1,0:T(8,128)(2,1)S(1)} %copy-done, bf16[128,8,8,128]{3,2,1,0:T(8,128)(2,1)S(1)} %bitcast.10), kind=kOutput, calls=%fused_computation.2 | convolution fusion | flops 17825792 | bytes 4243456 | tf_op jit(solution)/shard_map/dot_general | solution.py:133
  12.8 0.5 %collective-permute-start.6 = (f32[8,1024]{1,0:T(8,128)S(1)}, f32[8,1024]{1,0:T(8,128)S(1)}, u32[]{:S(2)}, u32[]{:S(2)}) collective-permute-start(f32[8,1024]{1,0:T(8,128)S(1)} %fusion.1), channel_id=1, source_target_pairs={{0,4},{1,5},{2,10},{3,15},{4,0},{5,9},{6,14},{7,19},{8,12},{9,13},... | collective-permute-start | bytes 98312 | tf_op jit(solution)/shard_map/ppermute | solution.py:28
  13.3 0.0 collective-permute-done.3
  13.3 0.1 fusion.11
  13.4 0.1 collective-permute-start.4
  13.5 0.7 %fusion = f32[8,1024]{1,0:T(8,128)S(1)} fusion(bf16[1024,1024]{1,0:T(8,128)(2,1)S(1)} %copy-done, bf16[128,8,8,128]{3,2,1,0:T(8,128)(2,1)S(1)} %bitcast.11, bf16[8,1024]{1,0:T(8,128)(2,1)S(1)} %maximum_add_fusion, bf16[8,1024]{1,0:T(8,128)(2,1)S(1)} %collective-permute-done.3, pred[]{:T(512)S(6)} %lt.14, pred[]{:T(512)S(6)} %eq.18), kind=kOutput, calls=%fused_computation.1 | convolution fusion | flops 17842176 | bytes 4259842 | tf_op jit(solution)/shard_map/dot_general | solution.py:143
  14.2 0.5 %collective-permute-done.4 = f32[8,8]{1,0:T(8,128)S(1)} collective-permute-done((f32[8,8]{1,0:T(8,128)S(1)}, f32[8,8]{1,0:T(8,128)S(1)}, u32[]{:S(2)}, u32[]{:S(2)}) %collective-permute-start.4) | collective-permute-done | bytes 288 | tf_op jit(solution)/shard_map/ppermute | solution.py:28
  14.7 1.3 %collective-permute-start.5 = (f32[8,8]{1,0:T(8,128)S(1)}, f32[8,8]{1,0:T(8,128)S(1)}, u32[]{:S(2)}, u32[]{:S(2)}) collective-permute-start(f32[8,8]{1,0:T(8,128)S(1)} %add.41), channel_id=1, source_target_pairs={{0,12},{1,13},{2,14},{3,15},{4,8},{5,9},{6,10},{7,11},{8,4},{9,5},... | collective-permute-start | bytes 776 | tf_op jit(solution)/shard_map/ppermute | solution.py:28
  15.9 1.4 %collective-permute-start.8 = (f32[8,8]{1,0:T(8,128)S(1)}, f32[8,8]{1,0:T(8,128)S(1)}, u32[]{:S(2)}, u32[]{:S(2)}) collective-permute-start(f32[8,8]{1,0:T(8,128)S(1)} %add.41), channel_id=1, source_target_pairs={{0,28},{1,29},{2,30},{3,31},{4,24},{5,25},{6,26},{7,27},{8,20},{9,... | collective-permute-start | bytes 776 | tf_op jit(solution)/shard_map/ppermute | solution.py:28
  17.4 0.3 %collective-permute-start.7 = (f32[8,8]{1,0:T(8,128)S(1)}, f32[8,8]{1,0:T(8,128)S(1)}, u32[]{:S(2)}, u32[]{:S(2)}) collective-permute-start(f32[8,8]{1,0:T(8,128)S(1)} %add.41), channel_id=1, source_target_pairs={{0,20},{1,21},{2,22},{3,23},{4,16},{5,17},{6,18},{7,19},{8,28},{9,... | collective-permute-start | bytes 776 | tf_op jit(solution)/shard_map/ppermute | solution.py:28
  17.6 0.1 collective-permute-done.5
  17.7 0.0 collective-permute-done.6
  17.7 2.1 %collective-permute-done.8 = f32[8,8]{1,0:T(8,128)S(1)} collective-permute-done((f32[8,8]{1,0:T(8,128)S(1)}, f32[8,8]{1,0:T(8,128)S(1)}, u32[]{:S(2)}, u32[]{:S(2)}) %collective-permute-start.8) | collective-permute-done | bytes 288 | tf_op jit(solution)/shard_map/ppermute | solution.py:28
  19.8 0.6 %collective-permute-done.7 = f32[8,8]{1,0:T(8,128)S(1)} collective-permute-done((f32[8,8]{1,0:T(8,128)S(1)}, f32[8,8]{1,0:T(8,128)S(1)}, u32[]{:S(2)}, u32[]{:S(2)}) %collective-permute-start.7) | collective-permute-done | bytes 288 | tf_op jit(solution)/shard_map/ppermute | solution.py:28
  20.4 0.1 collective-permute-start.11
  20.5 2.8 %collective-permute-start.9 = (f32[8,384]{1,0:T(8,128)S(1)}, f32[8,384]{1,0:T(8,128)S(1)}, u32[]{:S(2)}, u32[]{:S(2)}) collective-permute-start(f32[8,384]{1,0:T(8,128)S(1)} %get-tuple-element.37), channel_id=1, source_target_pairs={{0,3},{1,2},{2,1},{3,0},{4,7},{5,6},{6,5},{7,4},{8,11},{9,10},{10,... | collective-permute-start | bytes 36872 | tf_op jit(solution)/shard_map/ppermute | solution.py:28
  23.3 1.8 %collective-permute-start.10 = (f32[8,384]{1,0:T(8,128)S(1)}, f32[8,384]{1,0:T(8,128)S(1)}, u32[]{:S(2)}, u32[]{:S(2)}) collective-permute-start(f32[8,384]{1,0:T(8,128)S(1)} %get-tuple-element.38), channel_id=1, source_target_pairs={{0,2},{1,0},{2,3},{3,1},{4,6},{5,4},{6,7},{7,5},{8,10},{9,8},{10,1... | collective-permute-start | bytes 36872 | tf_op jit(solution)/shard_map/ppermute | solution.py:28
  25.1 0.0 collective-permute-done.11
  25.1 1.0 %collective-permute-done.9 = f32[8,384]{1,0:T(8,128)S(1)} collective-permute-done((f32[8,384]{1,0:T(8,128)S(1)}, f32[8,384]{1,0:T(8,128)S(1)}, u32[]{:S(2)}, u32[]{:S(2)}) %collective-permute-start.9) | collective-permute-done | bytes 12320 | tf_op jit(solution)/shard_map/ppermute | solution.py:28
  26.1 0.9 %collective-permute-done.10 = f32[8,384]{1,0:T(8,128)S(1)} collective-permute-done((f32[8,384]{1,0:T(8,128)S(1)}, f32[8,384]{1,0:T(8,128)S(1)}, u32[]{:S(2)}, u32[]{:S(2)}) %collective-permute-start.10) | collective-permute-done | bytes 12320 | tf_op jit(solution)/shard_map/ppermute | solution.py:28
  27.0 0.7 %shard_map.50 = (f32[8,256]{1,0:T(8,128)}, f32[8,8]{1,0:T(8,128)}) custom-call(f32[8,384]{1,0:T(8,128)S(1)} %fusion.5.both_ref), custom_call_target="tpu_custom_call" | custom-call | tf_op jit(solution)/shard_map/pallas_call | solution.py:175
  (10 shorter events, 0.1 us)
Async XLA Ops:
  0.6 11.7 %copy-start = (bf16[1024,1024]{1,0:T(8,128)(2,1)S(1)}, bf16[1024,1024]{1,0:T(8,128)(2,1)}, u32[]{:S(2)}) copy-start(bf16[1024,1024]{1,0:T(8,128)(2,1)} %param.3) | copy-start | bytes 6291460
  0.6 7.1 %collective-permute-start = (bf16[8,256]{1,0:T(8,128)(2,1)}, bf16[8,256]{1,0:T(8,128)(2,1)S(1)}, u32[]{:S(2)}, u32[]{:S(2)}) collective-permute-start(bf16[8,256]{1,0:T(8,128)(2,1)} %param.5), channel_id=1, source_target_pairs={{0,2},{1,3},{2,0},{3,1},{4,6},{5,7},{6,4},{7,5},{8,10},{9,11},{10,... | collective-permute-start | bytes 12296 | tf_op jit(solution)/shard_map/ppermute | solution.py:28
  4.7 3.8 %collective-permute-start.2 = (bf16[8,256]{1,0:T(8,128)(2,1)}, bf16[8,256]{1,0:T(8,128)(2,1)S(1)}, u32[]{:S(2)}, u32[]{:S(2)}) collective-permute-start(bf16[8,256]{1,0:T(8,128)(2,1)} %param.5), channel_id=1, source_target_pairs={{0,1},{1,0},{2,3},{3,2},{4,5},{5,4},{6,7},{7,6},{8,9},{9,8},{10,11... | collective-permute-start | bytes 12296 | tf_op jit(solution)/shard_map/ppermute | solution.py:28
  6.3 5.6 %collective-permute-start.1 = (bf16[8,256]{1,0:T(8,128)(2,1)}, bf16[8,256]{1,0:T(8,128)(2,1)S(1)}, u32[]{:S(2)}, u32[]{:S(2)}) collective-permute-start(bf16[8,256]{1,0:T(8,128)(2,1)} %param.5), channel_id=1, source_target_pairs={{0,3},{1,2},{2,1},{3,0},{4,7},{5,6},{6,5},{7,4},{8,11},{9,10},{10,... | collective-permute-start | bytes 12296 | tf_op jit(solution)/shard_map/ppermute | solution.py:28
  12.0 1.4 %collective-permute-start.3 = (bf16[8,1024]{1,0:T(8,128)(2,1)S(1)}, bf16[8,1024]{1,0:T(8,128)(2,1)S(1)}, u32[]{:S(2)}, u32[]{:S(2)}) collective-permute-start(bf16[8,1024]{1,0:T(8,128)(2,1)S(1)} %maximum_add_fusion), channel_id=1, source_target_pairs={{0,4},{1,29},{2,26},{3,23},{4,0},{5,1},{6,30},{7,27},{8,12},{9,5},... | collective-permute-start | bytes 49160 | tf_op jit(solution)/shard_map/ppermute | solution.py:28
  12.8 4.9 %collective-permute-start.6 = (f32[8,1024]{1,0:T(8,128)S(1)}, f32[8,1024]{1,0:T(8,128)S(1)}, u32[]{:S(2)}, u32[]{:S(2)}) collective-permute-start(f32[8,1024]{1,0:T(8,128)S(1)} %fusion.1), channel_id=1, source_target_pairs={{0,4},{1,5},{2,10},{3,15},{4,0},{5,9},{6,14},{7,19},{8,12},{9,13},... | collective-permute-start | bytes 98312 | tf_op jit(solution)/shard_map/ppermute | solution.py:28
  13.4 1.2 %collective-permute-start.4 = (f32[8,8]{1,0:T(8,128)S(1)}, f32[8,8]{1,0:T(8,128)S(1)}, u32[]{:S(2)}, u32[]{:S(2)}) collective-permute-start(f32[8,8]{1,0:T(8,128)S(1)} %fusion.11), channel_id=1, source_target_pairs={{0,4},{1,5},{2,6},{3,7},{4,0},{5,1},{6,2},{7,3},{8,12},{9,13},{10,... | collective-permute-start | bytes 776 | tf_op jit(solution)/shard_map/ppermute | solution.py:28
  14.7 3.0 %collective-permute-start.5 = (f32[8,8]{1,0:T(8,128)S(1)}, f32[8,8]{1,0:T(8,128)S(1)}, u32[]{:S(2)}, u32[]{:S(2)}) collective-permute-start(f32[8,8]{1,0:T(8,128)S(1)} %add.41), channel_id=1, source_target_pairs={{0,12},{1,13},{2,14},{3,15},{4,8},{5,9},{6,10},{7,11},{8,4},{9,5},... | collective-permute-start | bytes 776 | tf_op jit(solution)/shard_map/ppermute | solution.py:28
  15.9 3.9 %collective-permute-start.8 = (f32[8,8]{1,0:T(8,128)S(1)}, f32[8,8]{1,0:T(8,128)S(1)}, u32[]{:S(2)}, u32[]{:S(2)}) collective-permute-start(f32[8,8]{1,0:T(8,128)S(1)} %add.41), channel_id=1, source_target_pairs={{0,28},{1,29},{2,30},{3,31},{4,24},{5,25},{6,26},{7,27},{8,20},{9,... | collective-permute-start | bytes 776 | tf_op jit(solution)/shard_map/ppermute | solution.py:28
  17.4 3.1 %collective-permute-start.7 = (f32[8,8]{1,0:T(8,128)S(1)}, f32[8,8]{1,0:T(8,128)S(1)}, u32[]{:S(2)}, u32[]{:S(2)}) collective-permute-start(f32[8,8]{1,0:T(8,128)S(1)} %add.41), channel_id=1, source_target_pairs={{0,20},{1,21},{2,22},{3,23},{4,16},{5,17},{6,18},{7,19},{8,28},{9,... | collective-permute-start | bytes 776 | tf_op jit(solution)/shard_map/ppermute | solution.py:28
  20.4 4.6 %collective-permute-start.11 = (f32[8,384]{1,0:T(8,128)S(1)}, f32[8,384]{1,0:T(8,128)S(1)}, u32[]{:S(2)}, u32[]{:S(2)}) collective-permute-start(f32[8,384]{1,0:T(8,128)S(1)} %get-tuple-element.36), channel_id=1, source_target_pairs={{0,1},{1,3},{2,0},{3,2},{4,5},{5,7},{6,4},{7,6},{8,9},{9,11},{10,8... | collective-permute-start | bytes 36872 | tf_op jit(solution)/shard_map/ppermute | solution.py:28
  20.5 5.6 %collective-permute-start.9 = (f32[8,384]{1,0:T(8,128)S(1)}, f32[8,384]{1,0:T(8,128)S(1)}, u32[]{:S(2)}, u32[]{:S(2)}) collective-permute-start(f32[8,384]{1,0:T(8,128)S(1)} %get-tuple-element.37), channel_id=1, source_target_pairs={{0,3},{1,2},{2,1},{3,0},{4,7},{5,6},{6,5},{7,4},{8,11},{9,10},{10,... | collective-permute-start | bytes 36872 | tf_op jit(solution)/shard_map/ppermute | solution.py:28
  23.3 3.7 %collective-permute-start.10 = (f32[8,384]{1,0:T(8,128)S(1)}, f32[8,384]{1,0:T(8,128)S(1)}, u32[]{:S(2)}, u32[]{:S(2)}) collective-permute-start(f32[8,384]{1,0:T(8,128)S(1)} %get-tuple-element.38), channel_id=1, source_target_pairs={{0,2},{1,0},{2,3},{3,1},{4,6},{5,4},{6,7},{7,5},{8,10},{9,8},{10,1... | collective-permute-start | bytes 36872 | tf_op jit(solution)/shard_map/ppermute | solution.py:28

commit v5 on v4

--- a/solution.py
+++ b/solution.py
@@ -10,12 +10,12 @@
 SUB = 128
 AXES = ("row", "col")
 ONE = ((1, 0),)
-ROW_TABLES = ((1, 0, 3, 2), (2, 3, 0, 1), (3, 2, 1, 0))
-ROW_ORDER = (0, 1, 2)
-GATHER_TABLES = ((1, 0, 3, 2), (2, 3, 0, 1), (3, 2, 1, 0))
-GATHER_ORDER = (1, 2, 0)
-SUM_TABLES = ((1, 3, 0, 2), (3, 2, 1, 0), (2, 0, 3, 1))
-SUM_ORDER = (1, 2, 0)
+ROW_TABLES = ((2, 1, 0, 3), (1, 2, 3, 0), (3, 0, 1, 2), (0, 3, 2, 1))
+ROW_ORDER = (0, 2, 3, 1)
+GATHER_TABLES = ((2, 0, 3, 1), (0, 2, 1, 3), (3, 1, 0, 2), (1, 3, 2, 0))
+GATHER_ORDER = (0, 1, 2, 3)
+SUM_TABLES = ((1, 3, 2, 0), (2, 1, 0, 3), (3, 0, 1, 2), (0, 2, 3, 1))
+SUM_ORDER = (0, 1, 2, 3)
 
 
 def send(block, target):
@@ -37,7 +37,10 @@
     if axis == "row":
         goes = [lambda r, c, t=t: (moved(r, bit, t) ^ 1, c) for t in tables]
     else:
-        goes = [lambda r, c, t=t: (r, moved(c, bit, t)) for t in tables]
+        goes = [
+            lambda r, c, t=t: (r ^ (moved(c, bit, t) == c), moved(c, bit, t))
+            for t in tables
+        ]
     return [send(block, to) for block, to in zip(blocks, goes)]
 
 
@@ -68,7 +71,7 @@
 
 
 def in_place(own, got, tables, place):
-    members = len(tables) + 1
+    members = len(tables[0])
 
     def source(d, k):
         return next(g for g, t in zip(got, tables) if t[d ^ k] == d)

time: 27.9 us -> 26.2 us (0.939)
  waiting for transfers between devices: 9.38 us -> 6.31 us
  starting transfers between devices: 13.9 us -> 15.2 us
    ppermute x12 -> x15, waiting for transfers between devices: 9.38 us -> 6.31 us  [send(): return lax.ppermute(block, AXES, pairs)]
    ppermute x12 -> x15, starting transfers between devices: 13.9 us -> 15.2 us  [send(): return lax.ppermute(block, AXES, pairs)]
  transfers between devices with their start and end apart: 12 -> 15, of which waited for: 8 -> 5; matrix products, arithmetic and copies ran while one was open for 11% -> 11% of each run, Pallas kernels for 0% -> 0%
where the time goes in v5:
time: 26.2 us; the launch traced here: 26 us
  starting transfers between devices  15.2 us (58%)
  waiting for transfers between devices  6.31 us (24%)
  other arithmetic  1.47 us (6%)
  matrix products  1.23 us (5%)
  between operations  0.74 us (3%)
  Pallas kernels  0.66 us (3%)
  local copies, waits for them, and re-layouts  0.34 us (1%)
    ppermute x15, starting transfers between devices, send(): return lax.ppermute(block, AXES, pairs)  15.2 us
    ppermute x15, waiting for transfers between devices, send(): return lax.ppermute(block, AXES, pairs)  6.31 us
    select_n x1, other arithmetic, on_device(): jnp.where(place == at, source, zero)  0.69 us
    convert_element_type x1, other arithmetic, on_device(): keep = block_map[0, 0].astype(jnp.bfloat16)  0.69 us
    pallas_call x1, Pallas kernels, on_device(): pl.pallas_call(functools.partial(write_results, 1.0 / (width * rows) ** 0...  0.66 us
    dot_general x1, matrix products, on_device(): lax.dot_general(far_vec, matrix, (((1,), (1,)), ((), ())), preferred_elem...  0.65 us
  transfers between devices with their start and end apart: 15, of which 5 were waited for; matrix products, arithmetic and copies ran while one was open for 11% of the time, Pallas kernels for 0%

profile of v5, /device:TPU:0, one launch (start us, length us, event | category | flops | bytes accessed | tf_op | source)
XLA Modules:
  0.0 26.0 jit_solution(3603765915490689989)
XLA Ops:
  0.6 4.1 %collective-permute-start = (bf16[8,256]{1,0:T(8,128)(2,1)}, bf16[8,256]{1,0:T(8,128)(2,1)S(1)}, u32[]{:S(2)}, u32[]{:S(2)}) collective-permute-start(bf16[8,256]{1,0:T(8,128)(2,1)} %param.5), channel_id=1, source_target_pairs={{0,2},{1,0},{2,3},{3,1},{4,6},{5,4},{6,7},{7,5},{8,10},{9,8},{10,1... | collective-permute-start | bytes 12296 | tf_op jit(solution)/shard_map/ppermute | solution.py:28
  4.7 1.3 %collective-permute-start.2 = (bf16[8,256]{1,0:T(8,128)(2,1)}, bf16[8,256]{1,0:T(8,128)(2,1)S(1)}, u32[]{:S(2)}, u32[]{:S(2)}) collective-permute-start(bf16[8,256]{1,0:T(8,128)(2,1)} %param.5), channel_id=1, source_target_pairs={{0,3},{1,5},{2,0},{3,2},{4,7},{5,1},{6,4},{7,6},{8,11},{9,13},{10,... | collective-permute-start | bytes 12296 | tf_op jit(solution)/shard_map/ppermute | solution.py:28
  6.1 0.8 %collective-permute-start.3 = (bf16[8,256]{1,0:T(8,128)(2,1)}, bf16[8,256]{1,0:T(8,128)(2,1)S(1)}, u32[]{:S(2)}, u32[]{:S(2)}) collective-permute-start(bf16[8,256]{1,0:T(8,128)(2,1)} %param.5), channel_id=1, source_target_pairs={{0,1},{1,3},{2,6},{3,0},{4,5},{5,7},{6,2},{7,4},{8,9},{9,11},{10,1... | collective-permute-start | bytes 12296 | tf_op jit(solution)/shard_map/ppermute | solution.py:28
  6.9 0.7 %convert_bitcast_fusion = bf16[8,8]{1,0:T(8,128)(2,1)S(1)} fusion(s32[1,1,8,8]{3,2,1,0:T(8,128)} %param.4), kind=kLoop, calls=%fused_computation.47 | loop fusion | flops 64 | bytes 384 | tf_op jit(solution)/shard_map/convert_element_type | solution.py:108
  7.6 0.7 %broadcast_select_fusion.3 = (bf16[8,256]{1,0:T(8,128)(2,1)S(1)}, bf16[8,256]{1,0:T(8,128)(2,1)S(1)}, bf16[8,256]{1,0:T(8,128)(2,1)S(1)}, bf16[8,256]{1,0:T(8,128)(2,1)S(1)}) fusion(bf16[8,256]{1,0:T(8,128)(2,1)} %param.5, pred[]{:T(512)S(6)} %eq.20, pred[]{:T(512)S(6)} %eq.23, pred[]{:T(512)S(6)} %eq.22, pred[]{:T(512)S(6)} %eq.21), kind=kLoop, calls=%fused_computation.45 | loop fusion | flops 8192 | bytes 20484 | tf_op jit(solution)/shard_map/jit(_where)/select_n | solution.py:122
  8.3 0.0 collective-permute-done
  8.3 0.0 collective-permute-done.1
  8.3 1.2 %collective-permute-done.2 = bf16[8,256]{1,0:T(8,128)(2,1)S(1)} collective-permute-done((bf16[8,256]{1,0:T(8,128)(2,1)}, bf16[8,256]{1,0:T(8,128)(2,1)S(1)}, u32[]{:S(2)}, u32[]{:S(2)}) %collective-permute-start.2) | collective-permute-done | bytes 4128 | tf_op jit(solution)/shard_map/ppermute | solution.py:28
  9.4 2.2 %collective-permute-done.3 = bf16[8,256]{1,0:T(8,128)(2,1)S(1)} collective-permute-done((bf16[8,256]{1,0:T(8,128)(2,1)}, bf16[8,256]{1,0:T(8,128)(2,1)S(1)}, u32[]{:S(2)}, u32[]{:S(2)}) %collective-permute-start.3) | collective-permute-done | bytes 4128 | tf_op jit(solution)/shard_map/ppermute | solution.py:28
  11.7 0.1 collective-permute-start.4
  11.8 0.3 %mul.11 = bf16[8,128,8,128]{3,2,1,0:T(8,128)(2,1)S(1)} broadcast(bf16[8,8]{1,0:T(8,128)(2,1)S(1)} %convert_bitcast_fusion), dimensions={0,2} | broadcast | bytes 2097280 | tf_op jit(solution)/shard_map/mul | solution.py:109
  12.2 0.5 %fusion.1 = f32[8,1024]{1,0:T(8,128)S(1)} fusion(bf16[8,1024]{1,0:T(8,128)(2,1)S(1)} %maximum_add_fusion, bf16[1024,1024]{1,0:T(8,128)(2,1)S(1)} %copy-done, bf16[128,8,8,128]{3,2,1,0:T(8,128)(2,1)S(1)} %bitcast.10), kind=kOutput, calls=%fused_computation.2 | convolution fusion | flops 17825792 | bytes 4243456 | tf_op jit(solution)/shard_map/dot_general | solution.py:136
  12.6 0.5 %collective-permute-start.7 = (f32[8,1024]{1,0:T(8,128)S(1)}, f32[8,1024]{1,0:T(8,128)S(1)}, u32[]{:S(2)}, u32[]{:S(2)}) collective-permute-start(f32[8,1024]{1,0:T(8,128)S(1)} %fusion.1), channel_id=1, source_target_pairs={{0,4},{1,5},{2,10},{3,15},{4,0},{5,9},{6,14},{7,19},{8,12},{9,13},... | collective-permute-start | bytes 98312 | tf_op jit(solution)/shard_map/ppermute | solution.py:28
  13.1 0.0 collective-permute-done.4
  13.1 0.1 fusion.19
  13.2 0.1 collective-permute-start.5
  13.3 0.7 %fusion = f32[8,1024]{1,0:T(8,128)S(1)} fusion(bf16[1024,1024]{1,0:T(8,128)(2,1)S(1)} %copy-done, bf16[128,8,8,128]{3,2,1,0:T(8,128)(2,1)S(1)} %bitcast.11, bf16[8,1024]{1,0:T(8,128)(2,1)S(1)} %maximum_add_fusion, bf16[8,1024]{1,0:T(8,128)(2,1)S(1)} %collective-permute-done.4, pred[]{:T(512)S(6)} %lt.16, pred[]{:T(512)S(6)} %eq.24), kind=kOutput, calls=%fused_computation.1 | convolution fusion | flops 17842176 | bytes 4259842 | tf_op jit(solution)/shard_map/dot_general | solution.py:146
  13.9 0.5 %collective-permute-done.5 = f32[8,8]{1,0:T(8,128)S(1)} collective-permute-done((f32[8,8]{1,0:T(8,128)S(1)}, f32[8,8]{1,0:T(8,128)S(1)}, u32[]{:S(2)}, u32[]{:S(2)}) %collective-permute-start.5) | collective-permute-done | bytes 288 | tf_op jit(solution)/shard_map/ppermute | solution.py:28
  14.4 1.3 %collective-permute-start.6 = (f32[8,8]{1,0:T(8,128)S(1)}, f32[8,8]{1,0:T(8,128)S(1)}, u32[]{:S(2)}, u32[]{:S(2)}) collective-permute-start(f32[8,8]{1,0:T(8,128)S(1)} %add.43), channel_id=1, source_target_pairs={{0,20},{1,21},{2,22},{3,23},{4,16},{5,17},{6,18},{7,19},{8,12},{9,... | collective-permute-start | bytes 776 | tf_op jit(solution)/shard_map/ppermute | solution.py:28
  15.7 0.3 %collective-permute-start.10 = (f32[8,8]{1,0:T(8,128)S(1)}, f32[8,8]{1,0:T(8,128)S(1)}, u32[]{:S(2)}, u32[]{:S(2)}) collective-permute-start(f32[8,8]{1,0:T(8,128)S(1)} %add.43), channel_id=1, source_target_pairs={{0,12},{1,13},{2,14},{3,15},{4,8},{5,9},{6,10},{7,11},{8,20},{9,21... | collective-permute-start | bytes 776 | tf_op jit(solution)/shard_map/ppermute | solution.py:28
  16.0 2.3 %collective-permute-start.8 = (f32[8,8]{1,0:T(8,128)S(1)}, f32[8,8]{1,0:T(8,128)S(1)}, u32[]{:S(2)}, u32[]{:S(2)}) collective-permute-start(f32[8,8]{1,0:T(8,128)S(1)} %add.43), channel_id=1, source_target_pairs={{0,28},{1,29},{2,30},{3,31},{4,24},{5,25},{6,26},{7,27},{8,4},{9,5... | collective-permute-start | bytes 776 | tf_op jit(solution)/shard_map/ppermute | solution.py:28
  18.4 0.3 %collective-permute-start.9 = (f32[8,8]{1,0:T(8,128)S(1)}, f32[8,8]{1,0:T(8,128)S(1)}, u32[]{:S(2)}, u32[]{:S(2)}) collective-permute-start(f32[8,8]{1,0:T(8,128)S(1)} %add.43), channel_id=1, source_target_pairs={{0,4},{1,5},{2,6},{3,7},{4,0},{5,1},{6,2},{7,3},{8,28},{9,29},{10,... | collective-permute-start | bytes 776 | tf_op jit(solution)/shard_map/ppermute | solution.py:28
  18.7 0.0 collective-permute-done.6
  18.7 0.0 collective-permute-done.7
  18.8 0.9 %collective-permute-done.10 = f32[8,8]{1,0:T(8,128)S(1)} collective-permute-done((f32[8,8]{1,0:T(8,128)S(1)}, f32[8,8]{1,0:T(8,128)S(1)}, u32[]{:S(2)}, u32[]{:S(2)}) %collective-permute-start.10) | collective-permute-done | bytes 288 | tf_op jit(solution)/shard_map/ppermute | solution.py:28
  19.7 0.0 collective-permute-done.8
  19.7 0.6 %collective-permute-start.11 = (f32[8,384]{1,0:T(8,128)S(1)}, f32[8,384]{1,0:T(8,128)S(1)}, u32[]{:S(2)}, u32[]{:S(2)}) collective-permute-start(f32[8,384]{1,0:T(8,128)S(1)} %get-tuple-element.46), channel_id=1, source_target_pairs={{0,1},{1,3},{2,6},{3,0},{4,5},{5,7},{6,2},{7,4},{8,9},{9,11},{10,1... | collective-permute-start | bytes 36872 | tf_op jit(solution)/shard_map/ppermute | solution.py:28
  20.3 0.8 %collective-permute-start.12 = (f32[8,384]{1,0:T(8,128)S(1)}, f32[8,384]{1,0:T(8,128)S(1)}, u32[]{:S(2)}, u32[]{:S(2)}) collective-permute-start(f32[8,384]{1,0:T(8,128)S(1)} %get-tuple-element.47), channel_id=1, source_target_pairs={{0,2},{1,5},{2,0},{3,7},{4,6},{5,1},{6,4},{7,3},{8,10},{9,13},{10,... | collective-permute-start | bytes 36872 | tf_op jit(solution)/shard_map/ppermute | solution.py:28
  21.1 2.6 %collective-permute-start.13 = (f32[8,384]{1,0:T(8,128)S(1)}, f32[8,384]{1,0:T(8,128)S(1)}, u32[]{:S(2)}, u32[]{:S(2)}) collective-permute-start(f32[8,384]{1,0:T(8,128)S(1)} %get-tuple-element.48), channel_id=1, source_target_pairs={{0,3},{1,0},{2,1},{3,2},{4,7},{5,4},{6,5},{7,6},{8,11},{9,8},{10,9... | collective-permute-start | bytes 36872 | tf_op jit(solution)/shard_map/ppermute | solution.py:28
  23.6 0.2 collective-permute-start.14
  23.8 1.4 %collective-permute-done.11 = f32[8,384]{1,0:T(8,128)S(1)} collective-permute-done((f32[8,384]{1,0:T(8,128)S(1)}, f32[8,384]{1,0:T(8,128)S(1)}, u32[]{:S(2)}, u32[]{:S(2)}) %collective-permute-start.11) | collective-permute-done | bytes 12320 | tf_op jit(solution)/shard_map/ppermute | solution.py:28
  25.3 0.7 %shard_map.50 = (f32[8,256]{1,0:T(8,128)}, f32[8,8]{1,0:T(8,128)}) custom-call(f32[8,384]{1,0:T(8,128)S(1)} %fusion.4.both_ref), custom_call_target="tpu_custom_call" | custom-call | tf_op jit(solution)/shard_map/pallas_call | solution.py:178
  (18 shorter events, 0.1 us)
Async XLA Ops:
  0.6 11.5 %copy-start = (bf16[1024,1024]{1,0:T(8,128)(2,1)S(1)}, bf16[1024,1024]{1,0:T(8,128)(2,1)}, u32[]{:S(2)}) copy-start(bf16[1024,1024]{1,0:T(8,128)(2,1)} %param.3) | copy-start | bytes 6291460
  0.6 7.6 %collective-permute-start = (bf16[8,256]{1,0:T(8,128)(2,1)}, bf16[8,256]{1,0:T(8,128)(2,1)S(1)}, u32[]{:S(2)}, u32[]{:S(2)}) collective-permute-start(bf16[8,256]{1,0:T(8,128)(2,1)} %param.5), channel_id=1, source_target_pairs={{0,2},{1,0},{2,3},{3,1},{4,6},{5,4},{6,7},{7,5},{8,10},{9,8},{10,1... | collective-permute-start | bytes 12296 | tf_op jit(solution)/shard_map/ppermute | solution.py:28
  4.7 3.5 %collective-permute-start.1 = (bf16[8,256]{1,0:T(8,128)(2,1)}, bf16[8,256]{1,0:T(8,128)(2,1)S(1)}, u32[]{:S(2)}, u32[]{:S(2)}) collective-permute-start(bf16[8,256]{1,0:T(8,128)(2,1)} %param.5), channel_id=1, source_target_pairs={{0,4},{1,2},{2,1},{3,7},{4,0},{5,6},{6,5},{7,3},{8,12},{9,10},{10,... | collective-permute-start | bytes 12296 | tf_op jit(solution)/shard_map/ppermute | solution.py:28
  4.7 4.7 %collective-permute-start.2 = (bf16[8,256]{1,0:T(8,128)(2,1)}, bf16[8,256]{1,0:T(8,128)(2,1)S(1)}, u32[]{:S(2)}, u32[]{:S(2)}) collective-permute-start(bf16[8,256]{1,0:T(8,128)(2,1)} %param.5), channel_id=1, source_target_pairs={{0,3},{1,5},{2,0},{3,2},{4,7},{5,1},{6,4},{7,6},{8,11},{9,13},{10,... | collective-permute-start | bytes 12296 | tf_op jit(solution)/shard_map/ppermute | solution.py:28
  6.1 5.6 %collective-permute-start.3 = (bf16[8,256]{1,0:T(8,128)(2,1)}, bf16[8,256]{1,0:T(8,128)(2,1)S(1)}, u32[]{:S(2)}, u32[]{:S(2)}) collective-permute-start(bf16[8,256]{1,0:T(8,128)(2,1)} %param.5), channel_id=1, source_target_pairs={{0,1},{1,3},{2,6},{3,0},{4,5},{5,7},{6,2},{7,4},{8,9},{9,11},{10,1... | collective-permute-start | bytes 12296 | tf_op jit(solution)/shard_map/ppermute | solution.py:28
  11.7 1.4 %collective-permute-start.4 = (bf16[8,1024]{1,0:T(8,128)(2,1)S(1)}, bf16[8,1024]{1,0:T(8,128)(2,1)S(1)}, u32[]{:S(2)}, u32[]{:S(2)}) collective-permute-start(bf16[8,1024]{1,0:T(8,128)(2,1)S(1)} %maximum_add_fusion), channel_id=1, source_target_pairs={{0,4},{1,29},{2,26},{3,23},{4,0},{5,1},{6,30},{7,27},{8,12},{9,5},... | collective-permute-start | bytes 49160 | tf_op jit(solution)/shard_map/ppermute | solution.py:28
  12.6 6.1 %collective-permute-start.7 = (f32[8,1024]{1,0:T(8,128)S(1)}, f32[8,1024]{1,0:T(8,128)S(1)}, u32[]{:S(2)}, u32[]{:S(2)}) collective-permute-start(f32[8,1024]{1,0:T(8,128)S(1)} %fusion.1), channel_id=1, source_target_pairs={{0,4},{1,5},{2,10},{3,15},{4,0},{5,9},{6,14},{7,19},{8,12},{9,13},... | collective-permute-start | bytes 98312 | tf_op jit(solution)/shard_map/ppermute | solution.py:28
  13.2 1.2 %collective-permute-start.5 = (f32[8,8]{1,0:T(8,128)S(1)}, f32[8,8]{1,0:T(8,128)S(1)}, u32[]{:S(2)}, u32[]{:S(2)}) collective-permute-start(f32[8,8]{1,0:T(8,128)S(1)} %fusion.19), channel_id=1, source_target_pairs={{0,4},{1,5},{2,6},{3,7},{4,0},{5,1},{6,2},{7,3},{8,12},{9,13},{10,... | collective-permute-start | bytes 776 | tf_op jit(solution)/shard_map/ppermute | solution.py:28
  14.4 4.3 %collective-permute-start.6 = (f32[8,8]{1,0:T(8,128)S(1)}, f32[8,8]{1,0:T(8,128)S(1)}, u32[]{:S(2)}, u32[]{:S(2)}) collective-permute-start(f32[8,8]{1,0:T(8,128)S(1)} %add.43), channel_id=1, source_target_pairs={{0,20},{1,21},{2,22},{3,23},{4,16},{5,17},{6,18},{7,19},{8,12},{9,... | collective-permute-start | bytes 776 | tf_op jit(solution)/shard_map/ppermute | solution.py:28
  15.7 3.9 %collective-permute-start.10 = (f32[8,8]{1,0:T(8,128)S(1)}, f32[8,8]{1,0:T(8,128)S(1)}, u32[]{:S(2)}, u32[]{:S(2)}) collective-permute-start(f32[8,8]{1,0:T(8,128)S(1)} %add.43), channel_id=1, source_target_pairs={{0,12},{1,13},{2,14},{3,15},{4,8},{5,9},{6,10},{7,11},{8,20},{9,21... | collective-permute-start | bytes 776 | tf_op jit(solution)/shard_map/ppermute | solution.py:28
  16.0 3.7 %collective-permute-start.8 = (f32[8,8]{1,0:T(8,128)S(1)}, f32[8,8]{1,0:T(8,128)S(1)}, u32[]{:S(2)}, u32[]{:S(2)}) collective-permute-start(f32[8,8]{1,0:T(8,128)S(1)} %add.43), channel_id=1, source_target_pairs={{0,28},{1,29},{2,30},{3,31},{4,24},{5,25},{6,26},{7,27},{8,4},{9,5... | collective-permute-start | bytes 776 | tf_op jit(solution)/shard_map/ppermute | solution.py:28
  18.4 1.3 %collective-permute-start.9 = (f32[8,8]{1,0:T(8,128)S(1)}, f32[8,8]{1,0:T(8,128)S(1)}, u32[]{:S(2)}, u32[]{:S(2)}) collective-permute-start(f32[8,8]{1,0:T(8,128)S(1)} %add.43), channel_id=1, source_target_pairs={{0,4},{1,5},{2,6},{3,7},{4,0},{5,1},{6,2},{7,3},{8,28},{9,29},{10,... | collective-permute-start | bytes 776 | tf_op jit(solution)/shard_map/ppermute | solution.py:28
  19.7 5.5 %collective-permute-start.11 = (f32[8,384]{1,0:T(8,128)S(1)}, f32[8,384]{1,0:T(8,128)S(1)}, u32[]{:S(2)}, u32[]{:S(2)}) collective-permute-start(f32[8,384]{1,0:T(8,128)S(1)} %get-tuple-element.46), channel_id=1, source_target_pairs={{0,1},{1,3},{2,6},{3,0},{4,5},{5,7},{6,2},{7,4},{8,9},{9,11},{10,1... | collective-permute-start | bytes 36872 | tf_op jit(solution)/shard_map/ppermute | solution.py:28
  20.3 5.0 %collective-permute-start.12 = (f32[8,384]{1,0:T(8,128)S(1)}, f32[8,384]{1,0:T(8,128)S(1)}, u32[]{:S(2)}, u32[]{:S(2)}) collective-permute-start(f32[8,384]{1,0:T(8,128)S(1)} %get-tuple-element.47), channel_id=1, source_target_pairs={{0,2},{1,5},{2,0},{3,7},{4,6},{5,1},{6,4},{7,3},{8,10},{9,13},{10,... | collective-permute-start | bytes 36872 | tf_op jit(solution)/shard_map/ppermute | solution.py:28
  21.1 4.2 %collective-permute-start.13 = (f32[8,384]{1,0:T(8,128)S(1)}, f32[8,384]{1,0:T(8,128)S(1)}, u32[]{:S(2)}, u32[]{:S(2)}) collective-permute-start(f32[8,384]{1,0:T(8,128)S(1)} %get-tuple-element.48), channel_id=1, source_target_pairs={{0,3},{1,0},{2,1},{3,2},{4,7},{5,4},{6,5},{7,6},{8,11},{9,8},{10,9... | collective-permute-start | bytes 36872 | tf_op jit(solution)/shard_map/ppermute | solution.py:28
  23.6 1.7 %collective-permute-start.14 = (f32[8,384]{1,0:T(8,128)S(1)}, f32[8,384]{1,0:T(8,128)S(1)}, u32[]{:S(2)}, u32[]{:S(2)}) collective-permute-start(f32[8,384]{1,0:T(8,128)S(1)} %get-tuple-element.45), channel_id=1, source_target_pairs={{0,4},{1,2},{2,3},{3,1},{4,0},{5,6},{6,7},{7,5},{8,12},{9,10},{10,... | collective-permute-start | bytes 36872 | tf_op jit(solution)/shard_map/ppermute | solution.py:28

commit v6 on v5

--- a/solution.py
+++ b/solution.py
@@ -12,7 +12,7 @@
 ONE = ((1, 0),)
 ROW_TABLES = ((2, 1, 0, 3), (1, 2, 3, 0), (3, 0, 1, 2), (0, 3, 2, 1))
 ROW_ORDER = (0, 2, 3, 1)
-GATHER_TABLES = ((2, 0, 3, 1), (0, 2, 1, 3), (3, 1, 0, 2), (1, 3, 2, 0))
+GATHER_TABLES = ((2, 3, 0, 1), (0, 1, 3, 2), (3, 2, 1, 0), (1, 0, 2, 3))
 GATHER_ORDER = (0, 1, 2, 3)
 SUM_TABLES = ((1, 3, 2, 0), (2, 1, 0, 3), (3, 0, 1, 2), (0, 2, 3, 1))
 SUM_ORDER = (0, 1, 2, 3)
@@ -36,6 +36,8 @@
 def exchanged(blocks, bit, tables, axis):
     if axis == "row":
         goes = [lambda r, c, t=t: (moved(r, bit, t) ^ 1, c) for t in tables]
+    elif axis == "cross":
+        goes = [lambda r, c, t=t: (r ^ 1, moved(c, bit, t)) for t in tables]
     else:
         goes = [
             lambda r, c, t=t: (r ^ (moved(c, bit, t) == c), moved(c, bit, t))
@@ -156,24 +158,37 @@
         got = exchanged([gram] * len(tables), bit, tables, "row")
         if bit == 1:
             got[0], arrived = lax.optimization_barrier((got[0], arrived))
+            arrived = jnp.where(row_idx >= col_idx, arrived, jnp.zeros_like(arrived))
+            arrived = jnp.where(col_idx == 0, mirror, arrived)
+            sums = plain + arrived
+            other = send(sums, lambda r, c: (r ^ 1, c))
         gram = tree_sum(in_place(gram, held(got, ROW_ORDER), tables, place))
 
     gram = jnp.pad(gram, ((0, 0), (0, SUB - vectors)))
-    arrived = jnp.where(row_idx >= col_idx, arrived, jnp.zeros_like(arrived))
-    arrived = jnp.where(col_idx == 0, mirror, arrived)
-    both = jnp.concatenate([plain + arrived, gram], axis=1)
+    mate = other
     for bit, members in reversed(groups_of(0, col_bits)):
         place = (col_idx >> bit) % members
         tables = SUM_TABLES if members == 4 else ONE
-        pieces = jnp.split(both[:, :-SUB], members, axis=1)
-        gram = both[:, -SUB:]
+        own_pieces = jnp.split(sums, members, axis=1)
+        mate_pieces = jnp.split(mate, members, axis=1)
+
+        def message(to, first, second):
+            blocks = [choose(to, first), choose(to, second), gram]
+            return jnp.concatenate(blocks if bit else [blocks[0], gram], axis=1)
+
         given = [
-            jnp.concatenate([choose(place, [pieces[to] for to in table]), gram], axis=1)
+            message(
+                place,
+                [mate_pieces[to] for to in table],
+                [own_pieces[to] for to in table],
+            )
             for table in tables
         ]
-        own = jnp.concatenate([choose(place, pieces), gram], axis=1)
-        got = held(exchanged(given, bit, tables, "col"), SUM_ORDER)
+        own = message(place, own_pieces, mate_pieces)
+        got = held(exchanged(given, bit, tables, "cross"), SUM_ORDER)
         both = tree_sum(in_place(own, got, tables, place))
+        piece = own_pieces[0].shape[1]
+        sums, mate, gram = both[:, :piece], both[:, piece:-SUB], both[:, -SUB:]
 
     return pl.pallas_call(
         functools.partial(write_results, 1.0 / (width * rows) ** 0.5),

time: 26.2 us -> 25.9 us (0.989)
  waiting for transfers between devices: 6.31 us -> 5.16 us
  starting transfers between devices: 15.2 us -> 15.8 us
    ppermute x15 -> x16, waiting for transfers between devices: 6.31 us -> 5.16 us  [send(): return lax.ppermute(block, AXES, pairs)]
    ppermute x15 -> x16, starting transfers between devices: 15.2 us -> 15.8 us  [send(): return lax.ppermute(block, AXES, pairs)]
  transfers between devices with their start and end apart: 15 -> 16, of which waited for: 5 -> 6; matrix products, arithmetic and copies ran while one was open for 11% -> 12% of each run, Pallas kernels for 0% -> 0%
where the time goes in v6:
time: 25.9 us; the launch traced here: 25.4 us
  starting transfers between devices  15.8 us (61%)
  waiting for transfers between devices  5.16 us (20%)
  other arithmetic  1.46 us (6%)
  matrix products  1.23 us (5%)
  between operations  0.72 us (3%)
  Pallas kernels  0.67 us (3%)
  local copies, waits for them, and re-layouts  0.34 us (1%)
    ppermute x16, starting transfers between devices, send(): return lax.ppermute(block, AXES, pairs)  15.8 us
    ppermute x16, waiting for transfers between devices, send(): return lax.ppermute(block, AXES, pairs)  5.16 us
    select_n x1, other arithmetic, on_device(): jnp.where(place == at, source, zero)  0.69 us
    convert_element_type x1, other arithmetic, on_device(): keep = block_map[0, 0].astype(jnp.bfloat16)  0.69 us
    pallas_call x1, Pallas kernels, on_device(): pl.pallas_call(functools.partial(write_results, 1.0 / (width * rows) ** 0...  0.67 us
    dot_general x1, matrix products, on_device(): lax.dot_general(far_vec, matrix, (((1,), (1,)), ((), ())), preferred_elem...  0.65 us
  transfers between devices with their start and end apart: 16, of which 6 were waited for; matrix products, arithmetic and copies ran while one was open for 12% of the time, Pallas kernels for 0%

profile of v6, /device:TPU:0, one launch (start us, length us, event | category | flops | bytes accessed | tf_op | source)
XLA Modules:
  0.0 25.4 jit_solution(6649349238272789656)
XLA Ops:
  0.6 4.1 %collective-permute-start = (bf16[8,256]{1,0:T(8,128)(2,1)}, bf16[8,256]{1,0:T(8,128)(2,1)S(1)}, u32[]{:S(2)}, u32[]{:S(2)}) collective-permute-start(bf16[8,256]{1,0:T(8,128)(2,1)} %param.5), channel_id=1, source_target_pairs={{0,2},{1,3},{2,0},{3,1},{4,6},{5,7},{6,4},{7,5},{8,10},{9,11},{10,... | collective-permute-start | bytes 12296 | tf_op jit(solution)/shard_map/ppermute | solution.py:28
  4.7 0.0 collective-permute-start.1
  4.7 1.5 %collective-permute-start.2 = (bf16[8,256]{1,0:T(8,128)(2,1)}, bf16[8,256]{1,0:T(8,128)(2,1)S(1)}, u32[]{:S(2)}, u32[]{:S(2)}) collective-permute-start(bf16[8,256]{1,0:T(8,128)(2,1)} %param.5), channel_id=1, source_target_pairs={{0,3},{1,2},{2,1},{3,0},{4,7},{5,6},{6,5},{7,4},{8,11},{9,10},{10,... | collective-permute-start | bytes 12296 | tf_op jit(solution)/shard_map/ppermute | solution.py:28
  6.3 0.9 %collective-permute-start.3 = (bf16[8,256]{1,0:T(8,128)(2,1)}, bf16[8,256]{1,0:T(8,128)(2,1)S(1)}, u32[]{:S(2)}, u32[]{:S(2)}) collective-permute-start(bf16[8,256]{1,0:T(8,128)(2,1)} %param.5), channel_id=1, source_target_pairs={{0,1},{1,0},{2,6},{3,7},{4,5},{5,4},{6,2},{7,3},{8,9},{9,8},{10,14... | collective-permute-start | bytes 12296 | tf_op jit(solution)/shard_map/ppermute | solution.py:28
  7.2 0.7 %convert_bitcast_fusion = bf16[8,8]{1,0:T(8,128)(2,1)S(1)} fusion(s32[1,1,8,8]{3,2,1,0:T(8,128)} %param.4), kind=kLoop, calls=%fused_computation.45 | loop fusion | flops 64 | bytes 384 | tf_op jit(solution)/shard_map/convert_element_type | solution.py:110
  7.9 0.7 %broadcast_select_fusion.3 = (bf16[8,256]{1,0:T(8,128)(2,1)S(1)}, bf16[8,256]{1,0:T(8,128)(2,1)S(1)}, bf16[8,256]{1,0:T(8,128)(2,1)S(1)}, bf16[8,256]{1,0:T(8,128)(2,1)S(1)}) fusion(bf16[8,256]{1,0:T(8,128)(2,1)} %param.5, pred[]{:T(512)S(6)} %eq.20, pred[]{:T(512)S(6)} %eq.23, pred[]{:T(512)S(6)} %eq.22, pred[]{:T(512)S(6)} %eq.21), kind=kLoop, calls=%fused_computation.43 | loop fusion | flops 8192 | bytes 20484 | tf_op jit(solution)/shard_map/jit(_where)/select_n | solution.py:124
  8.6 1.7 %collective-permute-done.2 = bf16[8,256]{1,0:T(8,128)(2,1)S(1)} collective-permute-done((bf16[8,256]{1,0:T(8,128)(2,1)}, bf16[8,256]{1,0:T(8,128)(2,1)S(1)}, u32[]{:S(2)}, u32[]{:S(2)}) %collective-permute-start.2) | collective-permute-done | bytes 4128 | tf_op jit(solution)/shard_map/ppermute | solution.py:28
  10.4 0.0 collective-permute-done.3
  10.4 0.1 collective-permute-start.4
  10.5 0.3 %mul.11 = bf16[8,128,8,128]{3,2,1,0:T(8,128)(2,1)S(1)} broadcast(bf16[8,8]{1,0:T(8,128)(2,1)S(1)} %convert_bitcast_fusion), dimensions={0,2} | broadcast | bytes 2097280 | tf_op jit(solution)/shard_map/mul | solution.py:111
  10.8 0.5 %fusion.1 = f32[8,1024]{1,0:T(8,128)S(1)} fusion(bf16[8,1024]{1,0:T(8,128)(2,1)S(1)} %maximum_add_fusion, bf16[1024,1024]{1,0:T(8,128)(2,1)S(1)} %copy-done, bf16[128,8,8,128]{3,2,1,0:T(8,128)(2,1)S(1)} %bitcast.10), kind=kOutput, calls=%fused_computation.2 | convolution fusion | flops 17825792 | bytes 4243456 | tf_op jit(solution)/shard_map/dot_general | solution.py:138
  11.3 0.5 %collective-permute-start.7 = (f32[8,1024]{1,0:T(8,128)S(1)}, f32[8,1024]{1,0:T(8,128)S(1)}, u32[]{:S(2)}, u32[]{:S(2)}) collective-permute-start(f32[8,1024]{1,0:T(8,128)S(1)} %fusion.1), channel_id=1, source_target_pairs={{0,4},{1,5},{2,10},{3,15},{4,0},{5,9},{6,14},{7,19},{8,12},{9,13},... | collective-permute-start | bytes 98312 | tf_op jit(solution)/shard_map/ppermute | solution.py:28
  11.8 0.0 collective-permute-done.4
  11.8 0.1 fusion.19
  11.9 0.1 collective-permute-start.5
  12.0 0.7 %fusion = f32[8,1024]{1,0:T(8,128)S(1)} fusion(bf16[1024,1024]{1,0:T(8,128)(2,1)S(1)} %copy-done, bf16[128,8,8,128]{3,2,1,0:T(8,128)(2,1)S(1)} %bitcast.11, bf16[8,1024]{1,0:T(8,128)(2,1)S(1)} %maximum_add_fusion, bf16[8,1024]{1,0:T(8,128)(2,1)S(1)} %collective-permute-done.4, pred[]{:T(512)S(6)} %lt.16, pred[]{:T(512)S(6)} %eq.24), kind=kOutput, calls=%fused_computation.1 | convolution fusion | flops 17842176 | bytes 4259842 | tf_op jit(solution)/shard_map/dot_general | solution.py:148
  12.6 0.5 %collective-permute-done.5 = f32[8,8]{1,0:T(8,128)S(1)} collective-permute-done((f32[8,8]{1,0:T(8,128)S(1)}, f32[8,8]{1,0:T(8,128)S(1)}, u32[]{:S(2)}, u32[]{:S(2)}) %collective-permute-start.5) | collective-permute-done | bytes 288 | tf_op jit(solution)/shard_map/ppermute | solution.py:28
  13.1 1.3 %collective-permute-start.6 = (f32[8,8]{1,0:T(8,128)S(1)}, f32[8,8]{1,0:T(8,128)S(1)}, u32[]{:S(2)}, u32[]{:S(2)}) collective-permute-start(f32[8,8]{1,0:T(8,128)S(1)} %add.43), channel_id=1, source_target_pairs={{0,20},{1,21},{2,22},{3,23},{4,16},{5,17},{6,18},{7,19},{8,12},{9,... | collective-permute-start | bytes 776 | tf_op jit(solution)/shard_map/ppermute | solution.py:28
  14.4 0.3 %collective-permute-start.10 = (f32[8,8]{1,0:T(8,128)S(1)}, f32[8,8]{1,0:T(8,128)S(1)}, u32[]{:S(2)}, u32[]{:S(2)}) collective-permute-start(f32[8,8]{1,0:T(8,128)S(1)} %add.43), channel_id=1, source_target_pairs={{0,12},{1,13},{2,14},{3,15},{4,8},{5,9},{6,10},{7,11},{8,20},{9,21... | collective-permute-start | bytes 776 | tf_op jit(solution)/shard_map/ppermute | solution.py:28
  14.8 2.3 %collective-permute-start.8 = (f32[8,8]{1,0:T(8,128)S(1)}, f32[8,8]{1,0:T(8,128)S(1)}, u32[]{:S(2)}, u32[]{:S(2)}) collective-permute-start(f32[8,8]{1,0:T(8,128)S(1)} %add.43), channel_id=1, source_target_pairs={{0,28},{1,29},{2,30},{3,31},{4,24},{5,25},{6,26},{7,27},{8,4},{9,5... | collective-permute-start | bytes 776 | tf_op jit(solution)/shard_map/ppermute | solution.py:28
  17.1 0.3 %collective-permute-start.9 = (f32[8,8]{1,0:T(8,128)S(1)}, f32[8,8]{1,0:T(8,128)S(1)}, u32[]{:S(2)}, u32[]{:S(2)}) collective-permute-start(f32[8,8]{1,0:T(8,128)S(1)} %add.43), channel_id=1, source_target_pairs={{0,4},{1,5},{2,6},{3,7},{4,0},{5,1},{6,2},{7,3},{8,28},{9,29},{10,... | collective-permute-start | bytes 776 | tf_op jit(solution)/shard_map/ppermute | solution.py:28
  17.5 0.2 collective-permute-start.11
  17.7 0.7 %collective-permute-done.10 = f32[8,8]{1,0:T(8,128)S(1)} collective-permute-done((f32[8,8]{1,0:T(8,128)S(1)}, f32[8,8]{1,0:T(8,128)S(1)}, u32[]{:S(2)}, u32[]{:S(2)}) %collective-permute-start.10) | collective-permute-done | bytes 288 | tf_op jit(solution)/shard_map/ppermute | solution.py:28
  18.4 0.0 collective-permute-done.8
  18.4 0.3 %collective-permute-done.11 = f32[8,1024]{1,0:T(8,128)S(1)} collective-permute-done((f32[8,1024]{1,0:T(8,128)S(1)}, f32[8,1024]{1,0:T(8,128)S(1)}, u32[]{:S(2)}, u32[]{:S(2)}) %collective-permute-start.11) | collective-permute-done | bytes 32800 | tf_op jit(solution)/shard_map/ppermute | solution.py:28
  18.7 2.0 %collective-permute-start.12 = (f32[8,384]{1,0:T(8,128)S(1)}, f32[8,384]{1,0:T(8,128)S(1)}, u32[]{:S(2)}, u32[]{:S(2)}) collective-permute-start(f32[8,384]{1,0:T(8,128)S(1)} %get-tuple-element.44), channel_id=1, source_target_pairs={{0,5},{1,7},{2,6},{3,4},{4,1},{5,3},{6,2},{7,0},{8,13},{9,15},{10,... | collective-permute-start | bytes 36872 | tf_op jit(solution)/shard_map/ppermute | solution.py:28
  20.7 0.7 %collective-permute-start.13 = (f32[8,384]{1,0:T(8,128)S(1)}, f32[8,384]{1,0:T(8,128)S(1)}, u32[]{:S(2)}, u32[]{:S(2)}) collective-permute-start(f32[8,384]{1,0:T(8,128)S(1)} %get-tuple-element.45), channel_id=1, source_target_pairs={{0,6},{1,5},{2,4},{3,7},{4,2},{5,1},{6,0},{7,3},{8,14},{9,13},{10,... | collective-permute-start | bytes 36872 | tf_op jit(solution)/shard_map/ppermute | solution.py:28
  21.4 1.3 %collective-permute-start.14 = (f32[8,384]{1,0:T(8,128)S(1)}, f32[8,384]{1,0:T(8,128)S(1)}, u32[]{:S(2)}, u32[]{:S(2)}) collective-permute-start(f32[8,384]{1,0:T(8,128)S(1)} %get-tuple-element.46), channel_id=1, source_target_pairs={{0,7},{1,4},{2,5},{3,6},{4,3},{5,0},{6,1},{7,2},{8,15},{9,12},{10,... | collective-permute-start | bytes 36872 | tf_op jit(solution)/shard_map/ppermute | solution.py:28
  22.7 0.2 collective-permute-start.15
  22.9 0.8 %collective-permute-done.12 = f32[8,384]{1,0:T(8,128)S(1)} collective-permute-done((f32[8,384]{1,0:T(8,128)S(1)}, f32[8,384]{1,0:T(8,128)S(1)}, u32[]{:S(2)}, u32[]{:S(2)}) %collective-permute-start.12) | collective-permute-done | bytes 12320 | tf_op jit(solution)/shard_map/ppermute | solution.py:28
  23.7 1.0 %collective-permute-done.13 = f32[8,384]{1,0:T(8,128)S(1)} collective-permute-done((f32[8,384]{1,0:T(8,128)S(1)}, f32[8,384]{1,0:T(8,128)S(1)}, u32[]{:S(2)}, u32[]{:S(2)}) %collective-permute-start.13) | collective-permute-done | bytes 12320 | tf_op jit(solution)/shard_map/ppermute | solution.py:28
  24.8 0.7 %shard_map.50 = (f32[8,256]{1,0:T(8,128)}, f32[8,8]{1,0:T(8,128)}) custom-call(f32[8,384]{1,0:T(8,128)S(1)} %fusion.4.both_ref), custom_call_target="tpu_custom_call" | custom-call | tf_op jit(solution)/shard_map/pallas_call | solution.py:193
  (20 shorter events, 0.1 us)
Async XLA Ops:
  0.6 10.2 %copy-start = (bf16[1024,1024]{1,0:T(8,128)(2,1)S(1)}, bf16[1024,1024]{1,0:T(8,128)(2,1)}, u32[]{:S(2)}) copy-start(bf16[1024,1024]{1,0:T(8,128)(2,1)} %param.3) | copy-start | bytes 6291460
  0.6 8.0 %collective-permute-start = (bf16[8,256]{1,0:T(8,128)(2,1)}, bf16[8,256]{1,0:T(8,128)(2,1)S(1)}, u32[]{:S(2)}, u32[]{:S(2)}) collective-permute-start(bf16[8,256]{1,0:T(8,128)(2,1)} %param.5), channel_id=1, source_target_pairs={{0,2},{1,3},{2,0},{3,1},{4,6},{5,7},{6,4},{7,5},{8,10},{9,11},{10,... | collective-permute-start | bytes 12296 | tf_op jit(solution)/shard_map/ppermute | solution.py:28
  4.7 3.9 %collective-permute-start.1 = (bf16[8,256]{1,0:T(8,128)(2,1)}, bf16[8,256]{1,0:T(8,128)(2,1)S(1)}, u32[]{:S(2)}, u32[]{:S(2)}) collective-permute-start(bf16[8,256]{1,0:T(8,128)(2,1)} %param.5), channel_id=1, source_target_pairs={{0,4},{1,5},{2,3},{3,2},{4,0},{5,1},{6,7},{7,6},{8,12},{9,13},{10,... | collective-permute-start | bytes 12296 | tf_op jit(solution)/shard_map/ppermute | solution.py:28
  4.7 5.6 %collective-permute-start.2 = (bf16[8,256]{1,0:T(8,128)(2,1)}, bf16[8,256]{1,0:T(8,128)(2,1)S(1)}, u32[]{:S(2)}, u32[]{:S(2)}) collective-permute-start(bf16[8,256]{1,0:T(8,128)(2,1)} %param.5), channel_id=1, source_target_pairs={{0,3},{1,2},{2,1},{3,0},{4,7},{5,6},{6,5},{7,4},{8,11},{9,10},{10,... | collective-permute-start | bytes 12296 | tf_op jit(solution)/shard_map/ppermute | solution.py:28
  6.3 4.1 %collective-permute-start.3 = (bf16[8,256]{1,0:T(8,128)(2,1)}, bf16[8,256]{1,0:T(8,128)(2,1)S(1)}, u32[]{:S(2)}, u32[]{:S(2)}) collective-permute-start(bf16[8,256]{1,0:T(8,128)(2,1)} %param.5), channel_id=1, source_target_pairs={{0,1},{1,0},{2,6},{3,7},{4,5},{5,4},{6,2},{7,3},{8,9},{9,8},{10,14... | collective-permute-start | bytes 12296 | tf_op jit(solution)/shard_map/ppermute | solution.py:28
  10.4 1.4 %collective-permute-start.4 = (bf16[8,1024]{1,0:T(8,128)(2,1)S(1)}, bf16[8,1024]{1,0:T(8,128)(2,1)S(1)}, u32[]{:S(2)}, u32[]{:S(2)}) collective-permute-start(bf16[8,1024]{1,0:T(8,128)(2,1)S(1)} %maximum_add_fusion), channel_id=1, source_target_pairs={{0,4},{1,29},{2,26},{3,23},{4,0},{5,1},{6,30},{7,27},{8,12},{9,5},... | collective-permute-start | bytes 49160 | tf_op jit(solution)/shard_map/ppermute | solution.py:28
  11.3 6.2 %collective-permute-start.7 = (f32[8,1024]{1,0:T(8,128)S(1)}, f32[8,1024]{1,0:T(8,128)S(1)}, u32[]{:S(2)}, u32[]{:S(2)}) collective-permute-start(f32[8,1024]{1,0:T(8,128)S(1)} %fusion.1), channel_id=1, source_target_pairs={{0,4},{1,5},{2,10},{3,15},{4,0},{5,9},{6,14},{7,19},{8,12},{9,13},... | collective-permute-start | bytes 98312 | tf_op jit(solution)/shard_map/ppermute | solution.py:28
  11.9 1.2 %collective-permute-start.5 = (f32[8,8]{1,0:T(8,128)S(1)}, f32[8,8]{1,0:T(8,128)S(1)}, u32[]{:S(2)}, u32[]{:S(2)}) collective-permute-start(f32[8,8]{1,0:T(8,128)S(1)} %fusion.19), channel_id=1, source_target_pairs={{0,4},{1,5},{2,6},{3,7},{4,0},{5,1},{6,2},{7,3},{8,12},{9,13},{10,... | collective-permute-start | bytes 776 | tf_op jit(solution)/shard_map/ppermute | solution.py:28
  13.1 4.3 %collective-permute-start.6 = (f32[8,8]{1,0:T(8,128)S(1)}, f32[8,8]{1,0:T(8,128)S(1)}, u32[]{:S(2)}, u32[]{:S(2)}) collective-permute-start(f32[8,8]{1,0:T(8,128)S(1)} %add.43), channel_id=1, source_target_pairs={{0,20},{1,21},{2,22},{3,23},{4,16},{5,17},{6,18},{7,19},{8,12},{9,... | collective-permute-start | bytes 776 | tf_op jit(solution)/shard_map/ppermute | solution.py:28
  14.4 3.9 %collective-permute-start.10 = (f32[8,8]{1,0:T(8,128)S(1)}, f32[8,8]{1,0:T(8,128)S(1)}, u32[]{:S(2)}, u32[]{:S(2)}) collective-permute-start(f32[8,8]{1,0:T(8,128)S(1)} %add.43), channel_id=1, source_target_pairs={{0,12},{1,13},{2,14},{3,15},{4,8},{5,9},{6,10},{7,11},{8,20},{9,21... | collective-permute-start | bytes 776 | tf_op jit(solution)/shard_map/ppermute | solution.py:28
  14.8 3.7 %collective-permute-start.8 = (f32[8,8]{1,0:T(8,128)S(1)}, f32[8,8]{1,0:T(8,128)S(1)}, u32[]{:S(2)}, u32[]{:S(2)}) collective-permute-start(f32[8,8]{1,0:T(8,128)S(1)} %add.43), channel_id=1, source_target_pairs={{0,28},{1,29},{2,30},{3,31},{4,24},{5,25},{6,26},{7,27},{8,4},{9,5... | collective-permute-start | bytes 776 | tf_op jit(solution)/shard_map/ppermute | solution.py:28
  17.1 1.3 %collective-permute-start.9 = (f32[8,8]{1,0:T(8,128)S(1)}, f32[8,8]{1,0:T(8,128)S(1)}, u32[]{:S(2)}, u32[]{:S(2)}) collective-permute-start(f32[8,8]{1,0:T(8,128)S(1)} %add.43), channel_id=1, source_target_pairs={{0,4},{1,5},{2,6},{3,7},{4,0},{5,1},{6,2},{7,3},{8,28},{9,29},{10,... | collective-permute-start | bytes 776 | tf_op jit(solution)/shard_map/ppermute | solution.py:28
  17.5 1.3 %collective-permute-start.11 = (f32[8,1024]{1,0:T(8,128)S(1)}, f32[8,1024]{1,0:T(8,128)S(1)}, u32[]{:S(2)}, u32[]{:S(2)}) collective-permute-start(f32[8,1024]{1,0:T(8,128)S(1)} %select_add_fusion), channel_id=1, source_target_pairs={{0,4},{1,5},{2,6},{3,7},{4,0},{5,1},{6,2},{7,3},{8,12},{9,13},{10,... | collective-permute-start | bytes 98312 | tf_op jit(solution)/shard_map/ppermute | solution.py:28
  18.7 5.0 %collective-permute-start.12 = (f32[8,384]{1,0:T(8,128)S(1)}, f32[8,384]{1,0:T(8,128)S(1)}, u32[]{:S(2)}, u32[]{:S(2)}) collective-permute-start(f32[8,384]{1,0:T(8,128)S(1)} %get-tuple-element.44), channel_id=1, source_target_pairs={{0,5},{1,7},{2,6},{3,4},{4,1},{5,3},{6,2},{7,0},{8,13},{9,15},{10,... | collective-permute-start | bytes 36872 | tf_op jit(solution)/shard_map/ppermute | solution.py:28
  20.7 4.0 %collective-permute-start.13 = (f32[8,384]{1,0:T(8,128)S(1)}, f32[8,384]{1,0:T(8,128)S(1)}, u32[]{:S(2)}, u32[]{:S(2)}) collective-permute-start(f32[8,384]{1,0:T(8,128)S(1)} %get-tuple-element.45), channel_id=1, source_target_pairs={{0,6},{1,5},{2,4},{3,7},{4,2},{5,1},{6,0},{7,3},{8,14},{9,13},{10,... | collective-permute-start | bytes 36872 | tf_op jit(solution)/shard_map/ppermute | solution.py:28
  21.4 3.4 %collective-permute-start.14 = (f32[8,384]{1,0:T(8,128)S(1)}, f32[8,384]{1,0:T(8,128)S(1)}, u32[]{:S(2)}, u32[]{:S(2)}) collective-permute-start(f32[8,384]{1,0:T(8,128)S(1)} %get-tuple-element.46), channel_id=1, source_target_pairs={{0,7},{1,4},{2,5},{3,6},{4,3},{5,0},{6,1},{7,2},{8,15},{9,12},{10,... | collective-permute-start | bytes 36872 | tf_op jit(solution)/shard_map/ppermute | solution.py:28
  22.7 2.1 %collective-permute-start.15 = (f32[8,384]{1,0:T(8,128)S(1)}, f32[8,384]{1,0:T(8,128)S(1)}, u32[]{:S(2)}, u32[]{:S(2)}) collective-permute-start(f32[8,384]{1,0:T(8,128)S(1)} %get-tuple-element.43), channel_id=1, source_target_pairs={{0,4},{1,6},{2,7},{3,5},{4,0},{5,2},{6,3},{7,1},{8,12},{9,14},{10,... | collective-permute-start | bytes 36872 | tf_op jit(solution)/shard_map/ppermute | solution.py:28

commit v7 on v6

--- a/solution.py
+++ b/solution.py
@@ -11,10 +11,11 @@
 AXES = ("row", "col")
 ONE = ((1, 0),)
 ROW_TABLES = ((2, 1, 0, 3), (1, 2, 3, 0), (3, 0, 1, 2), (0, 3, 2, 1))
-ROW_ORDER = (0, 2, 3, 1)
+ROW_ORDER = (0, 3, 1, 2)
 GATHER_TABLES = ((2, 3, 0, 1), (0, 1, 3, 2), (3, 2, 1, 0), (1, 0, 2, 3))
+GATHER_CROSS = (0, 0, 1, 1)
 GATHER_ORDER = (0, 1, 2, 3)
-SUM_TABLES = ((1, 3, 2, 0), (2, 1, 0, 3), (3, 0, 1, 2), (0, 2, 3, 1))
+SUM_TABLES = ((2, 1, 3, 0), (1, 0, 2, 3), (3, 2, 0, 1), (0, 3, 1, 2))
 SUM_ORDER = (0, 1, 2, 3)
 
 
@@ -40,8 +41,11 @@
         goes = [lambda r, c, t=t: (r ^ 1, moved(c, bit, t)) for t in tables]
     else:
         goes = [
-            lambda r, c, t=t: (r ^ (moved(c, bit, t) == c), moved(c, bit, t))
-            for t in tables
+            lambda r, c, t=t, x=x: (
+                r ^ (x or moved(c, bit, t) == c),
+                moved(c, bit, t),
+            )
+            for t, x in zip(tables, GATHER_CROSS)
         ]
     return [send(block, to) for block, to in zip(blocks, goes)]
 
@@ -107,18 +111,18 @@
     col_idx = lax.axis_index("col")
     row_bits, col_bits = rows.bit_length() - 1, cols.bit_length() - 1
 
-    keep = block_map[0, 0].astype(jnp.bfloat16)
-    matrix = (tiles.reshape(parts, SUB, parts, SUB) * keep[:, None, :, None]).reshape(
-        width, width
-    )
-
     source = lanczos_block
     for bit, members in groups_of(0, col_bits):
         place = (col_idx >> bit) % members
         tables = GATHER_TABLES if members == 4 else ONE
-        got = held(
-            exchanged([source] * len(tables), bit, tables, "col"), GATHER_ORDER
-        )
+        mate = send(source, lambda r, c: (r ^ 1, c))
+        given = [source] * len(tables)
+        if bit == 0:
+            mate, source, block_map = lax.optimization_barrier(
+                (mate, source, block_map)
+            )
+        given = [mate if x else block for block, x in zip(given, GATHER_CROSS)]
+        got = held(exchanged(given, bit, tables, "col"), GATHER_ORDER)
         zero = jnp.zeros_like(source)
         placed = jnp.concatenate(
             [jnp.where(place == at, source, zero) for at in range(members)], axis=1
@@ -134,6 +138,11 @@
             axis=1,
         )
 
+    keep = block_map[0, 0].astype(jnp.bfloat16)
+    matrix = (tiles.reshape(parts, SUB, parts, SUB) * keep[:, None, :, None]).reshape(
+        width, width
+    )
+
     far_vec = from_far(source)
     mirror = jnp.dot(source, matrix, preferred_element_type=jnp.float32)
     inside = row_idx + col_idx < rows

time: 25.9 us -> 25.4 us (0.981)
  waiting for transfers between devices: 5.16 us -> 4.48 us
  starting transfers between devices: 15.8 us -> 16.3 us
    ppermute x16 -> x17, waiting for transfers between devices: 5.16 us -> 4.48 us  [send(): return lax.ppermute(block, AXES, pairs)]
    ppermute x16 -> x17, starting transfers between devices: 15.8 us -> 16.3 us  [send(): return lax.ppermute(block, AXES, pairs)]
  transfers between devices with their start and end apart: 16 -> 17, of which waited for: 6 -> 8; matrix products, arithmetic and copies ran while one was open for 12% -> 12% of each run, Pallas kernels for 0% -> 0%
where the time goes in v7:
time: 25.4 us; the launch traced here: 25.2 us
  starting transfers between devices  16.3 us (64%)
  waiting for transfers between devices  4.48 us (18%)
  other arithmetic  1.46 us (6%)
  matrix products  1.23 us (5%)
  between operations  0.71 us (3%)
  Pallas kernels  0.67 us (3%)
  local copies, waits for them, and re-layouts  0.34 us (1%)
    ppermute x17, starting transfers between devices, send(): return lax.ppermute(block, AXES, pairs)  16.3 us
    ppermute x17, waiting for transfers between devices, send(): return lax.ppermute(block, AXES, pairs)  4.48 us
    select_n x1, other arithmetic, on_device(): jnp.where(place == at, source, zero)  0.69 us
    convert_element_type x1, other arithmetic, on_device(): keep = block_map[0, 0].astype(jnp.bfloat16)  0.69 us
    pallas_call x1, Pallas kernels, on_device(): pl.pallas_call(functools.partial(write_results, 1.0 / (width * rows) ** 0...  0.67 us
    dot_general x1, matrix products, on_device(): lax.dot_general(far_vec, matrix, (((1,), (1,)), ((), ())), preferred_elem...  0.65 us
  transfers between devices with their start and end apart: 17, of which 8 were waited for; matrix products, arithmetic and copies ran while one was open for 12% of the time, Pallas kernels for 0%

profile of v7, /device:TPU:0, one launch (start us, length us, event | category | flops | bytes accessed | tf_op | source)
XLA Modules:
  0.0 25.2 jit_solution(7539629407013311892)
XLA Ops:
  0.6 0.5 %collective-permute-start = (bf16[8,256]{1,0:T(8,128)(2,1)}, bf16[8,256]{1,0:T(8,128)(2,1)S(1)}, u32[]{:S(2)}, u32[]{:S(2)}) collective-permute-start(bf16[8,256]{1,0:T(8,128)(2,1)} %param.5), channel_id=1, source_target_pairs={{0,4},{1,5},{2,6},{3,7},{4,0},{5,1},{6,2},{7,3},{8,12},{9,13},{10,... | collective-permute-start | bytes 12296 | tf_op jit(solution)/shard_map/ppermute | solution.py:29
  1.2 3.7 %collective-permute-start.1 = (bf16[8,256]{1,0:T(8,128)(2,1)}, bf16[8,256]{1,0:T(8,128)(2,1)S(1)}, u32[]{:S(2)}, u32[]{:S(2)}) collective-permute-start(bf16[8,256]{1,0:T(8,128)(2,1)} %param.5), channel_id=1, source_target_pairs={{0,2},{1,3},{2,0},{3,1},{4,6},{5,7},{6,4},{7,5},{8,10},{9,11},{10,... | collective-permute-start | bytes 12296 | tf_op jit(solution)/shard_map/ppermute | solution.py:29
  4.8 0.2 collective-permute-start.2
  5.0 1.9 %collective-permute-start.3 = (bf16[8,256]{1,0:T(8,128)(2,1)S(1)}, bf16[8,256]{1,0:T(8,128)(2,1)S(1)}, u32[]{:S(2)}, u32[]{:S(2)}) collective-permute-start(bf16[8,256]{1,0:T(8,128)(2,1)S(1)} %collective-permute-done), channel_id=1, source_target_pairs={{0,7},{1,6},{2,5},{3,4},{4,3},{5,2},{6,1},{7,0},{8,15},{9,14},{10,... | collective-permute-start | bytes 12296 | tf_op jit(solution)/shard_map/ppermute | solution.py:29
  6.9 0.1 collective-permute-start.4
  7.0 0.7 %convert_bitcast_fusion = bf16[8,8]{1,0:T(8,128)(2,1)S(1)} fusion(s32[1,1,8,8]{3,2,1,0:T(8,128)} %param.4), kind=kLoop, calls=%fused_computation.45 | loop fusion | flops 64 | bytes 384 | tf_op jit(solution)/shard_map/convert_element_type | solution.py:141
  7.7 0.7 %broadcast_select_fusion.3 = (bf16[8,256]{1,0:T(8,128)(2,1)S(1)}, bf16[8,256]{1,0:T(8,128)(2,1)S(1)}, bf16[8,256]{1,0:T(8,128)(2,1)S(1)}, bf16[8,256]{1,0:T(8,128)(2,1)S(1)}) fusion(bf16[8,256]{1,0:T(8,128)(2,1)} %param.5, pred[]{:T(512)S(6)} %eq.20, pred[]{:T(512)S(6)} %eq.23, pred[]{:T(512)S(6)} %eq.22, pred[]{:T(512)S(6)} %eq.21), kind=kLoop, calls=%fused_computation.43 | loop fusion | flops 8192 | bytes 20484 | tf_op jit(solution)/shard_map/jit(_where)/select_n | solution.py:128
  8.4 1.4 %collective-permute-done.3 = bf16[8,256]{1,0:T(8,128)(2,1)S(1)} collective-permute-done((bf16[8,256]{1,0:T(8,128)(2,1)S(1)}, bf16[8,256]{1,0:T(8,128)(2,1)S(1)}, u32[]{:S(2)}, u32[]{:S(2)}) %collective-permute-start.3) | collective-permute-done | bytes 4128 | tf_op jit(solution)/shard_map/ppermute | solution.py:29
  9.8 0.1 collective-permute-done.4
  10.0 0.4 %collective-permute-start.5 = (bf16[8,1024]{1,0:T(8,128)(2,1)S(1)}, bf16[8,1024]{1,0:T(8,128)(2,1)S(1)}, u32[]{:S(2)}, u32[]{:S(2)}) collective-permute-start(bf16[8,1024]{1,0:T(8,128)(2,1)S(1)} %maximum_add_fusion), channel_id=1, source_target_pairs={{0,4},{1,29},{2,26},{3,23},{4,0},{5,1},{6,30},{7,27},{8,12},{9,5},... | collective-permute-start | bytes 49160 | tf_op jit(solution)/shard_map/ppermute | solution.py:29
  10.4 0.3 %mul.11 = bf16[8,128,8,128]{3,2,1,0:T(8,128)(2,1)S(1)} broadcast(bf16[8,8]{1,0:T(8,128)(2,1)S(1)} %convert_bitcast_fusion), dimensions={0,2} | broadcast | bytes 2097280 | tf_op jit(solution)/shard_map/mul | solution.py:142
  10.7 0.5 %fusion.1 = f32[8,1024]{1,0:T(8,128)S(1)} fusion(bf16[8,1024]{1,0:T(8,128)(2,1)S(1)} %maximum_add_fusion, bf16[1024,1024]{1,0:T(8,128)(2,1)S(1)} %copy-done, bf16[128,8,8,128]{3,2,1,0:T(8,128)(2,1)S(1)} %bitcast.10), kind=kOutput, calls=%fused_computation.2 | convolution fusion | flops 17825792 | bytes 4243456 | tf_op jit(solution)/shard_map/dot_general | solution.py:147
  11.2 0.2 collective-permute-start.8
  11.3 0.1 fusion.18
  11.5 0.4 %collective-permute-start.6 = (f32[8,8]{1,0:T(8,128)S(1)}, f32[8,8]{1,0:T(8,128)S(1)}, u32[]{:S(2)}, u32[]{:S(2)}) collective-permute-start(f32[8,8]{1,0:T(8,128)S(1)} %fusion.18), channel_id=1, source_target_pairs={{0,4},{1,5},{2,6},{3,7},{4,0},{5,1},{6,2},{7,3},{8,12},{9,13},{10,... | collective-permute-start | bytes 776 | tf_op jit(solution)/shard_map/ppermute | solution.py:29
  11.8 0.7 %fusion = f32[8,1024]{1,0:T(8,128)S(1)} fusion(bf16[1024,1024]{1,0:T(8,128)(2,1)S(1)} %copy-done, bf16[128,8,8,128]{3,2,1,0:T(8,128)(2,1)S(1)} %bitcast.11, bf16[8,1024]{1,0:T(8,128)(2,1)S(1)} %maximum_add_fusion, bf16[8,1024]{1,0:T(8,128)(2,1)S(1)} %collective-permute-done.5, pred[]{:T(512)S(6)} %lt.16, pred[]{:T(512)S(6)} %eq.24), kind=kOutput, calls=%fused_computation.1 | convolution fusion | flops 17842176 | bytes 4259842 | tf_op jit(solution)/shard_map/dot_general | solution.py:157
  12.5 0.2 collective-permute-done.6
  12.7 1.5 %collective-permute-start.7 = (f32[8,8]{1,0:T(8,128)S(1)}, f32[8,8]{1,0:T(8,128)S(1)}, u32[]{:S(2)}, u32[]{:S(2)}) collective-permute-start(f32[8,8]{1,0:T(8,128)S(1)} %add.43), channel_id=1, source_target_pairs={{0,20},{1,21},{2,22},{3,23},{4,16},{5,17},{6,18},{7,19},{8,12},{9,... | collective-permute-start | bytes 776 | tf_op jit(solution)/shard_map/ppermute | solution.py:29
  14.1 0.1 collective-permute-start.10
  14.3 2.5 %collective-permute-start.11 = (f32[8,8]{1,0:T(8,128)S(1)}, f32[8,8]{1,0:T(8,128)S(1)}, u32[]{:S(2)}, u32[]{:S(2)}) collective-permute-start(f32[8,8]{1,0:T(8,128)S(1)} %add.43), channel_id=1, source_target_pairs={{0,28},{1,29},{2,30},{3,31},{4,24},{5,25},{6,26},{7,27},{8,4},{9,5... | collective-permute-start | bytes 776 | tf_op jit(solution)/shard_map/ppermute | solution.py:29
  16.8 0.2 collective-permute-start.9
  17.0 0.4 %collective-permute-start.12 = (f32[8,1024]{1,0:T(8,128)S(1)}, f32[8,1024]{1,0:T(8,128)S(1)}, u32[]{:S(2)}, u32[]{:S(2)}) collective-permute-start(f32[8,1024]{1,0:T(8,128)S(1)} %select_add_fusion), channel_id=1, source_target_pairs={{0,4},{1,5},{2,6},{3,7},{4,0},{5,1},{6,2},{7,3},{8,12},{9,13},{10,... | collective-permute-start | bytes 98312 | tf_op jit(solution)/shard_map/ppermute | solution.py:29
  17.4 0.7 %collective-permute-done.10 = f32[8,8]{1,0:T(8,128)S(1)} collective-permute-done((f32[8,8]{1,0:T(8,128)S(1)}, f32[8,8]{1,0:T(8,128)S(1)}, u32[]{:S(2)}, u32[]{:S(2)}) %collective-permute-start.10) | collective-permute-done | bytes 288 | tf_op jit(solution)/shard_map/ppermute | solution.py:29
  18.1 0.1 collective-permute-done.12
  18.3 2.1 %collective-permute-start.13 = (f32[8,384]{1,0:T(8,128)S(1)}, f32[8,384]{1,0:T(8,128)S(1)}, u32[]{:S(2)}, u32[]{:S(2)}) collective-permute-start(f32[8,384]{1,0:T(8,128)S(1)} %get-tuple-element.50), channel_id=1, source_target_pairs={{0,6},{1,5},{2,7},{3,4},{4,2},{5,1},{6,3},{7,0},{8,14},{9,13},{10,... | collective-permute-start | bytes 36872 | tf_op jit(solution)/shard_map/ppermute | solution.py:29
  20.4 0.1 collective-permute-start.14
  20.5 1.9 %collective-permute-start.15 = (f32[8,384]{1,0:T(8,128)S(1)}, f32[8,384]{1,0:T(8,128)S(1)}, u32[]{:S(2)}, u32[]{:S(2)}) collective-permute-start(f32[8,384]{1,0:T(8,128)S(1)} %get-tuple-element.52), channel_id=1, source_target_pairs={{0,7},{1,6},{2,4},{3,5},{4,3},{5,2},{6,0},{7,1},{8,15},{9,14},{10,... | collective-permute-start | bytes 36872 | tf_op jit(solution)/shard_map/ppermute | solution.py:29
  22.4 0.2 collective-permute-start.16
  22.6 0.8 %collective-permute-done.13 = f32[8,384]{1,0:T(8,128)S(1)} collective-permute-done((f32[8,384]{1,0:T(8,128)S(1)}, f32[8,384]{1,0:T(8,128)S(1)}, u32[]{:S(2)}, u32[]{:S(2)}) %collective-permute-start.13) | collective-permute-done | bytes 12320 | tf_op jit(solution)/shard_map/ppermute | solution.py:29
  23.4 0.1 collective-permute-done.14
  23.5 1.0 %collective-permute-done.15 = f32[8,384]{1,0:T(8,128)S(1)} collective-permute-done((f32[8,384]{1,0:T(8,128)S(1)}, f32[8,384]{1,0:T(8,128)S(1)}, u32[]{:S(2)}, u32[]{:S(2)}) %collective-permute-start.15) | collective-permute-done | bytes 12320 | tf_op jit(solution)/shard_map/ppermute | solution.py:29
  24.5 0.7 %shard_map.50 = (f32[8,256]{1,0:T(8,128)}, f32[8,8]{1,0:T(8,128)}) custom-call(f32[8,384]{1,0:T(8,128)S(1)} %fusion.3.both_ref), custom_call_target="tpu_custom_call" | custom-call | tf_op jit(solution)/shard_map/pallas_call | solution.py:202
  (22 shorter events, 0.1 us)
Async XLA Ops:
  0.6 10.1 %copy-start = (bf16[1024,1024]{1,0:T(8,128)(2,1)S(1)}, bf16[1024,1024]{1,0:T(8,128)(2,1)}, u32[]{:S(2)}) copy-start(bf16[1024,1024]{1,0:T(8,128)(2,1)} %param.3) | copy-start | bytes 6291460
  0.6 4.3 %collective-permute-start = (bf16[8,256]{1,0:T(8,128)(2,1)}, bf16[8,256]{1,0:T(8,128)(2,1)S(1)}, u32[]{:S(2)}, u32[]{:S(2)}) collective-permute-start(bf16[8,256]{1,0:T(8,128)(2,1)} %param.5), channel_id=1, source_target_pairs={{0,4},{1,5},{2,6},{3,7},{4,0},{5,1},{6,2},{7,3},{8,12},{9,13},{10,... | collective-permute-start | bytes 12296 | tf_op jit(solution)/shard_map/ppermute | solution.py:29
  1.2 7.3 %collective-permute-start.1 = (bf16[8,256]{1,0:T(8,128)(2,1)}, bf16[8,256]{1,0:T(8,128)(2,1)S(1)}, u32[]{:S(2)}, u32[]{:S(2)}) collective-permute-start(bf16[8,256]{1,0:T(8,128)(2,1)} %param.5), channel_id=1, source_target_pairs={{0,2},{1,3},{2,0},{3,1},{4,6},{5,7},{6,4},{7,5},{8,10},{9,11},{10,... | collective-permute-start | bytes 12296 | tf_op jit(solution)/shard_map/ppermute | solution.py:29
  4.8 3.6 %collective-permute-start.2 = (bf16[8,256]{1,0:T(8,128)(2,1)}, bf16[8,256]{1,0:T(8,128)(2,1)S(1)}, u32[]{:S(2)}, u32[]{:S(2)}) collective-permute-start(bf16[8,256]{1,0:T(8,128)(2,1)} %param.5), channel_id=1, source_target_pairs={{0,4},{1,5},{2,3},{3,2},{4,0},{5,1},{6,7},{7,6},{8,12},{9,13},{10,... | collective-permute-start | bytes 12296 | tf_op jit(solution)/shard_map/ppermute | solution.py:29
  5.0 4.8 %collective-permute-start.3 = (bf16[8,256]{1,0:T(8,128)(2,1)S(1)}, bf16[8,256]{1,0:T(8,128)(2,1)S(1)}, u32[]{:S(2)}, u32[]{:S(2)}) collective-permute-start(bf16[8,256]{1,0:T(8,128)(2,1)S(1)} %collective-permute-done), channel_id=1, source_target_pairs={{0,7},{1,6},{2,5},{3,4},{4,3},{5,2},{6,1},{7,0},{8,15},{9,14},{10,... | collective-permute-start | bytes 12296 | tf_op jit(solution)/shard_map/ppermute | solution.py:29
  6.9 3.0 %collective-permute-start.4 = (bf16[8,256]{1,0:T(8,128)(2,1)S(1)}, bf16[8,256]{1,0:T(8,128)(2,1)S(1)}, u32[]{:S(2)}, u32[]{:S(2)}) collective-permute-start(bf16[8,256]{1,0:T(8,128)(2,1)S(1)} %collective-permute-done), channel_id=1, source_target_pairs={{0,5},{1,4},{2,6},{3,7},{4,1},{5,0},{6,2},{7,3},{8,13},{9,12},{10,... | collective-permute-start | bytes 12296 | tf_op jit(solution)/shard_map/ppermute | solution.py:29
  10.0 1.4 %collective-permute-start.5 = (bf16[8,1024]{1,0:T(8,128)(2,1)S(1)}, bf16[8,1024]{1,0:T(8,128)(2,1)S(1)}, u32[]{:S(2)}, u32[]{:S(2)}) collective-permute-start(bf16[8,1024]{1,0:T(8,128)(2,1)S(1)} %maximum_add_fusion), channel_id=1, source_target_pairs={{0,4},{1,29},{2,26},{3,23},{4,0},{5,1},{6,30},{7,27},{8,12},{9,5},... | collective-permute-start | bytes 49160 | tf_op jit(solution)/shard_map/ppermute | solution.py:29
  11.2 5.8 %collective-permute-start.8 = (f32[8,1024]{1,0:T(8,128)S(1)}, f32[8,1024]{1,0:T(8,128)S(1)}, u32[]{:S(2)}, u32[]{:S(2)}) collective-permute-start(f32[8,1024]{1,0:T(8,128)S(1)} %fusion.1), channel_id=1, source_target_pairs={{0,4},{1,5},{2,10},{3,15},{4,0},{5,9},{6,14},{7,19},{8,12},{9,13},... | collective-permute-start | bytes 98312 | tf_op jit(solution)/shard_map/ppermute | solution.py:29
  11.5 1.2 %collective-permute-start.6 = (f32[8,8]{1,0:T(8,128)S(1)}, f32[8,8]{1,0:T(8,128)S(1)}, u32[]{:S(2)}, u32[]{:S(2)}) collective-permute-start(f32[8,8]{1,0:T(8,128)S(1)} %fusion.18), channel_id=1, source_target_pairs={{0,4},{1,5},{2,6},{3,7},{4,0},{5,1},{6,2},{7,3},{8,12},{9,13},{10,... | collective-permute-start | bytes 776 | tf_op jit(solution)/shard_map/ppermute | solution.py:29
  12.7 4.3 %collective-permute-start.7 = (f32[8,8]{1,0:T(8,128)S(1)}, f32[8,8]{1,0:T(8,128)S(1)}, u32[]{:S(2)}, u32[]{:S(2)}) collective-permute-start(f32[8,8]{1,0:T(8,128)S(1)} %add.43), channel_id=1, source_target_pairs={{0,20},{1,21},{2,22},{3,23},{4,16},{5,17},{6,18},{7,19},{8,12},{9,... | collective-permute-start | bytes 776 | tf_op jit(solution)/shard_map/ppermute | solution.py:29
  14.1 3.9 %collective-permute-start.10 = (f32[8,8]{1,0:T(8,128)S(1)}, f32[8,8]{1,0:T(8,128)S(1)}, u32[]{:S(2)}, u32[]{:S(2)}) collective-permute-start(f32[8,8]{1,0:T(8,128)S(1)} %add.43), channel_id=1, source_target_pairs={{0,12},{1,13},{2,14},{3,15},{4,8},{5,9},{6,10},{7,11},{8,20},{9,21... | collective-permute-start | bytes 776 | tf_op jit(solution)/shard_map/ppermute | solution.py:29
  14.3 3.8 %collective-permute-start.11 = (f32[8,8]{1,0:T(8,128)S(1)}, f32[8,8]{1,0:T(8,128)S(1)}, u32[]{:S(2)}, u32[]{:S(2)}) collective-permute-start(f32[8,8]{1,0:T(8,128)S(1)} %add.43), channel_id=1, source_target_pairs={{0,28},{1,29},{2,30},{3,31},{4,24},{5,25},{6,26},{7,27},{8,4},{9,5... | collective-permute-start | bytes 776 | tf_op jit(solution)/shard_map/ppermute | solution.py:29
  16.8 1.3 %collective-permute-start.9 = (f32[8,8]{1,0:T(8,128)S(1)}, f32[8,8]{1,0:T(8,128)S(1)}, u32[]{:S(2)}, u32[]{:S(2)}) collective-permute-start(f32[8,8]{1,0:T(8,128)S(1)} %add.43), channel_id=1, source_target_pairs={{0,4},{1,5},{2,6},{3,7},{4,0},{5,1},{6,2},{7,3},{8,28},{9,29},{10,... | collective-permute-start | bytes 776 | tf_op jit(solution)/shard_map/ppermute | solution.py:29
  17.0 1.3 %collective-permute-start.12 = (f32[8,1024]{1,0:T(8,128)S(1)}, f32[8,1024]{1,0:T(8,128)S(1)}, u32[]{:S(2)}, u32[]{:S(2)}) collective-permute-start(f32[8,1024]{1,0:T(8,128)S(1)} %select_add_fusion), channel_id=1, source_target_pairs={{0,4},{1,5},{2,6},{3,7},{4,0},{5,1},{6,2},{7,3},{8,12},{9,13},{10,... | collective-permute-start | bytes 98312 | tf_op jit(solution)/shard_map/ppermute | solution.py:29
  18.3 5.1 %collective-permute-start.13 = (f32[8,384]{1,0:T(8,128)S(1)}, f32[8,384]{1,0:T(8,128)S(1)}, u32[]{:S(2)}, u32[]{:S(2)}) collective-permute-start(f32[8,384]{1,0:T(8,128)S(1)} %get-tuple-element.50), channel_id=1, source_target_pairs={{0,6},{1,5},{2,7},{3,4},{4,2},{5,1},{6,3},{7,0},{8,14},{9,13},{10,... | collective-permute-start | bytes 36872 | tf_op jit(solution)/shard_map/ppermute | solution.py:29
  20.4 3.1 %collective-permute-start.14 = (f32[8,384]{1,0:T(8,128)S(1)}, f32[8,384]{1,0:T(8,128)S(1)}, u32[]{:S(2)}, u32[]{:S(2)}) collective-permute-start(f32[8,384]{1,0:T(8,128)S(1)} %get-tuple-element.51), channel_id=1, source_target_pairs={{0,5},{1,4},{2,6},{3,7},{4,1},{5,0},{6,2},{7,3},{8,13},{9,12},{10,... | collective-permute-start | bytes 36872 | tf_op jit(solution)/shard_map/ppermute | solution.py:29
  20.5 4.0 %collective-permute-start.15 = (f32[8,384]{1,0:T(8,128)S(1)}, f32[8,384]{1,0:T(8,128)S(1)}, u32[]{:S(2)}, u32[]{:S(2)}) collective-permute-start(f32[8,384]{1,0:T(8,128)S(1)} %get-tuple-element.52), channel_id=1, source_target_pairs={{0,7},{1,6},{2,4},{3,5},{4,3},{5,2},{6,0},{7,1},{8,15},{9,14},{10,... | collective-permute-start | bytes 36872 | tf_op jit(solution)/shard_map/ppermute | solution.py:29
  22.4 2.1 %collective-permute-start.16 = (f32[8,384]{1,0:T(8,128)S(1)}, f32[8,384]{1,0:T(8,128)S(1)}, u32[]{:S(2)}, u32[]{:S(2)}) collective-permute-start(f32[8,384]{1,0:T(8,128)S(1)} %get-tuple-element.49), channel_id=1, source_target_pairs={{0,4},{1,7},{2,5},{3,6},{4,0},{5,3},{6,1},{7,2},{8,12},{9,15},{10,... | collective-permute-start | bytes 36872 | tf_op jit(solution)/shard_map/ppermute | solution.py:29

commit v8 on v7

--- a/solution.py
+++ b/solution.py
@@ -11,7 +11,7 @@
 AXES = ("row", "col")
 ONE = ((1, 0),)
 ROW_TABLES = ((2, 1, 0, 3), (1, 2, 3, 0), (3, 0, 1, 2), (0, 3, 2, 1))
-ROW_ORDER = (0, 3, 1, 2)
+ROW_ORDER = (0, 1, 2, 3)
 GATHER_TABLES = ((2, 3, 0, 1), (0, 1, 3, 2), (3, 2, 1, 0), (1, 0, 2, 3))
 GATHER_CROSS = (0, 0, 1, 1)
 GATHER_ORDER = (0, 1, 2, 3)
@@ -158,15 +158,27 @@
         far_vec, matrix, (((1,), (1,)), ((), ())), preferred_element_type=jnp.float32
     )
 
-    gram = gram + send(gram, lambda r, c: (r ^ 1, c))
-    gram, plain = lax.optimization_barrier((gram, plain))
+    mate_gram = send(gram, lambda r, c: (r ^ 1, c))
     arrived = to_far(mirror)
     for bit, members in groups_of(1, row_bits):
         place = (row_idx >> bit) % members
         tables = ROW_TABLES if members == 4 else ONE
-        got = exchanged([gram] * len(tables), bit, tables, "row")
+        early = members == 4 and bit == 1
+        if early:
+            first = exchanged([gram], bit, tables[:1], "row")[0]
         if bit == 1:
-            got[0], arrived = lax.optimization_barrier((got[0], arrived))
+            gram = gram + mate_gram
+            plain, gram = lax.optimization_barrier((plain, gram))
+        if early:
+            first, arrived = lax.optimization_barrier((first, arrived))
+            last = jnp.where(place % 2 == 0, first, gram)
+            got = exchanged([gram, gram, last], bit, tables[1:], "row")
+            got = [first + got[2]] + got
+        else:
+            got = exchanged([gram] * len(tables), bit, tables, "row")
+        if bit == 1:
+            if not early:
+                got[0], arrived = lax.optimization_barrier((got[0], arrived))
             arrived = jnp.where(row_idx >= col_idx, arrived, jnp.zeros_like(arrived))
             arrived = jnp.where(col_idx == 0, mirror, arrived)
             sums = plain + arrived

time: 25.4 us -> 25.4 us (level)
  transfers between devices with their start and end apart: 17 -> 17, of which waited for: 8 -> 7; matrix products, arithmetic and copies ran while one was open for 12% -> 12% of each run, Pallas kernels for 0% -> 0%
where the time goes in v8:
time: 25.4 us; the launch traced here: 25.1 us
  starting transfers between devices  16.2 us (64%)
  waiting for transfers between devices  4.49 us (18%)
  other arithmetic  1.47 us (6%)
  matrix products  1.23 us (5%)
  between operations  0.71 us (3%)
  Pallas kernels  0.67 us (3%)
  local copies, waits for them, and re-layouts  0.34 us (1%)
    ppermute x17, starting transfers between devices, send(): return lax.ppermute(block, AXES, pairs)  16.2 us
    ppermute x17, waiting for transfers between devices, send(): return lax.ppermute(block, AXES, pairs)  4.49 us
    select_n x1, other arithmetic, on_device(): jnp.where(place == at, source, zero)  0.69 us
    convert_element_type x1, other arithmetic, on_device(): keep = block_map[0, 0].astype(jnp.bfloat16)  0.69 us
    pallas_call x1, Pallas kernels, on_device(): pl.pallas_call(functools.partial(write_results, 1.0 / (width * rows) ** 0...  0.67 us
    dot_general x1, matrix products, on_device(): lax.dot_general(far_vec, matrix, (((1,), (1,)), ((), ())), preferred_elem...  0.65 us
  transfers between devices with their start and end apart: 17, of which 7 were waited for; matrix products, arithmetic and copies ran while one was open for 12% of the time, Pallas kernels for 0%

profile of v8, /device:TPU:0, one launch (start us, length us, event | category | flops | bytes accessed | tf_op | source)
XLA Modules:
  0.0 25.1 jit_solution(11109341239047123565)
XLA Ops:
  0.6 0.5 %collective-permute-start = (bf16[8,256]{1,0:T(8,128)(2,1)}, bf16[8,256]{1,0:T(8,128)(2,1)S(1)}, u32[]{:S(2)}, u32[]{:S(2)}) collective-permute-start(bf16[8,256]{1,0:T(8,128)(2,1)} %param.5), channel_id=1, source_target_pairs={{0,4},{1,5},{2,6},{3,7},{4,0},{5,1},{6,2},{7,3},{8,12},{9,13},{10,... | collective-permute-start | bytes 12296 | tf_op jit(solution)/shard_map/ppermute | solution.py:29
  1.2 3.7 %collective-permute-start.1 = (bf16[8,256]{1,0:T(8,128)(2,1)}, bf16[8,256]{1,0:T(8,128)(2,1)S(1)}, u32[]{:S(2)}, u32[]{:S(2)}) collective-permute-start(bf16[8,256]{1,0:T(8,128)(2,1)} %param.5), channel_id=1, source_target_pairs={{0,2},{1,3},{2,0},{3,1},{4,6},{5,7},{6,4},{7,5},{8,10},{9,11},{10,... | collective-permute-start | bytes 12296 | tf_op jit(solution)/shard_map/ppermute | solution.py:29
  4.8 0.2 collective-permute-start.2
  5.0 1.9 %collective-permute-start.3 = (bf16[8,256]{1,0:T(8,128)(2,1)S(1)}, bf16[8,256]{1,0:T(8,128)(2,1)S(1)}, u32[]{:S(2)}, u32[]{:S(2)}) collective-permute-start(bf16[8,256]{1,0:T(8,128)(2,1)S(1)} %collective-permute-done), channel_id=1, source_target_pairs={{0,7},{1,6},{2,5},{3,4},{4,3},{5,2},{6,1},{7,0},{8,15},{9,14},{10,... | collective-permute-start | bytes 12296 | tf_op jit(solution)/shard_map/ppermute | solution.py:29
  6.9 0.1 collective-permute-start.4
  7.0 0.7 %convert_bitcast_fusion = bf16[8,8]{1,0:T(8,128)(2,1)S(1)} fusion(s32[1,1,8,8]{3,2,1,0:T(8,128)} %param.4), kind=kLoop, calls=%fused_computation.45 | loop fusion | flops 64 | bytes 384 | tf_op jit(solution)/shard_map/convert_element_type | solution.py:141
  7.7 0.7 %broadcast_select_fusion.3 = (bf16[8,256]{1,0:T(8,128)(2,1)S(1)}, bf16[8,256]{1,0:T(8,128)(2,1)S(1)}, bf16[8,256]{1,0:T(8,128)(2,1)S(1)}, bf16[8,256]{1,0:T(8,128)(2,1)S(1)}) fusion(bf16[8,256]{1,0:T(8,128)(2,1)} %param.5, pred[]{:T(512)S(6)} %eq.23, pred[]{:T(512)S(6)} %eq.27, pred[]{:T(512)S(6)} %eq.26, pred[]{:T(512)S(6)} %eq.25), kind=kLoop, calls=%fused_computation.43 | loop fusion | flops 8192 | bytes 20484 | tf_op jit(solution)/shard_map/jit(_where)/select_n | solution.py:128
  8.4 1.4 %collective-permute-done.3 = bf16[8,256]{1,0:T(8,128)(2,1)S(1)} collective-permute-done((bf16[8,256]{1,0:T(8,128)(2,1)S(1)}, bf16[8,256]{1,0:T(8,128)(2,1)S(1)}, u32[]{:S(2)}, u32[]{:S(2)}) %collective-permute-start.3) | collective-permute-done | bytes 4128 | tf_op jit(solution)/shard_map/ppermute | solution.py:29
  9.8 0.1 collective-permute-done.4
  10.0 0.4 %collective-permute-start.5 = (bf16[8,1024]{1,0:T(8,128)(2,1)S(1)}, bf16[8,1024]{1,0:T(8,128)(2,1)S(1)}, u32[]{:S(2)}, u32[]{:S(2)}) collective-permute-start(bf16[8,1024]{1,0:T(8,128)(2,1)S(1)} %maximum_add_fusion), channel_id=1, source_target_pairs={{0,4},{1,29},{2,26},{3,23},{4,0},{5,1},{6,30},{7,27},{8,12},{9,5},... | collective-permute-start | bytes 49160 | tf_op jit(solution)/shard_map/ppermute | solution.py:29
  10.4 0.3 %mul.11 = bf16[8,128,8,128]{3,2,1,0:T(8,128)(2,1)S(1)} broadcast(bf16[8,8]{1,0:T(8,128)(2,1)S(1)} %convert_bitcast_fusion), dimensions={0,2} | broadcast | bytes 2097280 | tf_op jit(solution)/shard_map/mul | solution.py:142
  10.7 0.5 %fusion = f32[8,1024]{1,0:T(8,128)S(1)} fusion(bf16[8,1024]{1,0:T(8,128)(2,1)S(1)} %maximum_add_fusion, bf16[1024,1024]{1,0:T(8,128)(2,1)S(1)} %copy-done, bf16[128,8,8,128]{3,2,1,0:T(8,128)(2,1)S(1)} %bitcast.10), kind=kOutput, calls=%fused_computation.1 | convolution fusion | flops 17825792 | bytes 4243456 | tf_op jit(solution)/shard_map/dot_general | solution.py:147
  11.2 0.2 collective-permute-start.8
  11.3 0.1 fusion.18
  11.5 0.4 %collective-permute-start.6 = (f32[8,8]{1,0:T(8,128)S(1)}, f32[8,8]{1,0:T(8,128)S(1)}, u32[]{:S(2)}, u32[]{:S(2)}) collective-permute-start(f32[8,8]{1,0:T(8,128)S(1)} %fusion.18), channel_id=1, source_target_pairs={{0,4},{1,5},{2,6},{3,7},{4,0},{5,1},{6,2},{7,3},{8,12},{9,13},{10,... | collective-permute-start | bytes 776 | tf_op jit(solution)/shard_map/ppermute | solution.py:29
  11.8 1.3 %collective-permute-start.7 = (f32[8,8]{1,0:T(8,128)S(1)}, f32[8,8]{1,0:T(8,128)S(1)}, u32[]{:S(2)}, u32[]{:S(2)}) collective-permute-start(f32[8,8]{1,0:T(8,128)S(1)} %fusion.18), channel_id=1, source_target_pairs={{0,20},{1,21},{2,22},{3,23},{4,16},{5,17},{6,18},{7,19},{8,12},{9,... | collective-permute-start | bytes 776 | tf_op jit(solution)/shard_map/ppermute | solution.py:29
  13.1 0.7 %fusion.1 = f32[8,1024]{1,0:T(8,128)S(1)} fusion(bf16[1024,1024]{1,0:T(8,128)(2,1)S(1)} %copy-done, bf16[128,8,8,128]{3,2,1,0:T(8,128)(2,1)S(1)} %bitcast.11, bf16[8,1024]{1,0:T(8,128)(2,1)S(1)} %maximum_add_fusion, bf16[8,1024]{1,0:T(8,128)(2,1)S(1)} %collective-permute-done.5, pred[]{:T(512)S(6)} %lt.20, pred[]{:T(512)S(6)} %eq.24), kind=kOutput, calls=%fused_computation.2 | convolution fusion | flops 17842176 | bytes 4259842 | tf_op jit(solution)/shard_map/dot_general | solution.py:157
  13.8 0.4 %collective-permute-start.10 = (f32[8,8]{1,0:T(8,128)S(1)}, f32[8,8]{1,0:T(8,128)S(1)}, u32[]{:S(2)}, u32[]{:S(2)}) collective-permute-start(f32[8,8]{1,0:T(8,128)S(1)} %add.49), channel_id=1, source_target_pairs={{0,12},{1,13},{2,14},{3,15},{4,8},{5,9},{6,10},{7,11},{8,20},{9,21... | collective-permute-start | bytes 776 | tf_op jit(solution)/shard_map/ppermute | solution.py:29
  14.2 2.3 %collective-permute-start.11 = (f32[8,8]{1,0:T(8,128)S(1)}, f32[8,8]{1,0:T(8,128)S(1)}, u32[]{:S(2)}, u32[]{:S(2)}) collective-permute-start(f32[8,8]{1,0:T(8,128)S(1)} %add.49), channel_id=1, source_target_pairs={{0,28},{1,29},{2,30},{3,31},{4,24},{5,25},{6,26},{7,27},{8,4},{9,5... | collective-permute-start | bytes 776 | tf_op jit(solution)/shard_map/ppermute | solution.py:29
  16.5 0.4 %collective-permute-start.9 = (f32[8,8]{1,0:T(8,128)S(1)}, f32[8,8]{1,0:T(8,128)S(1)}, u32[]{:S(2)}, u32[]{:S(2)}) collective-permute-start(f32[8,8]{1,0:T(8,128)S(1)} %broadcast_select_fusion.4), channel_id=1, source_target_pairs={{0,4},{1,5},{2,6},{3,7},{4,0},{5,1},{6,2},{7,3},{8,28},{9,29},{10,... | collective-permute-start | bytes 776 | tf_op jit(solution)/shard_map/ppermute | solution.py:29
  16.9 0.2 collective-permute-start.12
  17.2 0.6 %collective-permute-done.9 = f32[8,8]{1,0:T(8,128)S(1)} collective-permute-done((f32[8,8]{1,0:T(8,128)S(1)}, f32[8,8]{1,0:T(8,128)S(1)}, u32[]{:S(2)}, u32[]{:S(2)}) %collective-permute-start.9) | collective-permute-done | bytes 288 | tf_op jit(solution)/shard_map/ppermute | solution.py:29
  17.8 0.0 collective-permute-done.11
  17.8 0.4 %collective-permute-done.12 = f32[8,1024]{1,0:T(8,128)S(1)} collective-permute-done((f32[8,1024]{1,0:T(8,128)S(1)}, f32[8,1024]{1,0:T(8,128)S(1)}, u32[]{:S(2)}, u32[]{:S(2)}) %collective-permute-start.12) | collective-permute-done | bytes 32800 | tf_op jit(solution)/shard_map/ppermute | solution.py:29
  18.2 2.1 %collective-permute-start.13 = (f32[8,384]{1,0:T(8,128)S(1)}, f32[8,384]{1,0:T(8,128)S(1)}, u32[]{:S(2)}, u32[]{:S(2)}) collective-permute-start(f32[8,384]{1,0:T(8,128)S(1)} %get-tuple-element.50), channel_id=1, source_target_pairs={{0,6},{1,5},{2,7},{3,4},{4,2},{5,1},{6,3},{7,0},{8,14},{9,13},{10,... | collective-permute-start | bytes 36872 | tf_op jit(solution)/shard_map/ppermute | solution.py:29
  20.3 0.1 collective-permute-start.14
  20.4 1.7 %collective-permute-start.15 = (f32[8,384]{1,0:T(8,128)S(1)}, f32[8,384]{1,0:T(8,128)S(1)}, u32[]{:S(2)}, u32[]{:S(2)}) collective-permute-start(f32[8,384]{1,0:T(8,128)S(1)} %get-tuple-element.52), channel_id=1, source_target_pairs={{0,7},{1,6},{2,4},{3,5},{4,3},{5,2},{6,0},{7,1},{8,15},{9,14},{10,... | collective-permute-start | bytes 36872 | tf_op jit(solution)/shard_map/ppermute | solution.py:29
  22.2 0.3 %collective-permute-start.16 = (f32[8,384]{1,0:T(8,128)S(1)}, f32[8,384]{1,0:T(8,128)S(1)}, u32[]{:S(2)}, u32[]{:S(2)}) collective-permute-start(f32[8,384]{1,0:T(8,128)S(1)} %get-tuple-element.49), channel_id=1, source_target_pairs={{0,4},{1,7},{2,5},{3,6},{4,0},{5,3},{6,1},{7,2},{8,12},{9,15},{10,... | collective-permute-start | bytes 36872 | tf_op jit(solution)/shard_map/ppermute | solution.py:29
  22.5 0.8 %collective-permute-done.13 = f32[8,384]{1,0:T(8,128)S(1)} collective-permute-done((f32[8,384]{1,0:T(8,128)S(1)}, f32[8,384]{1,0:T(8,128)S(1)}, u32[]{:S(2)}, u32[]{:S(2)}) %collective-permute-start.13) | collective-permute-done | bytes 12320 | tf_op jit(solution)/shard_map/ppermute | solution.py:29
  23.3 0.1 collective-permute-done.14
  23.4 1.0 %collective-permute-done.15 = f32[8,384]{1,0:T(8,128)S(1)} collective-permute-done((f32[8,384]{1,0:T(8,128)S(1)}, f32[8,384]{1,0:T(8,128)S(1)}, u32[]{:S(2)}, u32[]{:S(2)}) %collective-permute-start.15) | collective-permute-done | bytes 12320 | tf_op jit(solution)/shard_map/ppermute | solution.py:29
  24.5 0.7 %shard_map.50 = (f32[8,256]{1,0:T(8,128)}, f32[8,8]{1,0:T(8,128)}) custom-call(f32[8,384]{1,0:T(8,128)S(1)} %fusion.3.both_ref), custom_call_target="tpu_custom_call" | custom-call | tf_op jit(solution)/shard_map/pallas_call | solution.py:214
  (24 shorter events, 0.1 us)
Async XLA Ops:
  0.6 10.1 %copy-start = (bf16[1024,1024]{1,0:T(8,128)(2,1)S(1)}, bf16[1024,1024]{1,0:T(8,128)(2,1)}, u32[]{:S(2)}) copy-start(bf16[1024,1024]{1,0:T(8,128)(2,1)} %param.3) | copy-start | bytes 6291460
  0.6 4.3 %collective-permute-start = (bf16[8,256]{1,0:T(8,128)(2,1)}, bf16[8,256]{1,0:T(8,128)(2,1)S(1)}, u32[]{:S(2)}, u32[]{:S(2)}) collective-permute-start(bf16[8,256]{1,0:T(8,128)(2,1)} %param.5), channel_id=1, source_target_pairs={{0,4},{1,5},{2,6},{3,7},{4,0},{5,1},{6,2},{7,3},{8,12},{9,13},{10,... | collective-permute-start | bytes 12296 | tf_op jit(solution)/shard_map/ppermute | solution.py:29
  1.2 7.3 %collective-permute-start.1 = (bf16[8,256]{1,0:T(8,128)(2,1)}, bf16[8,256]{1,0:T(8,128)(2,1)S(1)}, u32[]{:S(2)}, u32[]{:S(2)}) collective-permute-start(bf16[8,256]{1,0:T(8,128)(2,1)} %param.5), channel_id=1, source_target_pairs={{0,2},{1,3},{2,0},{3,1},{4,6},{5,7},{6,4},{7,5},{8,10},{9,11},{10,... | collective-permute-start | bytes 12296 | tf_op jit(solution)/shard_map/ppermute | solution.py:29
  4.8 3.6 %collective-permute-start.2 = (bf16[8,256]{1,0:T(8,128)(2,1)}, bf16[8,256]{1,0:T(8,128)(2,1)S(1)}, u32[]{:S(2)}, u32[]{:S(2)}) collective-permute-start(bf16[8,256]{1,0:T(8,128)(2,1)} %param.5), channel_id=1, source_target_pairs={{0,4},{1,5},{2,3},{3,2},{4,0},{5,1},{6,7},{7,6},{8,12},{9,13},{10,... | collective-permute-start | bytes 12296 | tf_op jit(solution)/shard_map/ppermute | solution.py:29
  5.0 4.8 %collective-permute-start.3 = (bf16[8,256]{1,0:T(8,128)(2,1)S(1)}, bf16[8,256]{1,0:T(8,128)(2,1)S(1)}, u32[]{:S(2)}, u32[]{:S(2)}) collective-permute-start(bf16[8,256]{1,0:T(8,128)(2,1)S(1)} %collective-permute-done), channel_id=1, source_target_pairs={{0,7},{1,6},{2,5},{3,4},{4,3},{5,2},{6,1},{7,0},{8,15},{9,14},{10,... | collective-permute-start | bytes 12296 | tf_op jit(solution)/shard_map/ppermute | solution.py:29
  6.9 3.0 %collective-permute-start.4 = (bf16[8,256]{1,0:T(8,128)(2,1)S(1)}, bf16[8,256]{1,0:T(8,128)(2,1)S(1)}, u32[]{:S(2)}, u32[]{:S(2)}) collective-permute-start(bf16[8,256]{1,0:T(8,128)(2,1)S(1)} %collective-permute-done), channel_id=1, source_target_pairs={{0,5},{1,4},{2,6},{3,7},{4,1},{5,0},{6,2},{7,3},{8,13},{9,12},{10,... | collective-permute-start | bytes 12296 | tf_op jit(solution)/shard_map/ppermute | solution.py:29
  10.0 1.4 %collective-permute-start.5 = (bf16[8,1024]{1,0:T(8,128)(2,1)S(1)}, bf16[8,1024]{1,0:T(8,128)(2,1)S(1)}, u32[]{:S(2)}, u32[]{:S(2)}) collective-permute-start(bf16[8,1024]{1,0:T(8,128)(2,1)S(1)} %maximum_add_fusion), channel_id=1, source_target_pairs={{0,4},{1,29},{2,26},{3,23},{4,0},{5,1},{6,30},{7,27},{8,12},{9,5},... | collective-permute-start | bytes 49160 | tf_op jit(solution)/shard_map/ppermute | solution.py:29
  11.2 5.3 %collective-permute-start.8 = (f32[8,1024]{1,0:T(8,128)S(1)}, f32[8,1024]{1,0:T(8,128)S(1)}, u32[]{:S(2)}, u32[]{:S(2)}) collective-permute-start(f32[8,1024]{1,0:T(8,128)S(1)} %fusion), channel_id=1, source_target_pairs={{0,4},{1,5},{2,10},{3,15},{4,0},{5,9},{6,14},{7,19},{8,12},{9,13},... | collective-permute-start | bytes 98312 | tf_op jit(solution)/shard_map/ppermute | solution.py:29
  11.5 2.3 %collective-permute-start.6 = (f32[8,8]{1,0:T(8,128)S(1)}, f32[8,8]{1,0:T(8,128)S(1)}, u32[]{:S(2)}, u32[]{:S(2)}) collective-permute-start(f32[8,8]{1,0:T(8,128)S(1)} %fusion.18), channel_id=1, source_target_pairs={{0,4},{1,5},{2,6},{3,7},{4,0},{5,1},{6,2},{7,3},{8,12},{9,13},{10,... | collective-permute-start | bytes 776 | tf_op jit(solution)/shard_map/ppermute | solution.py:29
  11.8 4.7 %collective-permute-start.7 = (f32[8,8]{1,0:T(8,128)S(1)}, f32[8,8]{1,0:T(8,128)S(1)}, u32[]{:S(2)}, u32[]{:S(2)}) collective-permute-start(f32[8,8]{1,0:T(8,128)S(1)} %fusion.18), channel_id=1, source_target_pairs={{0,20},{1,21},{2,22},{3,23},{4,16},{5,17},{6,18},{7,19},{8,12},{9,... | collective-permute-start | bytes 776 | tf_op jit(solution)/shard_map/ppermute | solution.py:29
  13.8 4.0 %collective-permute-start.10 = (f32[8,8]{1,0:T(8,128)S(1)}, f32[8,8]{1,0:T(8,128)S(1)}, u32[]{:S(2)}, u32[]{:S(2)}) collective-permute-start(f32[8,8]{1,0:T(8,128)S(1)} %add.49), channel_id=1, source_target_pairs={{0,12},{1,13},{2,14},{3,15},{4,8},{5,9},{6,10},{7,11},{8,20},{9,21... | collective-permute-start | bytes 776 | tf_op jit(solution)/shard_map/ppermute | solution.py:29
  14.2 3.7 %collective-permute-start.11 = (f32[8,8]{1,0:T(8,128)S(1)}, f32[8,8]{1,0:T(8,128)S(1)}, u32[]{:S(2)}, u32[]{:S(2)}) collective-permute-start(f32[8,8]{1,0:T(8,128)S(1)} %add.49), channel_id=1, source_target_pairs={{0,28},{1,29},{2,30},{3,31},{4,24},{5,25},{6,26},{7,27},{8,4},{9,5... | collective-permute-start | bytes 776 | tf_op jit(solution)/shard_map/ppermute | solution.py:29
  16.5 1.2 %collective-permute-start.9 = (f32[8,8]{1,0:T(8,128)S(1)}, f32[8,8]{1,0:T(8,128)S(1)}, u32[]{:S(2)}, u32[]{:S(2)}) collective-permute-start(f32[8,8]{1,0:T(8,128)S(1)} %broadcast_select_fusion.4), channel_id=1, source_target_pairs={{0,4},{1,5},{2,6},{3,7},{4,0},{5,1},{6,2},{7,3},{8,28},{9,29},{10,... | collective-permute-start | bytes 776 | tf_op jit(solution)/shard_map/ppermute | solution.py:29
  16.9 1.3 %collective-permute-start.12 = (f32[8,1024]{1,0:T(8,128)S(1)}, f32[8,1024]{1,0:T(8,128)S(1)}, u32[]{:S(2)}, u32[]{:S(2)}) collective-permute-start(f32[8,1024]{1,0:T(8,128)S(1)} %select_add_fusion), channel_id=1, source_target_pairs={{0,4},{1,5},{2,6},{3,7},{4,0},{5,1},{6,2},{7,3},{8,12},{9,13},{10,... | collective-permute-start | bytes 98312 | tf_op jit(solution)/shard_map/ppermute | solution.py:29
  18.2 5.1 %collective-permute-start.13 = (f32[8,384]{1,0:T(8,128)S(1)}, f32[8,384]{1,0:T(8,128)S(1)}, u32[]{:S(2)}, u32[]{:S(2)}) collective-permute-start(f32[8,384]{1,0:T(8,128)S(1)} %get-tuple-element.50), channel_id=1, source_target_pairs={{0,6},{1,5},{2,7},{3,4},{4,2},{5,1},{6,3},{7,0},{8,14},{9,13},{10,... | collective-permute-start | bytes 36872 | tf_op jit(solution)/shard_map/ppermute | solution.py:29
  20.3 3.1 %collective-permute-start.14 = (f32[8,384]{1,0:T(8,128)S(1)}, f32[8,384]{1,0:T(8,128)S(1)}, u32[]{:S(2)}, u32[]{:S(2)}) collective-permute-start(f32[8,384]{1,0:T(8,128)S(1)} %get-tuple-element.51), channel_id=1, source_target_pairs={{0,5},{1,4},{2,6},{3,7},{4,1},{5,0},{6,2},{7,3},{8,13},{9,12},{10,... | collective-permute-start | bytes 36872 | tf_op jit(solution)/shard_map/ppermute | solution.py:29
  20.4 4.0 %collective-permute-start.15 = (f32[8,384]{1,0:T(8,128)S(1)}, f32[8,384]{1,0:T(8,128)S(1)}, u32[]{:S(2)}, u32[]{:S(2)}) collective-permute-start(f32[8,384]{1,0:T(8,128)S(1)} %get-tuple-element.52), channel_id=1, source_target_pairs={{0,7},{1,6},{2,4},{3,5},{4,3},{5,2},{6,0},{7,1},{8,15},{9,14},{10,... | collective-permute-start | bytes 36872 | tf_op jit(solution)/shard_map/ppermute | solution.py:29
  22.2 2.3 %collective-permute-start.16 = (f32[8,384]{1,0:T(8,128)S(1)}, f32[8,384]{1,0:T(8,128)S(1)}, u32[]{:S(2)}, u32[]{:S(2)}) collective-permute-start(f32[8,384]{1,0:T(8,128)S(1)} %get-tuple-element.49), channel_id=1, source_target_pairs={{0,4},{1,7},{2,5},{3,6},{4,0},{5,3},{6,1},{7,2},{8,12},{9,15},{10,... | collective-permute-start | bytes 36872 | tf_op jit(solution)/shard_map/ppermute | solution.py:29

commit v9 on v8

--- a/solution.py
+++ b/solution.py
@@ -93,10 +93,12 @@
     return blocks[0]
 
 
-def write_results(scale, both_ref, product_ref, projected_ref):
+def write_results(scale, *refs):
+    product_ref, projected_ref = refs[-2:]
+    both = tree_sum([ref[...] for ref in refs[:-2]])
     vectors = projected_ref.shape[0]
-    product_ref[...] = both_ref[:, :-SUB]
-    gram = both_ref[:, -SUB:]
+    product_ref[...] = both[:, :-SUB]
+    gram = both[:, -SUB:]
     square = jnp.concatenate([gram, jnp.zeros((SUB - vectors, SUB), jnp.float32)])
     gram = gram + square.T[:vectors]
     projected_ref[...] = (gram * scale)[:, :vectors]
@@ -207,7 +209,10 @@
         ]
         own = message(place, own_pieces, mate_pieces)
         got = held(exchanged(given, bit, tables, "cross"), SUM_ORDER)
-        both = tree_sum(in_place(own, got, tables, place))
+        terms = in_place(own, got, tables, place)
+        if not bit:
+            break
+        both = tree_sum(terms)
         piece = own_pieces[0].shape[1]
         sums, mate, gram = both[:, :piece], both[:, piece:-SUB], both[:, -SUB:]
 
@@ -217,10 +222,10 @@
             jax.ShapeDtypeStruct(lanczos_block.shape, jnp.float32),
             jax.ShapeDtypeStruct((vectors, vectors), jnp.float32),
         ),
-        in_specs=[pl.BlockSpec(memory_space=pltpu.VMEM)],
+        in_specs=[pl.BlockSpec(memory_space=pltpu.VMEM)] * len(terms),
         out_specs=(pl.BlockSpec(memory_space=pltpu.VMEM),) * 2,
         compiler_params=pltpu.CompilerParams(vmem_limit_bytes=1 << 20),
-    )(both)
+    )(*terms)
 
 
 def solution(mesh):

time: 25.4 us -> 25.4 us (level)
  no operation moved by 1% of the time
where the time goes in v9:
time: 25.4 us; the launch traced here: 25.1 us
  starting transfers between devices  16.2 us (64%)
  waiting for transfers between devices  4.49 us (18%)
  other arithmetic  1.47 us (6%)
  matrix products  1.23 us (5%)
  between operations  0.71 us (3%)
  Pallas kernels  0.67 us (3%)
  local copies, waits for them, and re-layouts  0.34 us (1%)
    ppermute x17, starting transfers between devices, send(): return lax.ppermute(block, AXES, pairs)  16.2 us
    ppermute x17, waiting for transfers between devices, send(): return lax.ppermute(block, AXES, pairs)  4.49 us
    select_n x1, other arithmetic, on_device(): jnp.where(place == at, source, zero)  0.69 us
    convert_element_type x1, other arithmetic, on_device(): keep = block_map[0, 0].astype(jnp.bfloat16)  0.69 us
    pallas_call x1, Pallas kernels, on_device(): pl.pallas_call(functools.partial(write_results, 1.0 / (width * rows) ** 0...  0.67 us
    dot_general x1, matrix products, on_device(): lax.dot_general(far_vec, matrix, (((1,), (1,)), ((), ())), preferred_elem...  0.65 us
  transfers between devices with their start and end apart: 17, of which 7 were waited for; matrix products, arithmetic and copies ran while one was open for 12% of the time, Pallas kernels for 0%

profile of v9, /device:TPU:0, one launch (start us, length us, event | category | flops | bytes accessed | tf_op | source)
XLA Modules:
  0.0 25.1 jit_solution(3055895371740525993)
XLA Ops:
  0.6 0.5 %collective-permute-start = (bf16[8,256]{1,0:T(8,128)(2,1)}, bf16[8,256]{1,0:T(8,128)(2,1)S(1)}, u32[]{:S(2)}, u32[]{:S(2)}) collective-permute-start(bf16[8,256]{1,0:T(8,128)(2,1)} %param.5), channel_id=1, source_target_pairs={{0,4},{1,5},{2,6},{3,7},{4,0},{5,1},{6,2},{7,3},{8,12},{9,13},{10,... | collective-permute-start | bytes 12296 | tf_op jit(solution)/shard_map/ppermute | solution.py:29
  1.2 3.7 %collective-permute-start.1 = (bf16[8,256]{1,0:T(8,128)(2,1)}, bf16[8,256]{1,0:T(8,128)(2,1)S(1)}, u32[]{:S(2)}, u32[]{:S(2)}) collective-permute-start(bf16[8,256]{1,0:T(8,128)(2,1)} %param.5), channel_id=1, source_target_pairs={{0,2},{1,3},{2,0},{3,1},{4,6},{5,7},{6,4},{7,5},{8,10},{9,11},{10,... | collective-permute-start | bytes 12296 | tf_op jit(solution)/shard_map/ppermute | solution.py:29
  4.8 0.2 collective-permute-start.2
  5.0 1.9 %collective-permute-start.3 = (bf16[8,256]{1,0:T(8,128)(2,1)S(1)}, bf16[8,256]{1,0:T(8,128)(2,1)S(1)}, u32[]{:S(2)}, u32[]{:S(2)}) collective-permute-start(bf16[8,256]{1,0:T(8,128)(2,1)S(1)} %collective-permute-done), channel_id=1, source_target_pairs={{0,7},{1,6},{2,5},{3,4},{4,3},{5,2},{6,1},{7,0},{8,15},{9,14},{10,... | collective-permute-start | bytes 12296 | tf_op jit(solution)/shard_map/ppermute | solution.py:29
  6.9 0.1 collective-permute-start.4
  7.0 0.7 %convert_bitcast_fusion = bf16[8,8]{1,0:T(8,128)(2,1)S(1)} fusion(s32[1,1,8,8]{3,2,1,0:T(8,128)} %param.4), kind=kLoop, calls=%fused_computation.43 | loop fusion | flops 64 | bytes 384 | tf_op jit(solution)/shard_map/convert_element_type | solution.py:143
  7.7 0.7 %broadcast_select_fusion.3 = (bf16[8,256]{1,0:T(8,128)(2,1)S(1)}, bf16[8,256]{1,0:T(8,128)(2,1)S(1)}, bf16[8,256]{1,0:T(8,128)(2,1)S(1)}, bf16[8,256]{1,0:T(8,128)(2,1)S(1)}) fusion(bf16[8,256]{1,0:T(8,128)(2,1)} %param.5, pred[]{:T(512)S(6)} %eq.23, pred[]{:T(512)S(6)} %eq.27, pred[]{:T(512)S(6)} %eq.26, pred[]{:T(512)S(6)} %eq.25), kind=kLoop, calls=%fused_computation.41 | loop fusion | flops 8192 | bytes 20484 | tf_op jit(solution)/shard_map/jit(_where)/select_n | solution.py:130
  8.4 1.4 %collective-permute-done.3 = bf16[8,256]{1,0:T(8,128)(2,1)S(1)} collective-permute-done((bf16[8,256]{1,0:T(8,128)(2,1)S(1)}, bf16[8,256]{1,0:T(8,128)(2,1)S(1)}, u32[]{:S(2)}, u32[]{:S(2)}) %collective-permute-start.3) | collective-permute-done | bytes 4128 | tf_op jit(solution)/shard_map/ppermute | solution.py:29
  9.8 0.1 collective-permute-done.4
  10.0 0.4 %collective-permute-start.5 = (bf16[8,1024]{1,0:T(8,128)(2,1)S(1)}, bf16[8,1024]{1,0:T(8,128)(2,1)S(1)}, u32[]{:S(2)}, u32[]{:S(2)}) collective-permute-start(bf16[8,1024]{1,0:T(8,128)(2,1)S(1)} %maximum_add_fusion), channel_id=1, source_target_pairs={{0,4},{1,29},{2,26},{3,23},{4,0},{5,1},{6,30},{7,27},{8,12},{9,5},... | collective-permute-start | bytes 49160 | tf_op jit(solution)/shard_map/ppermute | solution.py:29
  10.4 0.3 %mul.11 = bf16[8,128,8,128]{3,2,1,0:T(8,128)(2,1)S(1)} broadcast(bf16[8,8]{1,0:T(8,128)(2,1)S(1)} %convert_bitcast_fusion), dimensions={0,2} | broadcast | bytes 2097280 | tf_op jit(solution)/shard_map/mul | solution.py:144
  10.7 0.5 %fusion = f32[8,1024]{1,0:T(8,128)S(1)} fusion(bf16[8,1024]{1,0:T(8,128)(2,1)S(1)} %maximum_add_fusion, bf16[1024,1024]{1,0:T(8,128)(2,1)S(1)} %copy-done, bf16[128,8,8,128]{3,2,1,0:T(8,128)(2,1)S(1)} %bitcast.10), kind=kOutput, calls=%fused_computation.1 | convolution fusion | flops 17825792 | bytes 4243456 | tf_op jit(solution)/shard_map/dot_general | solution.py:149
  11.2 0.2 collective-permute-start.8
  11.3 0.1 fusion.15
  11.5 0.4 %collective-permute-start.6 = (f32[8,8]{1,0:T(8,128)S(1)}, f32[8,8]{1,0:T(8,128)S(1)}, u32[]{:S(2)}, u32[]{:S(2)}) collective-permute-start(f32[8,8]{1,0:T(8,128)S(1)} %fusion.15), channel_id=1, source_target_pairs={{0,4},{1,5},{2,6},{3,7},{4,0},{5,1},{6,2},{7,3},{8,12},{9,13},{10,... | collective-permute-start | bytes 776 | tf_op jit(solution)/shard_map/ppermute | solution.py:29
  11.8 1.3 %collective-permute-start.7 = (f32[8,8]{1,0:T(8,128)S(1)}, f32[8,8]{1,0:T(8,128)S(1)}, u32[]{:S(2)}, u32[]{:S(2)}) collective-permute-start(f32[8,8]{1,0:T(8,128)S(1)} %fusion.15), channel_id=1, source_target_pairs={{0,20},{1,21},{2,22},{3,23},{4,16},{5,17},{6,18},{7,19},{8,12},{9,... | collective-permute-start | bytes 776 | tf_op jit(solution)/shard_map/ppermute | solution.py:29
  13.1 0.7 %fusion.1 = f32[8,1024]{1,0:T(8,128)S(1)} fusion(bf16[1024,1024]{1,0:T(8,128)(2,1)S(1)} %copy-done, bf16[128,8,8,128]{3,2,1,0:T(8,128)(2,1)S(1)} %bitcast.11, bf16[8,1024]{1,0:T(8,128)(2,1)S(1)} %maximum_add_fusion, bf16[8,1024]{1,0:T(8,128)(2,1)S(1)} %collective-permute-done.5, pred[]{:T(512)S(6)} %lt.20, pred[]{:T(512)S(6)} %eq.24), kind=kOutput, calls=%fused_computation.2 | convolution fusion | flops 17842176 | bytes 4259842 | tf_op jit(solution)/shard_map/dot_general | solution.py:159
  13.8 0.4 %collective-permute-start.10 = (f32[8,8]{1,0:T(8,128)S(1)}, f32[8,8]{1,0:T(8,128)S(1)}, u32[]{:S(2)}, u32[]{:S(2)}) collective-permute-start(f32[8,8]{1,0:T(8,128)S(1)} %add.40), channel_id=1, source_target_pairs={{0,12},{1,13},{2,14},{3,15},{4,8},{5,9},{6,10},{7,11},{8,20},{9,21... | collective-permute-start | bytes 776 | tf_op jit(solution)/shard_map/ppermute | solution.py:29
  14.2 2.3 %collective-permute-start.11 = (f32[8,8]{1,0:T(8,128)S(1)}, f32[8,8]{1,0:T(8,128)S(1)}, u32[]{:S(2)}, u32[]{:S(2)}) collective-permute-start(f32[8,8]{1,0:T(8,128)S(1)} %add.40), channel_id=1, source_target_pairs={{0,28},{1,29},{2,30},{3,31},{4,24},{5,25},{6,26},{7,27},{8,4},{9,5... | collective-permute-start | bytes 776 | tf_op jit(solution)/shard_map/ppermute | solution.py:29
  16.5 0.4 %collective-permute-start.9 = (f32[8,8]{1,0:T(8,128)S(1)}, f32[8,8]{1,0:T(8,128)S(1)}, u32[]{:S(2)}, u32[]{:S(2)}) collective-permute-start(f32[8,8]{1,0:T(8,128)S(1)} %broadcast_select_fusion.4), channel_id=1, source_target_pairs={{0,4},{1,5},{2,6},{3,7},{4,0},{5,1},{6,2},{7,3},{8,28},{9,29},{10,... | collective-permute-start | bytes 776 | tf_op jit(solution)/shard_map/ppermute | solution.py:29
  16.9 0.2 collective-permute-start.12
  17.2 0.6 %collective-permute-done.9 = f32[8,8]{1,0:T(8,128)S(1)} collective-permute-done((f32[8,8]{1,0:T(8,128)S(1)}, f32[8,8]{1,0:T(8,128)S(1)}, u32[]{:S(2)}, u32[]{:S(2)}) %collective-permute-start.9) | collective-permute-done | bytes 288 | tf_op jit(solution)/shard_map/ppermute | solution.py:29
  17.8 0.0 collective-permute-done.11
  17.8 0.4 %collective-permute-done.12 = f32[8,1024]{1,0:T(8,128)S(1)} collective-permute-done((f32[8,1024]{1,0:T(8,128)S(1)}, f32[8,1024]{1,0:T(8,128)S(1)}, u32[]{:S(2)}, u32[]{:S(2)}) %collective-permute-start.12) | collective-permute-done | bytes 32800 | tf_op jit(solution)/shard_map/ppermute | solution.py:29
  18.2 2.1 %collective-permute-start.13 = (f32[8,384]{1,0:T(8,128)S(1)}, f32[8,384]{1,0:T(8,128)S(1)}, u32[]{:S(2)}, u32[]{:S(2)}) collective-permute-start(f32[8,384]{1,0:T(8,128)S(1)} %get-tuple-element.54), channel_id=1, source_target_pairs={{0,6},{1,5},{2,7},{3,4},{4,2},{5,1},{6,3},{7,0},{8,14},{9,13},{10,... | collective-permute-start | bytes 36872 | tf_op jit(solution)/shard_map/ppermute | solution.py:29
  20.3 0.1 collective-permute-start.14
  20.4 1.7 %collective-permute-start.15 = (f32[8,384]{1,0:T(8,128)S(1)}, f32[8,384]{1,0:T(8,128)S(1)}, u32[]{:S(2)}, u32[]{:S(2)}) collective-permute-start(f32[8,384]{1,0:T(8,128)S(1)} %get-tuple-element.56), channel_id=1, source_target_pairs={{0,7},{1,6},{2,4},{3,5},{4,3},{5,2},{6,0},{7,1},{8,15},{9,14},{10,... | collective-permute-start | bytes 36872 | tf_op jit(solution)/shard_map/ppermute | solution.py:29
  22.2 0.3 %collective-permute-start.16 = (f32[8,384]{1,0:T(8,128)S(1)}, f32[8,384]{1,0:T(8,128)S(1)}, u32[]{:S(2)}, u32[]{:S(2)}) collective-permute-start(f32[8,384]{1,0:T(8,128)S(1)} %get-tuple-element.52), channel_id=1, source_target_pairs={{0,4},{1,7},{2,5},{3,6},{4,0},{5,3},{6,1},{7,2},{8,12},{9,15},{10,... | collective-permute-start | bytes 36872 | tf_op jit(solution)/shard_map/ppermute | solution.py:29
  22.5 0.8 %collective-permute-done.13 = f32[8,384]{1,0:T(8,128)S(1)} collective-permute-done((f32[8,384]{1,0:T(8,128)S(1)}, f32[8,384]{1,0:T(8,128)S(1)}, u32[]{:S(2)}, u32[]{:S(2)}) %collective-permute-start.13) | collective-permute-done | bytes 12320 | tf_op jit(solution)/shard_map/ppermute | solution.py:29
  23.3 0.1 collective-permute-done.14
  23.4 1.0 %collective-permute-done.15 = f32[8,384]{1,0:T(8,128)S(1)} collective-permute-done((f32[8,384]{1,0:T(8,128)S(1)}, f32[8,384]{1,0:T(8,128)S(1)}, u32[]{:S(2)}, u32[]{:S(2)}) %collective-permute-start.15) | collective-permute-done | bytes 12320 | tf_op jit(solution)/shard_map/ppermute | solution.py:29
  24.5 0.7 %shard_map.50 = (f32[8,256]{1,0:T(8,128)}, f32[8,8]{1,0:T(8,128)}) custom-call(f32[8,384]{1,0:T(8,128)S(1)} %get-tuple-element.53.refs_0_, f32[8,384]{1,0:T(8,128)S(1)} %get-tuple-element.48.refs_1_, f32[8,384]{1,0:T(8,128)S(1)} %get-tuple-element.43.refs_2_, f32[8,384]{1,0:T(8,128)S(1)} %get-tuple-element.42.refs_3_), custom_call_target="tpu_custom_call" | custom-call | tf_op jit(solution)/shard_map/pallas_call | solution.py:219
  (24 shorter events, 0.1 us)
Async XLA Ops:
  0.6 10.1 %copy-start = (bf16[1024,1024]{1,0:T(8,128)(2,1)S(1)}, bf16[1024,1024]{1,0:T(8,128)(2,1)}, u32[]{:S(2)}) copy-start(bf16[1024,1024]{1,0:T(8,128)(2,1)} %param.3) | copy-start | bytes 6291460
  0.6 4.3 %collective-permute-start = (bf16[8,256]{1,0:T(8,128)(2,1)}, bf16[8,256]{1,0:T(8,128)(2,1)S(1)}, u32[]{:S(2)}, u32[]{:S(2)}) collective-permute-start(bf16[8,256]{1,0:T(8,128)(2,1)} %param.5), channel_id=1, source_target_pairs={{0,4},{1,5},{2,6},{3,7},{4,0},{5,1},{6,2},{7,3},{8,12},{9,13},{10,... | collective-permute-start | bytes 12296 | tf_op jit(solution)/shard_map/ppermute | solution.py:29
  1.2 7.3 %collective-permute-start.1 = (bf16[8,256]{1,0:T(8,128)(2,1)}, bf16[8,256]{1,0:T(8,128)(2,1)S(1)}, u32[]{:S(2)}, u32[]{:S(2)}) collective-permute-start(bf16[8,256]{1,0:T(8,128)(2,1)} %param.5), channel_id=1, source_target_pairs={{0,2},{1,3},{2,0},{3,1},{4,6},{5,7},{6,4},{7,5},{8,10},{9,11},{10,... | collective-permute-start | bytes 12296 | tf_op jit(solution)/shard_map/ppermute | solution.py:29
  4.8 3.6 %collective-permute-start.2 = (bf16[8,256]{1,0:T(8,128)(2,1)}, bf16[8,256]{1,0:T(8,128)(2,1)S(1)}, u32[]{:S(2)}, u32[]{:S(2)}) collective-permute-start(bf16[8,256]{1,0:T(8,128)(2,1)} %param.5), channel_id=1, source_target_pairs={{0,4},{1,5},{2,3},{3,2},{4,0},{5,1},{6,7},{7,6},{8,12},{9,13},{10,... | collective-permute-start | bytes 12296 | tf_op jit(solution)/shard_map/ppermute | solution.py:29
  5.0 4.8 %collective-permute-start.3 = (bf16[8,256]{1,0:T(8,128)(2,1)S(1)}, bf16[8,256]{1,0:T(8,128)(2,1)S(1)}, u32[]{:S(2)}, u32[]{:S(2)}) collective-permute-start(bf16[8,256]{1,0:T(8,128)(2,1)S(1)} %collective-permute-done), channel_id=1, source_target_pairs={{0,7},{1,6},{2,5},{3,4},{4,3},{5,2},{6,1},{7,0},{8,15},{9,14},{10,... | collective-permute-start | bytes 12296 | tf_op jit(solution)/shard_map/ppermute | solution.py:29
  6.9 3.0 %collective-permute-start.4 = (bf16[8,256]{1,0:T(8,128)(2,1)S(1)}, bf16[8,256]{1,0:T(8,128)(2,1)S(1)}, u32[]{:S(2)}, u32[]{:S(2)}) collective-permute-start(bf16[8,256]{1,0:T(8,128)(2,1)S(1)} %collective-permute-done), channel_id=1, source_target_pairs={{0,5},{1,4},{2,6},{3,7},{4,1},{5,0},{6,2},{7,3},{8,13},{9,12},{10,... | collective-permute-start | bytes 12296 | tf_op jit(solution)/shard_map/ppermute | solution.py:29
  10.0 1.4 %collective-permute-start.5 = (bf16[8,1024]{1,0:T(8,128)(2,1)S(1)}, bf16[8,1024]{1,0:T(8,128)(2,1)S(1)}, u32[]{:S(2)}, u32[]{:S(2)}) collective-permute-start(bf16[8,1024]{1,0:T(8,128)(2,1)S(1)} %maximum_add_fusion), channel_id=1, source_target_pairs={{0,4},{1,29},{2,26},{3,23},{4,0},{5,1},{6,30},{7,27},{8,12},{9,5},... | collective-permute-start | bytes 49160 | tf_op jit(solution)/shard_map/ppermute | solution.py:29
  11.2 5.3 %collective-permute-start.8 = (f32[8,1024]{1,0:T(8,128)S(1)}, f32[8,1024]{1,0:T(8,128)S(1)}, u32[]{:S(2)}, u32[]{:S(2)}) collective-permute-start(f32[8,1024]{1,0:T(8,128)S(1)} %fusion), channel_id=1, source_target_pairs={{0,4},{1,5},{2,10},{3,15},{4,0},{5,9},{6,14},{7,19},{8,12},{9,13},... | collective-permute-start | bytes 98312 | tf_op jit(solution)/shard_map/ppermute | solution.py:29
  11.5 2.3 %collective-permute-start.6 = (f32[8,8]{1,0:T(8,128)S(1)}, f32[8,8]{1,0:T(8,128)S(1)}, u32[]{:S(2)}, u32[]{:S(2)}) collective-permute-start(f32[8,8]{1,0:T(8,128)S(1)} %fusion.15), channel_id=1, source_target_pairs={{0,4},{1,5},{2,6},{3,7},{4,0},{5,1},{6,2},{7,3},{8,12},{9,13},{10,... | collective-permute-start | bytes 776 | tf_op jit(solution)/shard_map/ppermute | solution.py:29
  11.8 4.7 %collective-permute-start.7 = (f32[8,8]{1,0:T(8,128)S(1)}, f32[8,8]{1,0:T(8,128)S(1)}, u32[]{:S(2)}, u32[]{:S(2)}) collective-permute-start(f32[8,8]{1,0:T(8,128)S(1)} %fusion.15), channel_id=1, source_target_pairs={{0,20},{1,21},{2,22},{3,23},{4,16},{5,17},{6,18},{7,19},{8,12},{9,... | collective-permute-start | bytes 776 | tf_op jit(solution)/shard_map/ppermute | solution.py:29
  13.8 4.0 %collective-permute-start.10 = (f32[8,8]{1,0:T(8,128)S(1)}, f32[8,8]{1,0:T(8,128)S(1)}, u32[]{:S(2)}, u32[]{:S(2)}) collective-permute-start(f32[8,8]{1,0:T(8,128)S(1)} %add.40), channel_id=1, source_target_pairs={{0,12},{1,13},{2,14},{3,15},{4,8},{5,9},{6,10},{7,11},{8,20},{9,21... | collective-permute-start | bytes 776 | tf_op jit(solution)/shard_map/ppermute | solution.py:29
  14.2 3.7 %collective-permute-start.11 = (f32[8,8]{1,0:T(8,128)S(1)}, f32[8,8]{1,0:T(8,128)S(1)}, u32[]{:S(2)}, u32[]{:S(2)}) collective-permute-start(f32[8,8]{1,0:T(8,128)S(1)} %add.40), channel_id=1, source_target_pairs={{0,28},{1,29},{2,30},{3,31},{4,24},{5,25},{6,26},{7,27},{8,4},{9,5... | collective-permute-start | bytes 776 | tf_op jit(solution)/shard_map/ppermute | solution.py:29
  16.5 1.2 %collective-permute-start.9 = (f32[8,8]{1,0:T(8,128)S(1)}, f32[8,8]{1,0:T(8,128)S(1)}, u32[]{:S(2)}, u32[]{:S(2)}) collective-permute-start(f32[8,8]{1,0:T(8,128)S(1)} %broadcast_select_fusion.4), channel_id=1, source_target_pairs={{0,4},{1,5},{2,6},{3,7},{4,0},{5,1},{6,2},{7,3},{8,28},{9,29},{10,... | collective-permute-start | bytes 776 | tf_op jit(solution)/shard_map/ppermute | solution.py:29
  16.9 1.3 %collective-permute-start.12 = (f32[8,1024]{1,0:T(8,128)S(1)}, f32[8,1024]{1,0:T(8,128)S(1)}, u32[]{:S(2)}, u32[]{:S(2)}) collective-permute-start(f32[8,1024]{1,0:T(8,128)S(1)} %select_add_fusion), channel_id=1, source_target_pairs={{0,4},{1,5},{2,6},{3,7},{4,0},{5,1},{6,2},{7,3},{8,12},{9,13},{10,... | collective-permute-start | bytes 98312 | tf_op jit(solution)/shard_map/ppermute | solution.py:29
  18.2 5.1 %collective-permute-start.13 = (f32[8,384]{1,0:T(8,128)S(1)}, f32[8,384]{1,0:T(8,128)S(1)}, u32[]{:S(2)}, u32[]{:S(2)}) collective-permute-start(f32[8,384]{1,0:T(8,128)S(1)} %get-tuple-element.54), channel_id=1, source_target_pairs={{0,6},{1,5},{2,7},{3,4},{4,2},{5,1},{6,3},{7,0},{8,14},{9,13},{10,... | collective-permute-start | bytes 36872 | tf_op jit(solution)/shard_map/ppermute | solution.py:29
  20.3 3.1 %collective-permute-start.14 = (f32[8,384]{1,0:T(8,128)S(1)}, f32[8,384]{1,0:T(8,128)S(1)}, u32[]{:S(2)}, u32[]{:S(2)}) collective-permute-start(f32[8,384]{1,0:T(8,128)S(1)} %get-tuple-element.55), channel_id=1, source_target_pairs={{0,5},{1,4},{2,6},{3,7},{4,1},{5,0},{6,2},{7,3},{8,13},{9,12},{10,... | collective-permute-start | bytes 36872 | tf_op jit(solution)/shard_map/ppermute | solution.py:29
  20.4 4.0 %collective-permute-start.15 = (f32[8,384]{1,0:T(8,128)S(1)}, f32[8,384]{1,0:T(8,128)S(1)}, u32[]{:S(2)}, u32[]{:S(2)}) collective-permute-start(f32[8,384]{1,0:T(8,128)S(1)} %get-tuple-element.56), channel_id=1, source_target_pairs={{0,7},{1,6},{2,4},{3,5},{4,3},{5,2},{6,0},{7,1},{8,15},{9,14},{10,... | collective-permute-start | bytes 36872 | tf_op jit(solution)/shard_map/ppermute | solution.py:29
  22.2 2.3 %collective-permute-start.16 = (f32[8,384]{1,0:T(8,128)S(1)}, f32[8,384]{1,0:T(8,128)S(1)}, u32[]{:S(2)}, u32[]{:S(2)}) collective-permute-start(f32[8,384]{1,0:T(8,128)S(1)} %get-tuple-element.52), channel_id=1, source_target_pairs={{0,4},{1,7},{2,5},{3,6},{4,0},{5,3},{6,1},{7,2},{8,12},{9,15},{10,... | collective-permute-start | bytes 36872 | tf_op jit(solution)/shard_map/ppermute | solution.py:29

commit v10 on v9

--- a/solution.py
+++ b/solution.py
@@ -16,6 +16,7 @@
 GATHER_CROSS = (0, 0, 1, 1)
 GATHER_ORDER = (0, 1, 2, 3)
 SUM_TABLES = ((2, 1, 3, 0), (1, 0, 2, 3), (3, 2, 0, 1), (0, 3, 1, 2))
+SUM_CROSS = (1, 0, 1, 1)
 SUM_ORDER = (0, 1, 2, 3)
 
 
@@ -38,7 +39,13 @@
     if axis == "row":
         goes = [lambda r, c, t=t: (moved(r, bit, t) ^ 1, c) for t in tables]
     elif axis == "cross":
-        goes = [lambda r, c, t=t: (r ^ 1, moved(c, bit, t)) for t in tables]
+        goes = [
+            lambda r, c, t=t, x=x: (
+                r ^ (x or moved(c, bit, t) == c),
+                moved(c, bit, t),
+            )
+            for t, x in zip(tables, SUM_CROSS)
+        ]
     else:
         goes = [
             lambda r, c, t=t, x=x: (
@@ -199,14 +206,13 @@
             blocks = [choose(to, first), choose(to, second), gram]
             return jnp.concatenate(blocks if bit else [blocks[0], gram], axis=1)
 
-        given = [
-            message(
-                place,
-                [mate_pieces[to] for to in table],
-                [own_pieces[to] for to in table],
-            )
-            for table in tables
-        ]
+        given = []
+        for table, cross in zip(tables, SUM_CROSS):
+            own_rows = [own_pieces[to] for to in table]
+            mate_rows = [mate_pieces[to] for to in table]
+            if cross:
+                own_rows, mate_rows = mate_rows, own_rows
+            given.append(message(place, own_rows, mate_rows))
         own = message(place, own_pieces, mate_pieces)
         got = held(exchanged(given, bit, tables, "cross"), SUM_ORDER)
         terms = in_place(own, got, tables, place)

time: 25.4 us -> 25.4 us (level)
  no operation moved by 1% of the time
where the time goes in v10:
time: 25.4 us; the launch traced here: 25.2 us
  starting transfers between devices  16.2 us (64%)
  waiting for transfers between devices  4.53 us (18%)
  other arithmetic  1.47 us (6%)
  matrix products  1.23 us (5%)
  between operations  0.71 us (3%)
  Pallas kernels  0.67 us (3%)
  local copies, waits for them, and re-layouts  0.34 us (1%)
    ppermute x17, starting transfers between devices, send(): return lax.ppermute(block, AXES, pairs)  16.2 us
    ppermute x17, waiting for transfers between devices, send(): return lax.ppermute(block, AXES, pairs)  4.53 us
    select_n x1, other arithmetic, on_device(): jnp.where(place == at, source, zero)  0.69 us
    convert_element_type x1, other arithmetic, on_device(): keep = block_map[0, 0].astype(jnp.bfloat16)  0.69 us
    pallas_call x1, Pallas kernels, on_device(): pl.pallas_call(functools.partial(write_results, 1.0 / (width * rows) ** 0...  0.67 us
    dot_general x1, matrix products, on_device(): lax.dot_general(far_vec, matrix, (((1,), (1,)), ((), ())), preferred_elem...  0.65 us
  transfers between devices with their start and end apart: 17, of which 7 were waited for; matrix products, arithmetic and copies ran while one was open for 12% of the time, Pallas kernels for 0%

profile of v10, /device:TPU:0, one launch (start us, length us, event | category | flops | bytes accessed | tf_op | source)
XLA Modules:
  0.0 25.2 jit_solution(5303308631194224718)
XLA Ops:
  0.6 0.5 %collective-permute-start = (bf16[8,256]{1,0:T(8,128)(2,1)}, bf16[8,256]{1,0:T(8,128)(2,1)S(1)}, u32[]{:S(2)}, u32[]{:S(2)}) collective-permute-start(bf16[8,256]{1,0:T(8,128)(2,1)} %param.5), channel_id=1, source_target_pairs={{0,4},{1,5},{2,6},{3,7},{4,0},{5,1},{6,2},{7,3},{8,12},{9,13},{10,... | collective-permute-start | bytes 12296 | tf_op jit(solution)/shard_map/ppermute | solution.py:30
  1.2 3.7 %collective-permute-start.1 = (bf16[8,256]{1,0:T(8,128)(2,1)}, bf16[8,256]{1,0:T(8,128)(2,1)S(1)}, u32[]{:S(2)}, u32[]{:S(2)}) collective-permute-start(bf16[8,256]{1,0:T(8,128)(2,1)} %param.5), channel_id=1, source_target_pairs={{0,2},{1,3},{2,0},{3,1},{4,6},{5,7},{6,4},{7,5},{8,10},{9,11},{10,... | collective-permute-start | bytes 12296 | tf_op jit(solution)/shard_map/ppermute | solution.py:30
  4.8 0.2 collective-permute-start.2
  5.0 1.9 %collective-permute-start.3 = (bf16[8,256]{1,0:T(8,128)(2,1)S(1)}, bf16[8,256]{1,0:T(8,128)(2,1)S(1)}, u32[]{:S(2)}, u32[]{:S(2)}) collective-permute-start(bf16[8,256]{1,0:T(8,128)(2,1)S(1)} %collective-permute-done), channel_id=1, source_target_pairs={{0,7},{1,6},{2,5},{3,4},{4,3},{5,2},{6,1},{7,0},{8,15},{9,14},{10,... | collective-permute-start | bytes 12296 | tf_op jit(solution)/shard_map/ppermute | solution.py:30
  6.9 0.1 collective-permute-start.4
  7.0 0.7 %convert_bitcast_fusion = bf16[8,8]{1,0:T(8,128)(2,1)S(1)} fusion(s32[1,1,8,8]{3,2,1,0:T(8,128)} %param.4), kind=kLoop, calls=%fused_computation.42 | loop fusion | flops 64 | bytes 384 | tf_op jit(solution)/shard_map/convert_element_type | solution.py:150
  7.7 0.7 %broadcast_select_fusion.3 = (bf16[8,256]{1,0:T(8,128)(2,1)S(1)}, bf16[8,256]{1,0:T(8,128)(2,1)S(1)}, bf16[8,256]{1,0:T(8,128)(2,1)S(1)}, bf16[8,256]{1,0:T(8,128)(2,1)S(1)}) fusion(bf16[8,256]{1,0:T(8,128)(2,1)} %param.5, pred[]{:T(512)S(6)} %eq.23, pred[]{:T(512)S(6)} %eq.27, pred[]{:T(512)S(6)} %eq.26, pred[]{:T(512)S(6)} %eq.25), kind=kLoop, calls=%fused_computation.40 | loop fusion | flops 8192 | bytes 20484 | tf_op jit(solution)/shard_map/jit(_where)/select_n | solution.py:137
  8.4 1.4 %collective-permute-done.3 = bf16[8,256]{1,0:T(8,128)(2,1)S(1)} collective-permute-done((bf16[8,256]{1,0:T(8,128)(2,1)S(1)}, bf16[8,256]{1,0:T(8,128)(2,1)S(1)}, u32[]{:S(2)}, u32[]{:S(2)}) %collective-permute-start.3) | collective-permute-done | bytes 4128 | tf_op jit(solution)/shard_map/ppermute | solution.py:30
  9.8 0.1 collective-permute-done.4
  10.0 0.4 %collective-permute-start.5 = (bf16[8,1024]{1,0:T(8,128)(2,1)S(1)}, bf16[8,1024]{1,0:T(8,128)(2,1)S(1)}, u32[]{:S(2)}, u32[]{:S(2)}) collective-permute-start(bf16[8,1024]{1,0:T(8,128)(2,1)S(1)} %maximum_add_fusion), channel_id=1, source_target_pairs={{0,4},{1,29},{2,26},{3,23},{4,0},{5,1},{6,30},{7,27},{8,12},{9,5},... | collective-permute-start | bytes 49160 | tf_op jit(solution)/shard_map/ppermute | solution.py:30
  10.4 0.3 %mul.11 = bf16[8,128,8,128]{3,2,1,0:T(8,128)(2,1)S(1)} broadcast(bf16[8,8]{1,0:T(8,128)(2,1)S(1)} %convert_bitcast_fusion), dimensions={0,2} | broadcast | bytes 2097280 | tf_op jit(solution)/shard_map/mul | solution.py:151
  10.7 0.5 %fusion = f32[8,1024]{1,0:T(8,128)S(1)} fusion(bf16[8,1024]{1,0:T(8,128)(2,1)S(1)} %maximum_add_fusion, bf16[1024,1024]{1,0:T(8,128)(2,1)S(1)} %copy-done, bf16[128,8,8,128]{3,2,1,0:T(8,128)(2,1)S(1)} %bitcast.10), kind=kOutput, calls=%fused_computation.1 | convolution fusion | flops 17825792 | bytes 4243456 | tf_op jit(solution)/shard_map/dot_general | solution.py:156
  11.2 0.2 collective-permute-start.8
  11.3 0.1 fusion.13
  11.5 0.4 %collective-permute-start.6 = (f32[8,8]{1,0:T(8,128)S(1)}, f32[8,8]{1,0:T(8,128)S(1)}, u32[]{:S(2)}, u32[]{:S(2)}) collective-permute-start(f32[8,8]{1,0:T(8,128)S(1)} %fusion.13), channel_id=1, source_target_pairs={{0,4},{1,5},{2,6},{3,7},{4,0},{5,1},{6,2},{7,3},{8,12},{9,13},{10,... | collective-permute-start | bytes 776 | tf_op jit(solution)/shard_map/ppermute | solution.py:30
  11.8 1.3 %collective-permute-start.7 = (f32[8,8]{1,0:T(8,128)S(1)}, f32[8,8]{1,0:T(8,128)S(1)}, u32[]{:S(2)}, u32[]{:S(2)}) collective-permute-start(f32[8,8]{1,0:T(8,128)S(1)} %fusion.13), channel_id=1, source_target_pairs={{0,20},{1,21},{2,22},{3,23},{4,16},{5,17},{6,18},{7,19},{8,12},{9,... | collective-permute-start | bytes 776 | tf_op jit(solution)/shard_map/ppermute | solution.py:30
  13.1 0.7 %fusion.1 = f32[8,1024]{1,0:T(8,128)S(1)} fusion(bf16[1024,1024]{1,0:T(8,128)(2,1)S(1)} %copy-done, bf16[128,8,8,128]{3,2,1,0:T(8,128)(2,1)S(1)} %bitcast.11, bf16[8,1024]{1,0:T(8,128)(2,1)S(1)} %maximum_add_fusion, bf16[8,1024]{1,0:T(8,128)(2,1)S(1)} %collective-permute-done.5, pred[]{:T(512)S(6)} %lt.20, pred[]{:T(512)S(6)} %eq.24), kind=kOutput, calls=%fused_computation.2 | convolution fusion | flops 17842176 | bytes 4259842 | tf_op jit(solution)/shard_map/dot_general | solution.py:166
  13.8 0.4 %collective-permute-start.10 = (f32[8,8]{1,0:T(8,128)S(1)}, f32[8,8]{1,0:T(8,128)S(1)}, u32[]{:S(2)}, u32[]{:S(2)}) collective-permute-start(f32[8,8]{1,0:T(8,128)S(1)} %add.40), channel_id=1, source_target_pairs={{0,12},{1,13},{2,14},{3,15},{4,8},{5,9},{6,10},{7,11},{8,20},{9,21... | collective-permute-start | bytes 776 | tf_op jit(solution)/shard_map/ppermute | solution.py:30
  14.2 2.3 %collective-permute-start.11 = (f32[8,8]{1,0:T(8,128)S(1)}, f32[8,8]{1,0:T(8,128)S(1)}, u32[]{:S(2)}, u32[]{:S(2)}) collective-permute-start(f32[8,8]{1,0:T(8,128)S(1)} %add.40), channel_id=1, source_target_pairs={{0,28},{1,29},{2,30},{3,31},{4,24},{5,25},{6,26},{7,27},{8,4},{9,5... | collective-permute-start | bytes 776 | tf_op jit(solution)/shard_map/ppermute | solution.py:30
  16.5 0.4 %collective-permute-start.9 = (f32[8,8]{1,0:T(8,128)S(1)}, f32[8,8]{1,0:T(8,128)S(1)}, u32[]{:S(2)}, u32[]{:S(2)}) collective-permute-start(f32[8,8]{1,0:T(8,128)S(1)} %broadcast_select_fusion.4), channel_id=1, source_target_pairs={{0,4},{1,5},{2,6},{3,7},{4,0},{5,1},{6,2},{7,3},{8,28},{9,29},{10,... | collective-permute-start | bytes 776 | tf_op jit(solution)/shard_map/ppermute | solution.py:30
  16.9 0.2 collective-permute-start.12
  17.2 0.6 %collective-permute-done.9 = f32[8,8]{1,0:T(8,128)S(1)} collective-permute-done((f32[8,8]{1,0:T(8,128)S(1)}, f32[8,8]{1,0:T(8,128)S(1)}, u32[]{:S(2)}, u32[]{:S(2)}) %collective-permute-start.9) | collective-permute-done | bytes 288 | tf_op jit(solution)/shard_map/ppermute | solution.py:30
  17.8 0.0 collective-permute-done.11
  17.8 0.4 %collective-permute-done.12 = f32[8,1024]{1,0:T(8,128)S(1)} collective-permute-done((f32[8,1024]{1,0:T(8,128)S(1)}, f32[8,1024]{1,0:T(8,128)S(1)}, u32[]{:S(2)}, u32[]{:S(2)}) %collective-permute-start.12) | collective-permute-done | bytes 32800 | tf_op jit(solution)/shard_map/ppermute | solution.py:30
  18.2 2.1 %collective-permute-start.13 = (f32[8,384]{1,0:T(8,128)S(1)}, f32[8,384]{1,0:T(8,128)S(1)}, u32[]{:S(2)}, u32[]{:S(2)}) collective-permute-start(f32[8,384]{1,0:T(8,128)S(1)} %get-tuple-element.55), channel_id=1, source_target_pairs={{0,6},{1,5},{2,7},{3,4},{4,2},{5,1},{6,3},{7,0},{8,14},{9,13},{10,... | collective-permute-start | bytes 36872 | tf_op jit(solution)/shard_map/ppermute | solution.py:30
  20.3 0.2 collective-permute-start.14
  20.5 1.7 %collective-permute-start.15 = (f32[8,384]{1,0:T(8,128)S(1)}, f32[8,384]{1,0:T(8,128)S(1)}, u32[]{:S(2)}, u32[]{:S(2)}) collective-permute-start(f32[8,384]{1,0:T(8,128)S(1)} %get-tuple-element.57), channel_id=1, source_target_pairs={{0,7},{1,6},{2,4},{3,5},{4,3},{5,2},{6,0},{7,1},{8,15},{9,14},{10,... | collective-permute-start | bytes 36872 | tf_op jit(solution)/shard_map/ppermute | solution.py:30
  22.2 0.3 %collective-permute-start.16 = (f32[8,384]{1,0:T(8,128)S(1)}, f32[8,384]{1,0:T(8,128)S(1)}, u32[]{:S(2)}, u32[]{:S(2)}) collective-permute-start(f32[8,384]{1,0:T(8,128)S(1)} %get-tuple-element.53), channel_id=1, source_target_pairs={{0,4},{1,7},{2,5},{3,6},{4,0},{5,3},{6,1},{7,2},{8,12},{9,15},{10,... | collective-permute-start | bytes 36872 | tf_op jit(solution)/shard_map/ppermute | solution.py:30
  22.5 0.8 %collective-permute-done.13 = f32[8,384]{1,0:T(8,128)S(1)} collective-permute-done((f32[8,384]{1,0:T(8,128)S(1)}, f32[8,384]{1,0:T(8,128)S(1)}, u32[]{:S(2)}, u32[]{:S(2)}) %collective-permute-start.13) | collective-permute-done | bytes 12320 | tf_op jit(solution)/shard_map/ppermute | solution.py:30
  23.3 0.7 %collective-permute-done.14 = f32[8,384]{1,0:T(8,128)S(1)} collective-permute-done((f32[8,384]{1,0:T(8,128)S(1)}, f32[8,384]{1,0:T(8,128)S(1)}, u32[]{:S(2)}, u32[]{:S(2)}) %collective-permute-start.14) | collective-permute-done | bytes 12320 | tf_op jit(solution)/shard_map/ppermute | solution.py:30
  24.0 0.5 %collective-permute-done.15 = f32[8,384]{1,0:T(8,128)S(1)} collective-permute-done((f32[8,384]{1,0:T(8,128)S(1)}, f32[8,384]{1,0:T(8,128)S(1)}, u32[]{:S(2)}, u32[]{:S(2)}) %collective-permute-start.15) | collective-permute-done | bytes 12320 | tf_op jit(solution)/shard_map/ppermute | solution.py:30
  24.5 0.7 %shard_map.50 = (f32[8,256]{1,0:T(8,128)}, f32[8,8]{1,0:T(8,128)}) custom-call(f32[8,384]{1,0:T(8,128)S(1)} %get-tuple-element.54.refs_0_, f32[8,384]{1,0:T(8,128)S(1)} %get-tuple-element.49.refs_1_, f32[8,384]{1,0:T(8,128)S(1)} %get-tuple-element.43.refs_2_, f32[8,384]{1,0:T(8,128)S(1)} %get-tuple-element.42.refs_3_), custom_call_target="tpu_custom_call" | custom-call | tf_op jit(solution)/shard_map/pallas_call | solution.py:225
  (24 shorter events, 0.1 us)
Async XLA Ops:
  0.6 10.1 %copy-start = (bf16[1024,1024]{1,0:T(8,128)(2,1)S(1)}, bf16[1024,1024]{1,0:T(8,128)(2,1)}, u32[]{:S(2)}) copy-start(bf16[1024,1024]{1,0:T(8,128)(2,1)} %param.3) | copy-start | bytes 6291460
  0.6 4.3 %collective-permute-start = (bf16[8,256]{1,0:T(8,128)(2,1)}, bf16[8,256]{1,0:T(8,128)(2,1)S(1)}, u32[]{:S(2)}, u32[]{:S(2)}) collective-permute-start(bf16[8,256]{1,0:T(8,128)(2,1)} %param.5), channel_id=1, source_target_pairs={{0,4},{1,5},{2,6},{3,7},{4,0},{5,1},{6,2},{7,3},{8,12},{9,13},{10,... | collective-permute-start | bytes 12296 | tf_op jit(solution)/shard_map/ppermute | solution.py:30
  1.2 7.3 %collective-permute-start.1 = (bf16[8,256]{1,0:T(8,128)(2,1)}, bf16[8,256]{1,0:T(8,128)(2,1)S(1)}, u32[]{:S(2)}, u32[]{:S(2)}) collective-permute-start(bf16[8,256]{1,0:T(8,128)(2,1)} %param.5), channel_id=1, source_target_pairs={{0,2},{1,3},{2,0},{3,1},{4,6},{5,7},{6,4},{7,5},{8,10},{9,11},{10,... | collective-permute-start | bytes 12296 | tf_op jit(solution)/shard_map/ppermute | solution.py:30
  4.8 3.6 %collective-permute-start.2 = (bf16[8,256]{1,0:T(8,128)(2,1)}, bf16[8,256]{1,0:T(8,128)(2,1)S(1)}, u32[]{:S(2)}, u32[]{:S(2)}) collective-permute-start(bf16[8,256]{1,0:T(8,128)(2,1)} %param.5), channel_id=1, source_target_pairs={{0,4},{1,5},{2,3},{3,2},{4,0},{5,1},{6,7},{7,6},{8,12},{9,13},{10,... | collective-permute-start | bytes 12296 | tf_op jit(solution)/shard_map/ppermute | solution.py:30
  5.0 4.8 %collective-permute-start.3 = (bf16[8,256]{1,0:T(8,128)(2,1)S(1)}, bf16[8,256]{1,0:T(8,128)(2,1)S(1)}, u32[]{:S(2)}, u32[]{:S(2)}) collective-permute-start(bf16[8,256]{1,0:T(8,128)(2,1)S(1)} %collective-permute-done), channel_id=1, source_target_pairs={{0,7},{1,6},{2,5},{3,4},{4,3},{5,2},{6,1},{7,0},{8,15},{9,14},{10,... | collective-permute-start | bytes 12296 | tf_op jit(solution)/shard_map/ppermute | solution.py:30
  6.9 3.0 %collective-permute-start.4 = (bf16[8,256]{1,0:T(8,128)(2,1)S(1)}, bf16[8,256]{1,0:T(8,128)(2,1)S(1)}, u32[]{:S(2)}, u32[]{:S(2)}) collective-permute-start(bf16[8,256]{1,0:T(8,128)(2,1)S(1)} %collective-permute-done), channel_id=1, source_target_pairs={{0,5},{1,4},{2,6},{3,7},{4,1},{5,0},{6,2},{7,3},{8,13},{9,12},{10,... | collective-permute-start | bytes 12296 | tf_op jit(solution)/shard_map/ppermute | solution.py:30
  10.0 1.4 %collective-permute-start.5 = (bf16[8,1024]{1,0:T(8,128)(2,1)S(1)}, bf16[8,1024]{1,0:T(8,128)(2,1)S(1)}, u32[]{:S(2)}, u32[]{:S(2)}) collective-permute-start(bf16[8,1024]{1,0:T(8,128)(2,1)S(1)} %maximum_add_fusion), channel_id=1, source_target_pairs={{0,4},{1,29},{2,26},{3,23},{4,0},{5,1},{6,30},{7,27},{8,12},{9,5},... | collective-permute-start | bytes 49160 | tf_op jit(solution)/shard_map/ppermute | solution.py:30
  11.2 5.3 %collective-permute-start.8 = (f32[8,1024]{1,0:T(8,128)S(1)}, f32[8,1024]{1,0:T(8,128)S(1)}, u32[]{:S(2)}, u32[]{:S(2)}) collective-permute-start(f32[8,1024]{1,0:T(8,128)S(1)} %fusion), channel_id=1, source_target_pairs={{0,4},{1,5},{2,10},{3,15},{4,0},{5,9},{6,14},{7,19},{8,12},{9,13},... | collective-permute-start | bytes 98312 | tf_op jit(solution)/shard_map/ppermute | solution.py:30
  11.5 2.3 %collective-permute-start.6 = (f32[8,8]{1,0:T(8,128)S(1)}, f32[8,8]{1,0:T(8,128)S(1)}, u32[]{:S(2)}, u32[]{:S(2)}) collective-permute-start(f32[8,8]{1,0:T(8,128)S(1)} %fusion.13), channel_id=1, source_target_pairs={{0,4},{1,5},{2,6},{3,7},{4,0},{5,1},{6,2},{7,3},{8,12},{9,13},{10,... | collective-permute-start | bytes 776 | tf_op jit(solution)/shard_map/ppermute | solution.py:30
  11.8 4.7 %collective-permute-start.7 = (f32[8,8]{1,0:T(8,128)S(1)}, f32[8,8]{1,0:T(8,128)S(1)}, u32[]{:S(2)}, u32[]{:S(2)}) collective-permute-start(f32[8,8]{1,0:T(8,128)S(1)} %fusion.13), channel_id=1, source_target_pairs={{0,20},{1,21},{2,22},{3,23},{4,16},{5,17},{6,18},{7,19},{8,12},{9,... | collective-permute-start | bytes 776 | tf_op jit(solution)/shard_map/ppermute | solution.py:30
  13.8 4.0 %collective-permute-start.10 = (f32[8,8]{1,0:T(8,128)S(1)}, f32[8,8]{1,0:T(8,128)S(1)}, u32[]{:S(2)}, u32[]{:S(2)}) collective-permute-start(f32[8,8]{1,0:T(8,128)S(1)} %add.40), channel_id=1, source_target_pairs={{0,12},{1,13},{2,14},{3,15},{4,8},{5,9},{6,10},{7,11},{8,20},{9,21... | collective-permute-start | bytes 776 | tf_op jit(solution)/shard_map/ppermute | solution.py:30
  14.2 3.7 %collective-permute-start.11 = (f32[8,8]{1,0:T(8,128)S(1)}, f32[8,8]{1,0:T(8,128)S(1)}, u32[]{:S(2)}, u32[]{:S(2)}) collective-permute-start(f32[8,8]{1,0:T(8,128)S(1)} %add.40), channel_id=1, source_target_pairs={{0,28},{1,29},{2,30},{3,31},{4,24},{5,25},{6,26},{7,27},{8,4},{9,5... | collective-permute-start | bytes 776 | tf_op jit(solution)/shard_map/ppermute | solution.py:30
  16.5 1.2 %collective-permute-start.9 = (f32[8,8]{1,0:T(8,128)S(1)}, f32[8,8]{1,0:T(8,128)S(1)}, u32[]{:S(2)}, u32[]{:S(2)}) collective-permute-start(f32[8,8]{1,0:T(8,128)S(1)} %broadcast_select_fusion.4), channel_id=1, source_target_pairs={{0,4},{1,5},{2,6},{3,7},{4,0},{5,1},{6,2},{7,3},{8,28},{9,29},{10,... | collective-permute-start | bytes 776 | tf_op jit(solution)/shard_map/ppermute | solution.py:30
  16.9 1.3 %collective-permute-start.12 = (f32[8,1024]{1,0:T(8,128)S(1)}, f32[8,1024]{1,0:T(8,128)S(1)}, u32[]{:S(2)}, u32[]{:S(2)}) collective-permute-start(f32[8,1024]{1,0:T(8,128)S(1)} %select_add_fusion), channel_id=1, source_target_pairs={{0,4},{1,5},{2,6},{3,7},{4,0},{5,1},{6,2},{7,3},{8,12},{9,13},{10,... | collective-permute-start | bytes 98312 | tf_op jit(solution)/shard_map/ppermute | solution.py:30
  18.2 5.1 %collective-permute-start.13 = (f32[8,384]{1,0:T(8,128)S(1)}, f32[8,384]{1,0:T(8,128)S(1)}, u32[]{:S(2)}, u32[]{:S(2)}) collective-permute-start(f32[8,384]{1,0:T(8,128)S(1)} %get-tuple-element.55), channel_id=1, source_target_pairs={{0,6},{1,5},{2,7},{3,4},{4,2},{5,1},{6,3},{7,0},{8,14},{9,13},{10,... | collective-permute-start | bytes 36872 | tf_op jit(solution)/shard_map/ppermute | solution.py:30
  20.3 3.7 %collective-permute-start.14 = (f32[8,384]{1,0:T(8,128)S(1)}, f32[8,384]{1,0:T(8,128)S(1)}, u32[]{:S(2)}, u32[]{:S(2)}) collective-permute-start(f32[8,384]{1,0:T(8,128)S(1)} %get-tuple-element.56), channel_id=1, source_target_pairs={{0,1},{1,0},{2,6},{3,7},{4,5},{5,4},{6,2},{7,3},{8,9},{9,8},{10,14... | collective-permute-start | bytes 36872 | tf_op jit(solution)/shard_map/ppermute | solution.py:30
  20.5 4.0 %collective-permute-start.15 = (f32[8,384]{1,0:T(8,128)S(1)}, f32[8,384]{1,0:T(8,128)S(1)}, u32[]{:S(2)}, u32[]{:S(2)}) collective-permute-start(f32[8,384]{1,0:T(8,128)S(1)} %get-tuple-element.57), channel_id=1, source_target_pairs={{0,7},{1,6},{2,4},{3,5},{4,3},{5,2},{6,0},{7,1},{8,15},{9,14},{10,... | collective-permute-start | bytes 36872 | tf_op jit(solution)/shard_map/ppermute | solution.py:30
  22.2 2.3 %collective-permute-start.16 = (f32[8,384]{1,0:T(8,128)S(1)}, f32[8,384]{1,0:T(8,128)S(1)}, u32[]{:S(2)}, u32[]{:S(2)}) collective-permute-start(f32[8,384]{1,0:T(8,128)S(1)} %get-tuple-element.53), channel_id=1, source_target_pairs={{0,4},{1,7},{2,5},{3,6},{4,0},{5,3},{6,1},{7,2},{8,12},{9,15},{10,... | collective-permute-start | bytes 36872 | tf_op jit(solution)/shard_map/ppermute | solution.py:30

commit v11 on v10

--- a/solution.py
+++ b/solution.py
@@ -16,7 +16,7 @@
 GATHER_CROSS = (0, 0, 1, 1)
 GATHER_ORDER = (0, 1, 2, 3)
 SUM_TABLES = ((2, 1, 3, 0), (1, 0, 2, 3), (3, 2, 0, 1), (0, 3, 1, 2))
-SUM_CROSS = (1, 0, 1, 1)
+SUM_CROSS = (1, 0, 1, 0)
 SUM_ORDER = (0, 1, 2, 3)
 
 

time: 25.4 us -> 25.4 us (level)
  no operation moved by 1% of the time
where the time goes in v11:
time: 25.4 us; the launch traced here: 25.2 us
  starting transfers between devices  16.2 us (64%)
  waiting for transfers between devices  4.54 us (18%)
  other arithmetic  1.47 us (6%)
  matrix products  1.23 us (5%)
  between operations  0.72 us (3%)
  Pallas kernels  0.67 us (3%)
  local copies, waits for them, and re-layouts  0.34 us (1%)
    ppermute x17, starting transfers between devices, send(): return lax.ppermute(block, AXES, pairs)  16.2 us
    ppermute x17, waiting for transfers between devices, send(): return lax.ppermute(block, AXES, pairs)  4.54 us
    select_n x1, other arithmetic, on_device(): jnp.where(place == at, source, zero)  0.69 us
    convert_element_type x1, other arithmetic, on_device(): keep = block_map[0, 0].astype(jnp.bfloat16)  0.69 us
    pallas_call x1, Pallas kernels, on_device(): pl.pallas_call(functools.partial(write_results, 1.0 / (width * rows) ** 0...  0.67 us
    dot_general x1, matrix products, on_device(): lax.dot_general(far_vec, matrix, (((1,), (1,)), ((), ())), preferred_elem...  0.65 us
  transfers between devices with their start and end apart: 17, of which 7 were waited for; matrix products, arithmetic and copies ran while one was open for 12% of the time, Pallas kernels for 0%

profile of v11, /device:TPU:0, one launch (start us, length us, event | category | flops | bytes accessed | tf_op | source)
XLA Modules:
  0.0 25.2 jit_solution(2026923464108177786)
XLA Ops:
  0.6 0.5 %collective-permute-start = (bf16[8,256]{1,0:T(8,128)(2,1)}, bf16[8,256]{1,0:T(8,128)(2,1)S(1)}, u32[]{:S(2)}, u32[]{:S(2)}) collective-permute-start(bf16[8,256]{1,0:T(8,128)(2,1)} %param.5), channel_id=1, source_target_pairs={{0,4},{1,5},{2,6},{3,7},{4,0},{5,1},{6,2},{7,3},{8,12},{9,13},{10,... | collective-permute-start | bytes 12296 | tf_op jit(solution)/shard_map/ppermute | solution.py:30
  1.2 3.7 %collective-permute-start.1 = (bf16[8,256]{1,0:T(8,128)(2,1)}, bf16[8,256]{1,0:T(8,128)(2,1)S(1)}, u32[]{:S(2)}, u32[]{:S(2)}) collective-permute-start(bf16[8,256]{1,0:T(8,128)(2,1)} %param.5), channel_id=1, source_target_pairs={{0,2},{1,3},{2,0},{3,1},{4,6},{5,7},{6,4},{7,5},{8,10},{9,11},{10,... | collective-permute-start | bytes 12296 | tf_op jit(solution)/shard_map/ppermute | solution.py:30
  4.8 0.2 collective-permute-start.2
  5.0 1.9 %collective-permute-start.3 = (bf16[8,256]{1,0:T(8,128)(2,1)S(1)}, bf16[8,256]{1,0:T(8,128)(2,1)S(1)}, u32[]{:S(2)}, u32[]{:S(2)}) collective-permute-start(bf16[8,256]{1,0:T(8,128)(2,1)S(1)} %collective-permute-done), channel_id=1, source_target_pairs={{0,7},{1,6},{2,5},{3,4},{4,3},{5,2},{6,1},{7,0},{8,15},{9,14},{10,... | collective-permute-start | bytes 12296 | tf_op jit(solution)/shard_map/ppermute | solution.py:30
  6.9 0.1 collective-permute-start.4
  7.0 0.7 %convert_bitcast_fusion = bf16[8,8]{1,0:T(8,128)(2,1)S(1)} fusion(s32[1,1,8,8]{3,2,1,0:T(8,128)} %param.4), kind=kLoop, calls=%fused_computation.42 | loop fusion | flops 64 | bytes 384 | tf_op jit(solution)/shard_map/convert_element_type | solution.py:150
  7.7 0.7 %broadcast_select_fusion.3 = (bf16[8,256]{1,0:T(8,128)(2,1)S(1)}, bf16[8,256]{1,0:T(8,128)(2,1)S(1)}, bf16[8,256]{1,0:T(8,128)(2,1)S(1)}, bf16[8,256]{1,0:T(8,128)(2,1)S(1)}) fusion(bf16[8,256]{1,0:T(8,128)(2,1)} %param.5, pred[]{:T(512)S(6)} %eq.23, pred[]{:T(512)S(6)} %eq.27, pred[]{:T(512)S(6)} %eq.26, pred[]{:T(512)S(6)} %eq.25), kind=kLoop, calls=%fused_computation.40 | loop fusion | flops 8192 | bytes 20484 | tf_op jit(solution)/shard_map/jit(_where)/select_n | solution.py:137
  8.4 1.4 %collective-permute-done.3 = bf16[8,256]{1,0:T(8,128)(2,1)S(1)} collective-permute-done((bf16[8,256]{1,0:T(8,128)(2,1)S(1)}, bf16[8,256]{1,0:T(8,128)(2,1)S(1)}, u32[]{:S(2)}, u32[]{:S(2)}) %collective-permute-start.3) | collective-permute-done | bytes 4128 | tf_op jit(solution)/shard_map/ppermute | solution.py:30
  9.8 0.1 collective-permute-done.4
  10.0 0.4 %collective-permute-start.5 = (bf16[8,1024]{1,0:T(8,128)(2,1)S(1)}, bf16[8,1024]{1,0:T(8,128)(2,1)S(1)}, u32[]{:S(2)}, u32[]{:S(2)}) collective-permute-start(bf16[8,1024]{1,0:T(8,128)(2,1)S(1)} %maximum_add_fusion), channel_id=1, source_target_pairs={{0,4},{1,29},{2,26},{3,23},{4,0},{5,1},{6,30},{7,27},{8,12},{9,5},... | collective-permute-start | bytes 49160 | tf_op jit(solution)/shard_map/ppermute | solution.py:30
  10.4 0.3 %mul.11 = bf16[8,128,8,128]{3,2,1,0:T(8,128)(2,1)S(1)} broadcast(bf16[8,8]{1,0:T(8,128)(2,1)S(1)} %convert_bitcast_fusion), dimensions={0,2} | broadcast | bytes 2097280 | tf_op jit(solution)/shard_map/mul | solution.py:151
  10.7 0.5 %fusion = f32[8,1024]{1,0:T(8,128)S(1)} fusion(bf16[8,1024]{1,0:T(8,128)(2,1)S(1)} %maximum_add_fusion, bf16[1024,1024]{1,0:T(8,128)(2,1)S(1)} %copy-done, bf16[128,8,8,128]{3,2,1,0:T(8,128)(2,1)S(1)} %bitcast.10), kind=kOutput, calls=%fused_computation.1 | convolution fusion | flops 17825792 | bytes 4243456 | tf_op jit(solution)/shard_map/dot_general | solution.py:156
  11.2 0.2 collective-permute-start.8
  11.3 0.1 fusion.13
  11.5 0.4 %collective-permute-start.6 = (f32[8,8]{1,0:T(8,128)S(1)}, f32[8,8]{1,0:T(8,128)S(1)}, u32[]{:S(2)}, u32[]{:S(2)}) collective-permute-start(f32[8,8]{1,0:T(8,128)S(1)} %fusion.13), channel_id=1, source_target_pairs={{0,4},{1,5},{2,6},{3,7},{4,0},{5,1},{6,2},{7,3},{8,12},{9,13},{10,... | collective-permute-start | bytes 776 | tf_op jit(solution)/shard_map/ppermute | solution.py:30
  11.8 1.3 %collective-permute-start.7 = (f32[8,8]{1,0:T(8,128)S(1)}, f32[8,8]{1,0:T(8,128)S(1)}, u32[]{:S(2)}, u32[]{:S(2)}) collective-permute-start(f32[8,8]{1,0:T(8,128)S(1)} %fusion.13), channel_id=1, source_target_pairs={{0,20},{1,21},{2,22},{3,23},{4,16},{5,17},{6,18},{7,19},{8,12},{9,... | collective-permute-start | bytes 776 | tf_op jit(solution)/shard_map/ppermute | solution.py:30
  13.1 0.7 %fusion.1 = f32[8,1024]{1,0:T(8,128)S(1)} fusion(bf16[1024,1024]{1,0:T(8,128)(2,1)S(1)} %copy-done, bf16[128,8,8,128]{3,2,1,0:T(8,128)(2,1)S(1)} %bitcast.11, bf16[8,1024]{1,0:T(8,128)(2,1)S(1)} %maximum_add_fusion, bf16[8,1024]{1,0:T(8,128)(2,1)S(1)} %collective-permute-done.5, pred[]{:T(512)S(6)} %lt.20, pred[]{:T(512)S(6)} %eq.24), kind=kOutput, calls=%fused_computation.2 | convolution fusion | flops 17842176 | bytes 4259842 | tf_op jit(solution)/shard_map/dot_general | solution.py:166
  13.8 0.4 %collective-permute-start.10 = (f32[8,8]{1,0:T(8,128)S(1)}, f32[8,8]{1,0:T(8,128)S(1)}, u32[]{:S(2)}, u32[]{:S(2)}) collective-permute-start(f32[8,8]{1,0:T(8,128)S(1)} %add.40), channel_id=1, source_target_pairs={{0,12},{1,13},{2,14},{3,15},{4,8},{5,9},{6,10},{7,11},{8,20},{9,21... | collective-permute-start | bytes 776 | tf_op jit(solution)/shard_map/ppermute | solution.py:30
  14.2 2.3 %collective-permute-start.11 = (f32[8,8]{1,0:T(8,128)S(1)}, f32[8,8]{1,0:T(8,128)S(1)}, u32[]{:S(2)}, u32[]{:S(2)}) collective-permute-start(f32[8,8]{1,0:T(8,128)S(1)} %add.40), channel_id=1, source_target_pairs={{0,28},{1,29},{2,30},{3,31},{4,24},{5,25},{6,26},{7,27},{8,4},{9,5... | collective-permute-start | bytes 776 | tf_op jit(solution)/shard_map/ppermute | solution.py:30
  16.5 0.4 %collective-permute-start.9 = (f32[8,8]{1,0:T(8,128)S(1)}, f32[8,8]{1,0:T(8,128)S(1)}, u32[]{:S(2)}, u32[]{:S(2)}) collective-permute-start(f32[8,8]{1,0:T(8,128)S(1)} %broadcast_select_fusion.4), channel_id=1, source_target_pairs={{0,4},{1,5},{2,6},{3,7},{4,0},{5,1},{6,2},{7,3},{8,28},{9,29},{10,... | collective-permute-start | bytes 776 | tf_op jit(solution)/shard_map/ppermute | solution.py:30
  16.9 0.2 collective-permute-start.12
  17.2 0.6 %collective-permute-done.9 = f32[8,8]{1,0:T(8,128)S(1)} collective-permute-done((f32[8,8]{1,0:T(8,128)S(1)}, f32[8,8]{1,0:T(8,128)S(1)}, u32[]{:S(2)}, u32[]{:S(2)}) %collective-permute-start.9) | collective-permute-done | bytes 288 | tf_op jit(solution)/shard_map/ppermute | solution.py:30
  17.8 0.0 collective-permute-done.11
  17.8 0.4 %collective-permute-done.12 = f32[8,1024]{1,0:T(8,128)S(1)} collective-permute-done((f32[8,1024]{1,0:T(8,128)S(1)}, f32[8,1024]{1,0:T(8,128)S(1)}, u32[]{:S(2)}, u32[]{:S(2)}) %collective-permute-start.12) | collective-permute-done | bytes 32800 | tf_op jit(solution)/shard_map/ppermute | solution.py:30
  18.2 2.1 %collective-permute-start.13 = (f32[8,384]{1,0:T(8,128)S(1)}, f32[8,384]{1,0:T(8,128)S(1)}, u32[]{:S(2)}, u32[]{:S(2)}) collective-permute-start(f32[8,384]{1,0:T(8,128)S(1)} %get-tuple-element.55), channel_id=1, source_target_pairs={{0,6},{1,5},{2,7},{3,4},{4,2},{5,1},{6,3},{7,0},{8,14},{9,13},{10,... | collective-permute-start | bytes 36872 | tf_op jit(solution)/shard_map/ppermute | solution.py:30
  20.3 0.2 collective-permute-start.14
  20.5 1.7 %collective-permute-start.15 = (f32[8,384]{1,0:T(8,128)S(1)}, f32[8,384]{1,0:T(8,128)S(1)}, u32[]{:S(2)}, u32[]{:S(2)}) collective-permute-start(f32[8,384]{1,0:T(8,128)S(1)} %get-tuple-element.57), channel_id=1, source_target_pairs={{0,7},{1,6},{2,4},{3,5},{4,3},{5,2},{6,0},{7,1},{8,15},{9,14},{10,... | collective-permute-start | bytes 36872 | tf_op jit(solution)/shard_map/ppermute | solution.py:30
  22.2 0.3 %collective-permute-start.16 = (f32[8,384]{1,0:T(8,128)S(1)}, f32[8,384]{1,0:T(8,128)S(1)}, u32[]{:S(2)}, u32[]{:S(2)}) collective-permute-start(f32[8,384]{1,0:T(8,128)S(1)} %get-tuple-element.53), channel_id=1, source_target_pairs={{0,4},{1,3},{2,1},{3,2},{4,0},{5,7},{6,5},{7,6},{8,12},{9,11},{10,... | collective-permute-start | bytes 36872 | tf_op jit(solution)/shard_map/ppermute | solution.py:30
  22.5 0.8 %collective-permute-done.13 = f32[8,384]{1,0:T(8,128)S(1)} collective-permute-done((f32[8,384]{1,0:T(8,128)S(1)}, f32[8,384]{1,0:T(8,128)S(1)}, u32[]{:S(2)}, u32[]{:S(2)}) %collective-permute-start.13) | collective-permute-done | bytes 12320 | tf_op jit(solution)/shard_map/ppermute | solution.py:30
  23.3 0.7 %collective-permute-done.14 = f32[8,384]{1,0:T(8,128)S(1)} collective-permute-done((f32[8,384]{1,0:T(8,128)S(1)}, f32[8,384]{1,0:T(8,128)S(1)}, u32[]{:S(2)}, u32[]{:S(2)}) %collective-permute-start.14) | collective-permute-done | bytes 12320 | tf_op jit(solution)/shard_map/ppermute | solution.py:30
  24.0 0.5 %collective-permute-done.15 = f32[8,384]{1,0:T(8,128)S(1)} collective-permute-done((f32[8,384]{1,0:T(8,128)S(1)}, f32[8,384]{1,0:T(8,128)S(1)}, u32[]{:S(2)}, u32[]{:S(2)}) %collective-permute-start.15) | collective-permute-done | bytes 12320 | tf_op jit(solution)/shard_map/ppermute | solution.py:30
  24.5 0.7 %shard_map.50 = (f32[8,256]{1,0:T(8,128)}, f32[8,8]{1,0:T(8,128)}) custom-call(f32[8,384]{1,0:T(8,128)S(1)} %get-tuple-element.54.refs_0_, f32[8,384]{1,0:T(8,128)S(1)} %get-tuple-element.49.refs_1_, f32[8,384]{1,0:T(8,128)S(1)} %get-tuple-element.43.refs_2_, f32[8,384]{1,0:T(8,128)S(1)} %get-tuple-element.42.refs_3_), custom_call_target="tpu_custom_call" | custom-call | tf_op jit(solution)/shard_map/pallas_call | solution.py:225
  (24 shorter events, 0.1 us)
Async XLA Ops:
  0.6 10.1 %copy-start = (bf16[1024,1024]{1,0:T(8,128)(2,1)S(1)}, bf16[1024,1024]{1,0:T(8,128)(2,1)}, u32[]{:S(2)}) copy-start(bf16[1024,1024]{1,0:T(8,128)(2,1)} %param.3) | copy-start | bytes 6291460
  0.6 4.3 %collective-permute-start = (bf16[8,256]{1,0:T(8,128)(2,1)}, bf16[8,256]{1,0:T(8,128)(2,1)S(1)}, u32[]{:S(2)}, u32[]{:S(2)}) collective-permute-start(bf16[8,256]{1,0:T(8,128)(2,1)} %param.5), channel_id=1, source_target_pairs={{0,4},{1,5},{2,6},{3,7},{4,0},{5,1},{6,2},{7,3},{8,12},{9,13},{10,... | collective-permute-start | bytes 12296 | tf_op jit(solution)/shard_map/ppermute | solution.py:30
  1.2 7.3 %collective-permute-start.1 = (bf16[8,256]{1,0:T(8,128)(2,1)}, bf16[8,256]{1,0:T(8,128)(2,1)S(1)}, u32[]{:S(2)}, u32[]{:S(2)}) collective-permute-start(bf16[8,256]{1,0:T(8,128)(2,1)} %param.5), channel_id=1, source_target_pairs={{0,2},{1,3},{2,0},{3,1},{4,6},{5,7},{6,4},{7,5},{8,10},{9,11},{10,... | collective-permute-start | bytes 12296 | tf_op jit(solution)/shard_map/ppermute | solution.py:30
  4.8 3.6 %collective-permute-start.2 = (bf16[8,256]{1,0:T(8,128)(2,1)}, bf16[8,256]{1,0:T(8,128)(2,1)S(1)}, u32[]{:S(2)}, u32[]{:S(2)}) collective-permute-start(bf16[8,256]{1,0:T(8,128)(2,1)} %param.5), channel_id=1, source_target_pairs={{0,4},{1,5},{2,3},{3,2},{4,0},{5,1},{6,7},{7,6},{8,12},{9,13},{10,... | collective-permute-start | bytes 12296 | tf_op jit(solution)/shard_map/ppermute | solution.py:30
  5.0 4.8 %collective-permute-start.3 = (bf16[8,256]{1,0:T(8,128)(2,1)S(1)}, bf16[8,256]{1,0:T(8,128)(2,1)S(1)}, u32[]{:S(2)}, u32[]{:S(2)}) collective-permute-start(bf16[8,256]{1,0:T(8,128)(2,1)S(1)} %collective-permute-done), channel_id=1, source_target_pairs={{0,7},{1,6},{2,5},{3,4},{4,3},{5,2},{6,1},{7,0},{8,15},{9,14},{10,... | collective-permute-start | bytes 12296 | tf_op jit(solution)/shard_map/ppermute | solution.py:30
  6.9 3.0 %collective-permute-start.4 = (bf16[8,256]{1,0:T(8,128)(2,1)S(1)}, bf16[8,256]{1,0:T(8,128)(2,1)S(1)}, u32[]{:S(2)}, u32[]{:S(2)}) collective-permute-start(bf16[8,256]{1,0:T(8,128)(2,1)S(1)} %collective-permute-done), channel_id=1, source_target_pairs={{0,5},{1,4},{2,6},{3,7},{4,1},{5,0},{6,2},{7,3},{8,13},{9,12},{10,... | collective-permute-start | bytes 12296 | tf_op jit(solution)/shard_map/ppermute | solution.py:30
  10.0 1.4 %collective-permute-start.5 = (bf16[8,1024]{1,0:T(8,128)(2,1)S(1)}, bf16[8,1024]{1,0:T(8,128)(2,1)S(1)}, u32[]{:S(2)}, u32[]{:S(2)}) collective-permute-start(bf16[8,1024]{1,0:T(8,128)(2,1)S(1)} %maximum_add_fusion), channel_id=1, source_target_pairs={{0,4},{1,29},{2,26},{3,23},{4,0},{5,1},{6,30},{7,27},{8,12},{9,5},... | collective-permute-start | bytes 49160 | tf_op jit(solution)/shard_map/ppermute | solution.py:30
  11.2 5.3 %collective-permute-start.8 = (f32[8,1024]{1,0:T(8,128)S(1)}, f32[8,1024]{1,0:T(8,128)S(1)}, u32[]{:S(2)}, u32[]{:S(2)}) collective-permute-start(f32[8,1024]{1,0:T(8,128)S(1)} %fusion), channel_id=1, source_target_pairs={{0,4},{1,5},{2,10},{3,15},{4,0},{5,9},{6,14},{7,19},{8,12},{9,13},... | collective-permute-start | bytes 98312 | tf_op jit(solution)/shard_map/ppermute | solution.py:30
  11.5 2.3 %collective-permute-start.6 = (f32[8,8]{1,0:T(8,128)S(1)}, f32[8,8]{1,0:T(8,128)S(1)}, u32[]{:S(2)}, u32[]{:S(2)}) collective-permute-start(f32[8,8]{1,0:T(8,128)S(1)} %fusion.13), channel_id=1, source_target_pairs={{0,4},{1,5},{2,6},{3,7},{4,0},{5,1},{6,2},{7,3},{8,12},{9,13},{10,... | collective-permute-start | bytes 776 | tf_op jit(solution)/shard_map/ppermute | solution.py:30
  11.8 4.7 %collective-permute-start.7 = (f32[8,8]{1,0:T(8,128)S(1)}, f32[8,8]{1,0:T(8,128)S(1)}, u32[]{:S(2)}, u32[]{:S(2)}) collective-permute-start(f32[8,8]{1,0:T(8,128)S(1)} %fusion.13), channel_id=1, source_target_pairs={{0,20},{1,21},{2,22},{3,23},{4,16},{5,17},{6,18},{7,19},{8,12},{9,... | collective-permute-start | bytes 776 | tf_op jit(solution)/shard_map/ppermute | solution.py:30
  13.8 4.0 %collective-permute-start.10 = (f32[8,8]{1,0:T(8,128)S(1)}, f32[8,8]{1,0:T(8,128)S(1)}, u32[]{:S(2)}, u32[]{:S(2)}) collective-permute-start(f32[8,8]{1,0:T(8,128)S(1)} %add.40), channel_id=1, source_target_pairs={{0,12},{1,13},{2,14},{3,15},{4,8},{5,9},{6,10},{7,11},{8,20},{9,21... | collective-permute-start | bytes 776 | tf_op jit(solution)/shard_map/ppermute | solution.py:30
  14.2 3.7 %collective-permute-start.11 = (f32[8,8]{1,0:T(8,128)S(1)}, f32[8,8]{1,0:T(8,128)S(1)}, u32[]{:S(2)}, u32[]{:S(2)}) collective-permute-start(f32[8,8]{1,0:T(8,128)S(1)} %add.40), channel_id=1, source_target_pairs={{0,28},{1,29},{2,30},{3,31},{4,24},{5,25},{6,26},{7,27},{8,4},{9,5... | collective-permute-start | bytes 776 | tf_op jit(solution)/shard_map/ppermute | solution.py:30
  16.5 1.2 %collective-permute-start.9 = (f32[8,8]{1,0:T(8,128)S(1)}, f32[8,8]{1,0:T(8,128)S(1)}, u32[]{:S(2)}, u32[]{:S(2)}) collective-permute-start(f32[8,8]{1,0:T(8,128)S(1)} %broadcast_select_fusion.4), channel_id=1, source_target_pairs={{0,4},{1,5},{2,6},{3,7},{4,0},{5,1},{6,2},{7,3},{8,28},{9,29},{10,... | collective-permute-start | bytes 776 | tf_op jit(solution)/shard_map/ppermute | solution.py:30
  16.9 1.3 %collective-permute-start.12 = (f32[8,1024]{1,0:T(8,128)S(1)}, f32[8,1024]{1,0:T(8,128)S(1)}, u32[]{:S(2)}, u32[]{:S(2)}) collective-permute-start(f32[8,1024]{1,0:T(8,128)S(1)} %select_add_fusion), channel_id=1, source_target_pairs={{0,4},{1,5},{2,6},{3,7},{4,0},{5,1},{6,2},{7,3},{8,12},{9,13},{10,... | collective-permute-start | bytes 98312 | tf_op jit(solution)/shard_map/ppermute | solution.py:30
  18.2 5.1 %collective-permute-start.13 = (f32[8,384]{1,0:T(8,128)S(1)}, f32[8,384]{1,0:T(8,128)S(1)}, u32[]{:S(2)}, u32[]{:S(2)}) collective-permute-start(f32[8,384]{1,0:T(8,128)S(1)} %get-tuple-element.55), channel_id=1, source_target_pairs={{0,6},{1,5},{2,7},{3,4},{4,2},{5,1},{6,3},{7,0},{8,14},{9,13},{10,... | collective-permute-start | bytes 36872 | tf_op jit(solution)/shard_map/ppermute | solution.py:30
  20.3 3.7 %collective-permute-start.14 = (f32[8,384]{1,0:T(8,128)S(1)}, f32[8,384]{1,0:T(8,128)S(1)}, u32[]{:S(2)}, u32[]{:S(2)}) collective-permute-start(f32[8,384]{1,0:T(8,128)S(1)} %get-tuple-element.56), channel_id=1, source_target_pairs={{0,1},{1,0},{2,6},{3,7},{4,5},{5,4},{6,2},{7,3},{8,9},{9,8},{10,14... | collective-permute-start | bytes 36872 | tf_op jit(solution)/shard_map/ppermute | solution.py:30
  20.5 4.0 %collective-permute-start.15 = (f32[8,384]{1,0:T(8,128)S(1)}, f32[8,384]{1,0:T(8,128)S(1)}, u32[]{:S(2)}, u32[]{:S(2)}) collective-permute-start(f32[8,384]{1,0:T(8,128)S(1)} %get-tuple-element.57), channel_id=1, source_target_pairs={{0,7},{1,6},{2,4},{3,5},{4,3},{5,2},{6,0},{7,1},{8,15},{9,14},{10,... | collective-permute-start | bytes 36872 | tf_op jit(solution)/shard_map/ppermute | solution.py:30
  22.2 2.3 %collective-permute-start.16 = (f32[8,384]{1,0:T(8,128)S(1)}, f32[8,384]{1,0:T(8,128)S(1)}, u32[]{:S(2)}, u32[]{:S(2)}) collective-permute-start(f32[8,384]{1,0:T(8,128)S(1)} %get-tuple-element.53), channel_id=1, source_target_pairs={{0,4},{1,3},{2,1},{3,2},{4,0},{5,7},{6,5},{7,6},{8,12},{9,11},{10,... | collective-permute-start | bytes 36872 | tf_op jit(solution)/shard_map/ppermute | solution.py:30
